TPU v7x, 32 devices: a whole 2x2x4 slice. The times are simulated.
32 devices in a mesh: leaf: 8 (over z, y), near: 4 (over x, core).
Axes of the slice: x: 2, y: 2, z: 4, core: 2. Of those that a mesh axis runs over, the one named last changes fastest.
Arguments:
- bases: float32 [64, 64, 64], P('leaf'), may hold values from -1 to 4
- leaf_transfer: float32 [64, 64, 64], P('leaf'), may hold values from -1 to 4
- top_transfer: float32 [32, 64, 64], P('leaf'), may hold values from -1 to 4
- couplings: bfloat16 [4096, 64, 64], P(('leaf', 'near')), may hold values from -6 to 6
- coupling_target: int32 [4096], P(('leaf', 'near')), may hold values from 0 to 7
- coupling_dest: int32 [4096, 1], P(('leaf', 'near')), may hold values from 0 to 7; in each aligned block of 128 rows (0 to 127, 128 to 255, ...) at most 32 rows name the same one
- coupling_local: int32 [4096], P(('leaf', 'near')), may hold values from 0 to 7
- top_couplings: bfloat16 [512, 64, 64], P(('leaf', 'near')), may hold values from -0.59765625 to 0.59765625
- top_target: int32 [512], P(('leaf', 'near')), may hold values from 0 to 7
- top_source: int32 [512], P(('leaf', 'near')), may hold values from 0 to 15
Outputs:
- leaf_bases: float32 [64, 64, 64], P(('leaf', 'near'))
- leaf_transfers: float32 [64, 64, 64], P('leaf')
- top_transfers: float32 [32, 64, 64], P('leaf')
- new_couplings: bfloat16 [4096, 64, 64], P(('leaf', 'near'))
- new_top_couplings: bfloat16 [512, 64, 64], P(('leaf', 'near'))
Inputs may be any that keep to these rules, and one draw needn't show every extreme that they name: `coupling_dest`: among the leaf blocks of one device, at most 32 have their source in the same subtree.
All inputs are finite; a program needn't handle non-finite values.
Results may differ from a plain program's by a relative error of at most 0.0065.
Values may be sent and summed in bfloat16 or wider, within the bound.
No kernel may reach another device: no remote copies, remote signals or barrier semaphores. Data moves between devices by JAX's collectives and lax.ppermute only.
A program may use at most 128 MiB of HBM per device.

v0:
```python
import jax
import jax.numpy as jnp
from jax import lax
from jax.sharding import PartitionSpec as P

exact_mode = lax.Precision.HIGHEST


def swapped(value, axis, distance):
    mask = 2**distance
    pairs = [(source, source ^ mask) for source in range(lax.axis_size(axis))]
    return lax.ppermute(value, axis, pairs)


def gram_of(stacked):
    return jnp.einsum("nmk,nml->nkl", stacked, stacked, precision=exact_mode)


def right_solve(lower_part, stacked):

    def single(factor_one, block_one):
        return jax.scipy.linalg.solve_triangular(factor_one, block_one.T, lower=True).T

    return jax.vmap(single)(lower_part, stacked)


def on_device(
    bases,
    leaf_transfer,
    top_transfer,
    couplings,
    coupling_target,
    coupling_dest,
    coupling_local,
    top_couplings,
    top_target,
    top_source,
):
    leaves_here = bases.shape[0]
    rank_width = bases.shape[2]
    share = leaves_here // lax.axis_size("near")
    near_place = lax.axis_index("near")
    my_bases = lax.dynamic_slice_in_dim(bases, near_place * share, share, 0)
    lower_mine = jnp.linalg.cholesky(gram_of(my_bases))
    leaf_bases = right_solve(lower_mine, my_bases)
    leaf_factor = lax.all_gather(jnp.swapaxes(lower_mine, 1, 2), "near", axis=0, tiled=True)
    child_piece = jnp.einsum("nkr,nrl->nkl", leaf_factor, leaf_transfer, precision=exact_mode)
    sibling = swapped(child_piece, "leaf", 0)
    lower_middle = jnp.linalg.cholesky(gram_of(child_piece) + gram_of(sibling))
    leaf_transfers = right_solve(lower_middle, child_piece)
    mid_factor = jnp.swapaxes(lower_middle, 1, 2)
    leaf_place = lax.axis_index("leaf")
    parity = leaf_place % 2
    halfway = leaves_here // 2
    mid_mine = lax.dynamic_slice_in_dim(mid_factor, parity * halfway, halfway, 0)
    up_piece = jnp.einsum("nkr,nrl->nkl", mid_mine, top_transfer, precision=exact_mode)
    cousin = swapped(up_piece, "leaf", 1)
    lower_top = jnp.linalg.cholesky(gram_of(up_piece) + gram_of(cousin))
    top_transfers = right_solve(lower_top, up_piece)
    top_factor = jnp.swapaxes(lower_top, 1, 2)
    upper_bit = leaf_place // 2 % 2
    fourth = leaves_here // 4
    top_mine = lax.dynamic_slice_in_dim(top_factor, upper_bit * fourth, fourth, 0).astype(
        jnp.bfloat16
    )
    gathered = lax.all_gather(top_mine, "leaf", axis=0, tiled=True)
    quads = gathered.shape[0] // leaves_here
    top_table = gathered.reshape(quads, 2, 2, fourth, rank_width, rank_width)
    top_table = jnp.transpose(top_table, (0, 2, 1, 3, 4, 5)).reshape(
        quads * leaves_here, rank_width, rank_width
    )
    factor_low = leaf_factor.astype(jnp.bfloat16)
    target_rows = factor_low[coupling_target]
    halves = jnp.einsum(
        "nkr,nrl->nkl", target_rows, couplings, preferred_element_type=jnp.float32
    ).astype(jnp.bfloat16)
    destination = coupling_dest[:, 0]
    every_factor = lax.all_gather(factor_low, "leaf", axis=0, tiled=True)
    source_rows = every_factor[destination * leaves_here + coupling_local]
    new_couplings = jnp.einsum(
        "nkr,nlr->nkl", halves, source_rows, preferred_element_type=jnp.float32
    ).astype(jnp.bfloat16)
    quad_place = leaf_place // 4
    top_left = top_table[quad_place * leaves_here + top_target]
    top_right = top_table[top_source]
    half_top = jnp.einsum(
        "nkr,nrl->nkl", top_left, top_couplings, preferred_element_type=jnp.float32
    ).astype(jnp.bfloat16)
    new_top_couplings = jnp.einsum(
        "nkr,nlr->nkl", half_top, top_right, preferred_element_type=jnp.float32
    ).astype(jnp.bfloat16)
    return (leaf_bases, leaf_transfers, top_transfers, new_couplings, new_top_couplings)


def solution(mesh):
    in_specs = (
        P("leaf", None, None),
        P("leaf", None, None),
        P("leaf", None, None),
        P(("leaf", "near"), None, None),
        P(("leaf", "near")),
        P(("leaf", "near"), None),
        P(("leaf", "near")),
        P(("leaf", "near"), None, None),
        P(("leaf", "near")),
        P(("leaf", "near")),
    )
    out_specs = (
        P(("leaf", "near"), None, None),
        P("leaf", None, None),
        P("leaf", None, None),
        P(("leaf", "near"), None, None),
        P(("leaf", "near"), None, None),
    )
    return jax.shard_map(
        on_device, mesh=mesh, in_specs=in_specs, out_specs=out_specs, check_vma=False
    )
```

profile of v0, /device:TPU:0, one launch (start us, length us, event | category | flops | bytes accessed | tf_op | source)
XLA Modules:
  0.0 257.4 jit_solution(10267343427417949036)
XLA Ops:
  0.7 1.2 fusion.19
  2.0 11.7 %custom-call.24 = f32[2,64,64]{2,1,0:T(8,128)S(1)} custom-call(f32[2,64,64]{2,1,0:T(8,128)S(1)} %fusion.17), custom_call_target="Cholesky" | custom-call | tf_op jit(solution)/shard_map/jit(cholesky)/cholesky | solution.py:44
  13.8 0.1 compare_reduce_fusion.2
  14.1 7.2 %all_gather.9 = f32[8,64,64]{2,1,0:T(8,128)S(1)} all-gather(f32[2,64,64]{2,1,0:T(8,128)S(1)} %copy.98), channel_id=1, replica_groups=mesh['leaf'=8,'near'=4] {'near'}, dimensions={0}, use_global_device_ids=true | all-gather | bytes 163840 | tf_op jit(solution)/shard_map/all_gather | solution.py:46
  21.3 1.3 fusion.26
  22.6 1.6 collective-permute-start
  24.3 0.6 fusion.27
  24.9 9.8 %custom-call.25 = f32[2,1,64,64]{2,3,1,0:T(8,128)S(1)} custom-call(f32[2,1,64,64]{3,2,1,0:T(8,128)S(1)} %get-tuple-element.35), custom_call_target="InvertDiagBlocksLowerTriangular" | custom-call | tf_op jit(solution)/shard_map/vmap(jit(_solve_triangular))/triangular_solve | solution.py:22
  34.7 1.7 fusion.15
  36.4 33.3 %all_gather.10 = bf16[64,64,64]{2,1,0:T(8,128)(2,1)S(1)} all-gather(bf16[8,64,64]{2,1,0:T(8,128)(2,1)S(1)} %convert_element_type.21), channel_id=1, replica_groups=mesh['leaf'=8,'near'=4] {'leaf'}, dimensions={0}, use_global_device_ids=true | all-gather | bytes 589824 | tf_op jit(solution)/shard_map/all_gather | solution.py:78
  69.8 2.1 gather_fusion
  71.9 3.8 %copy.112 = bf16[128,64,64]{2,1,0:T(8,128)(2,1)} copy(bf16[128,64,64]{0,2,1:T(8,128)(2,1)S(1)} %copy-done.1) | data formatting | bytes 2097152 | tf_op args[3]
  75.7 2.2 gather_fusion.1
  77.9 4.7 %fusion.4 = bf16[128,64,64]{2,1,0:T(8,128)(2,1)S(1)} fusion(bf16[128,64,64]{2,1,0:T(8,128)(2,1)} %gather_fusion.1, bf16[128,64,64]{2,1,0:T(8,128)(2,1)} %gather_fusion, bf16[128,64,64]{2,1,0:T(8,128)(2,1)} %copy.112), kind=kOutput, calls=%fused_computation.7 | convolution fusion | flops 135266304 | bytes 4194304 | tf_op jit(solution)/shard_map/nkr,nlr->nkl/dot_general | solution.py:80
  82.6 2.9 %copy.115 = bf16[128,64,64]{0,2,1:T(8,128)(2,1)} copy(bf16[128,64,64]{2,1,0:T(8,128)(2,1)S(1)} %fusion.4) | data formatting | bytes 2097152
  85.6 0.6 convolution_add_fusion
  86.2 0.1 copy.103
  86.3 46.9 %custom-call.26 = f32[8,64,64]{2,1,0:T(8,128)S(1)} custom-call(f32[8,64,64]{2,1,0:T(8,128)S(1)} %fusion.9), custom_call_target="Cholesky" | custom-call | tf_op jit(solution)/shard_map/jit(cholesky)/cholesky | solution.py:49
  133.5 39.3 %custom-call.27 = f32[8,1,64,64]{2,3,1,0:T(8,128)S(1)} custom-call(f32[8,1,64,64]{3,2,1,0:T(8,128)S(1)} %get-tuple-element.32), custom_call_target="InvertDiagBlocksLowerTriangular" | custom-call | tf_op jit(solution)/shard_map/vmap(jit(_solve_triangular))/triangular_solve | solution.py:22
  172.8 1.1 fusion.7
  173.9 0.4 fusion.13
  174.4 0.4 fusion.28
  174.8 4.6 %collective-permute-done.1 = f32[4,64,64]{2,1,0:T(8,128)S(1)} collective-permute-done((f32[4,64,64]{2,1,0:T(8,128)S(1)}, f32[4,64,64]{2,1,0:T(8,128)S(1)}, u32[]{:S(2)}, u32[]{:S(2)}) %collective-permute-start.1) | collective-permute-done | bytes 65568 | tf_op jit(solution)/shard_map/ppermute | solution.py:12
  179.4 0.4 convolution_add_fusion.1
  179.9 23.5 %custom-call.28 = f32[4,64,64]{2,1,0:T(8,128)S(1)} custom-call(f32[4,64,64]{2,1,0:T(8,128)S(1)} %fusion.12), custom_call_target="Cholesky" | custom-call | tf_op jit(solution)/shard_map/jit(cholesky)/cholesky | solution.py:58
  203.4 0.1 compare_reduce_fusion.1
  203.6 19.7 %custom-call.29 = f32[4,1,64,64]{2,3,1,0:T(8,128)S(1)} custom-call(f32[4,1,64,64]{3,2,1,0:T(8,128)S(1)} %get-tuple-element.30), custom_call_target="InvertDiagBlocksLowerTriangular" | custom-call | tf_op jit(solution)/shard_map/vmap(jit(_solve_triangular))/triangular_solve | solution.py:22
  223.3 0.9 fusion.10
  224.3 30.7 %all_gather.11 = bf16[16,64,64]{2,1,0:T(8,128)(2,1)S(1)} all-gather(bf16[2,64,64]{2,1,0:T(8,128)(2,1)S(1)} %copy.113), channel_id=1, replica_groups=mesh['leaf'=8,'near'=4] {'leaf'}, dimensions={0}, use_global_device_ids=true | all-gather | bytes 147456 | tf_op jit(solution)/shard_map/all_gather | solution.py:66
  255.1 0.6 gather_fusion.3
  255.7 0.6 gather_fusion.2
  256.3 1.1 convolution_convert_fusion
  (45 shorter events, 1.1 us)
Async XLA Ops:
  0.6 255.7 %copy-start = (bf16[16,64,64]{2,1,0:T(8,128)(2,1)S(1)}, bf16[16,64,64]{2,1,0:T(8,128)(2,1)}, u32[]{:S(2)}) copy-start(bf16[16,64,64]{2,1,0:T(8,128)(2,1)} %param.17) | copy-start | bytes 393220
  2.0 67.7 %copy-start.3 = (s32[128]{0:T(128)S(1)}, s32[128]{0:T(128)}, u32[]{:S(2)}) copy-start(s32[128]{0:T(128)} %param.16) | copy-start | bytes 1540
  2.0 67.7 %copy-start.4 = (s32[128,1]{0,1:T(1,128)S(1)}, s32[128,1]{0,1:T(1,128)}, u32[]{:S(2)}) copy-start(s32[128,1]{0,1:T(1,128)} %param.15) | copy-start | bytes 1540
  2.0 67.7 %copy-start.5 = (s32[128]{0:T(128)S(1)}, s32[128]{0:T(128)}, u32[]{:S(2)}) copy-start(s32[128]{0:T(128)} %param.14) | copy-start | bytes 1540
  22.6 62.9 %collective-permute-start = (f32[8,64,64]{2,1,0:T(8,128)S(1)}, f32[8,64,64]{2,1,0:T(8,128)S(1)}, u32[]{:S(2)}, u32[]{:S(2)}) collective-permute-start(f32[8,64,64]{2,1,0:T(8,128)S(1)} %fusion.26), channel_id=1, source_target_pairs={{0,4},{4,0},{8,12},{12,8},{16,20},{20,16},{24,28},{28,24},{1,5},{5... | collective-permute-start | bytes 393224 | tf_op jit(solution)/shard_map/ppermute | solution.py:12
  69.8 2.1 copy-start.1
  71.9 3.8 %copy-start.6 = (s32[16]{0:T(128)S(1)}, s32[16]{0:T(128)}, u32[]{:S(2)}) copy-start(s32[16]{0:T(128)} %param.19) | copy-start | bytes 196
  75.7 2.2 copy-start.7
  85.5 88.4 %copy-start.2 = (f32[4,64,64]{2,1,0:T(8,128)S(1)}, f32[4,64,64]{2,1,0:T(8,128)}, u32[]{:S(2)}) copy-start(f32[4,64,64]{2,1,0:T(8,128)} %param.12) | copy-start | bytes 196612
  174.3 5.0 %collective-permute-start.1 = (f32[4,64,64]{2,1,0:T(8,128)S(1)}, f32[4,64,64]{2,1,0:T(8,128)S(1)}, u32[]{:S(2)}, u32[]{:S(2)}) collective-permute-start(f32[4,64,64]{2,1,0:T(8,128)S(1)} %fusion.13), channel_id=1, source_target_pairs={{0,8},{4,12},{8,0},{12,4},{16,24},{20,28},{24,16},{28,20},{1,9},{5... | collective-permute-start | bytes 196616 | tf_op jit(solution)/shard_map/ppermute | solution.py:12
where the time goes:
time: 258 us; the launch traced here: 257 us
  other arithmetic  152 us (59%)
  blocking collectives  71.2 us (28%)
  matrix products  14.3 us (6%)
  local copies, waits for them, and re-layouts  12.7 us (5%)
  waiting for transfers between devices  4.57 us (2%)
    another operation x6, other arithmetic, single(): jax.scipy.linalg.solve_triangular(factor_one, block_one.T, lower=True)  69 us
    another operation x3, other arithmetic, on_device(): lower_middle = jnp.linalg.cholesky(gram_of(child_piece) + gram_of(sibling))  47.1 us
    all_gather x1, blocking collectives, on_device(): every_factor = lax.all_gather(factor_low, 'leaf', axis=0, tiled=True)  33.3 us
    all_gather x1, blocking collectives, on_device(): gathered = lax.all_gather(top_mine, 'leaf', axis=0, tiled=True)  30.7 us
    another operation x3, other arithmetic, on_device(): lower_top = jnp.linalg.cholesky(gram_of(up_piece) + gram_of(cousin))  23.6 us
    another operation x4, other arithmetic, on_device(): lower_mine = jnp.linalg.cholesky(gram_of(my_bases))  11.9 us
    all_gather x1, blocking collectives, on_device(): lax.all_gather(jnp.swapaxes(lower_mine, 1, 2), 'near', axis=0, tiled=True)  7.19 us
    unnamed x18, local copies, waits for them, and re-layouts  6.78 us
  transfers between devices with their start and end apart: 2, of which 1 were waited for; matrix products, arithmetic and copies ran while one was open for 11% of the time, Pallas kernels for 0%

commit v1 on v0

v1 whole, which is shorter than its diff:
```python
import functools

import jax
import jax.numpy as jnp
from jax import lax
from jax.experimental import pallas as pl
from jax.experimental.pallas import tpu as pltpu
from jax.sharding import PartitionSpec as P

exact = lax.Precision.HIGHEST
f32 = jnp.float32
bf16 = jnp.bfloat16
BLOCK = 8
VMEM_LIMIT = 48 * 2**20


def swapped(value, axis, mask):
    pairs = [(source, source ^ mask) for source in range(lax.axis_size(axis))]
    return lax.ppermute(value, axis, pairs)


def gathered_by_xor(value, axis, bits):
    for bit in bits:
        value = jnp.concatenate([value, swapped(value, axis, 1 << bit)], axis=0)
    return value


def place_of(difference, bits):
    place = jnp.zeros_like(difference)
    for order, bit in enumerate(bits):
        place = place | (((difference >> bit) & 1) << order)
    return place


def dot_nn(a, b):
    return jnp.dot(a, b, precision=exact, preferred_element_type=f32)


def dot_tn(a, b):
    return lax.dot_general(a, b, (((0,), (0,)), ((), ())), precision=exact, preferred_element_type=f32)


def dot_nt(a, b):
    return lax.dot_general(a, b, (((1,), (1,)), ((), ())), precision=exact, preferred_element_type=f32)


def low_nn(a, b):
    return jnp.dot(a, b, preferred_element_type=f32).astype(bf16)


def low_nt(a, b):
    return lax.dot_general(a, b, (((1,), (1,)), ((), ())), preferred_element_type=f32).astype(bf16)


def across(rows, lane):
    return jnp.broadcast_to(rows[:, lane : lane + 1], rows.shape)


def reciprocal(value):
    guess = pltpu.reciprocal(value, approx=True)
    return guess * (2.0 - value * guess)


def square_places(rank):
    return (
        lax.broadcasted_iota(jnp.int32, (rank, rank), 0),
        lax.broadcasted_iota(jnp.int32, (rank, rank), 1),
    )


def put_matrix(work, place, gram):
    rank = gram.shape[0]
    rows, columns = square_places(rank)
    identity = (rows == columns).astype(f32)
    work[pl.ds(place, rank, stride=8), :] = jnp.concatenate([gram, identity], axis=1)


def eliminate(work, rank):
    def read(i):
        return work[i * 8 : (i + 1) * 8, :]

    for start in range(0, rank, BLOCK):
        rows = [read(start + a) for a in range(BLOCK)]
        entry = [[across(rows[a], start + b) if b >= a else None for b in range(BLOCK)] for a in range(BLOCK)]
        inverse = []
        for a in range(BLOCK):
            inverse.append(reciprocal(entry[a][a]))
            for b in range(a + 1, BLOCK):
                share = entry[a][b] * inverse[a]
                for c in range(b, BLOCK):
                    entry[b][c] = entry[b][c] - share * entry[a][c]
                rows[b] = rows[b] - share * rows[a]
        for a in range(1, BLOCK):
            work[(start + a) * 8 : (start + a + 1) * 8, :] = rows[a]
        scaled = [rows[a] * inverse[a] for a in range(BLOCK)]
        for i in range(start + BLOCK, rank):
            total = read(i)
            for a in range(BLOCK):
                total = total - across(scaled[a], i) * rows[a]
            work[i * 8 : (i + 1) * 8, :] = total


def take_matrix(work, place, rank):
    rows, columns = square_places(rank)
    both = work[pl.ds(place, rank, stride=8), :]
    diagonal = jnp.sum(jnp.where(rows == columns, both[:, :rank], 0.0), axis=1, keepdims=True)
    both = both * lax.rsqrt(diagonal)
    factor = jnp.where(columns >= rows, both[:, :rank], 0.0)
    return factor, both[:, rank:]


def leaf_kernel(bases, transfer, low, low_pairs, piece, gram, inverse, work):
    count, _, rank = bases.shape
    for b in range(count):
        put_matrix(work, b, dot_tn(bases[b], bases[b]))
    eliminate(work, rank)
    for pair in range(count // 2):
        grams, lows = [], []
        for b in (2 * pair, 2 * pair + 1):
            factor, inverse_part = take_matrix(work, b, rank)
            child = dot_nn(factor, transfer[b])
            piece[b] = child
            inverse[b] = inverse_part
            low[b] = factor.astype(bf16)
            lows.append(factor)
            grams.append(dot_tn(child, child))
        gram[pair] = jnp.concatenate(grams, axis=1)
        low_pairs[pair] = jnp.concatenate(lows, axis=1).astype(bf16)


def put_sums(work, mine, other, rank):
    for pair in range(mine.shape[0]):
        total = mine[pair] + other[pair]
        put_matrix(work, 2 * pair, total[:, :rank])
        put_matrix(work, 2 * pair + 1, total[:, rank:])


def middle_kernel(spot, mine, other, piece, top_mine, top_other, transfers, up, gram, work):
    count, _, rank = piece.shape
    half = count // 2
    put_sums(work, mine, other, rank)
    eliminate(work, rank)
    near, parity = spot[0], spot[1]
    grams = []
    for slot in range(count):
        place = (slot % half) + half * (parity if slot < half else 1 - parity)
        factor, inverse_part = take_matrix(work, place, rank)
        transfers[place] = dot_nt(piece[place], inverse_part)
        raised = dot_nn(factor, (top_mine if slot < half else top_other)[slot % half])
        if slot < half:
            up[slot] = raised
        grams.append(dot_tn(raised, raised))
        if slot % 2:
            gram[slot // 2] = jnp.concatenate(grams[-2:], axis=1)


def top_kernel(mine, other, up, transfers, low_pairs, work):
    half, _, rank = up.shape
    put_sums(work, mine, other, rank)
    eliminate(work, rank)
    lows = []
    for slot in range(2 * half):
        factor, inverse_part = take_matrix(work, slot, rank)
        if slot < half:
            transfers[slot] = dot_nt(up[slot], inverse_part)
        lows.append(factor)
        if slot % 2:
            low_pairs[slot // 2] = jnp.concatenate(lows[-2:], axis=1).astype(bf16)


def half_kernel(spot, target, source, couplings, low, bases, inverse, halves, leaf_bases):
    count, rank, _ = couplings.shape
    share = leaf_bases.shape[0]
    for k in range(share):
        place = spot[0] * share + k
        leaf_bases[k] = dot_nt(bases[place], inverse[place])

    def step(r, carry):
        product = low_nn(low[target[r]], couplings[r])
        odd = source[r] % 2
        halves[r, :, :rank] = jnp.where(odd == 0, product, jnp.zeros_like(product))
        halves[r, :, rank:] = jnp.where(odd == 1, product, jnp.zeros_like(product))
        return carry

    lax.fori_loop(0, count, step, 0, unroll=8)


def full_kernel(source, halves, table, out):
    count = halves.shape[0]

    def step(r, carry):
        out[r] = low_nt(halves[r], table[source[r] // 2])
        return carry

    lax.fori_loop(0, count, step, 0, unroll=8)


def top_project_kernel(target, source, couplings, table, out):
    count, rank, _ = couplings.shape
    for r in range(count):
        left, right = table[target[r] // 2], table[source[r] // 2]
        left = jnp.where(target[r] % 2 == 0, left[:, :rank], left[:, rank:])
        right = jnp.where(source[r] % 2 == 0, right[:, :rank], right[:, rank:])
        out[r] = low_nt(low_nn(left, couplings[r]), right)


vmem = pl.BlockSpec(memory_space=pltpu.VMEM)
smem = pl.BlockSpec(memory_space=pltpu.SMEM)


def call(kernel, scalars, arrays, outs, scratch=()):
    return pl.pallas_call(
        kernel,
        out_shape=[jax.ShapeDtypeStruct(shape, dtype) for shape, dtype in outs],
        in_specs=[smem] * len(scalars) + [vmem] * len(arrays),
        out_specs=[vmem] * len(outs),
        scratch_shapes=list(scratch),
        compiler_params=pltpu.CompilerParams(vmem_limit_bytes=VMEM_LIMIT),
    )(*scalars, *arrays)


def on_device(
    bases,
    leaf_transfer,
    top_transfer,
    couplings,
    coupling_target,
    coupling_dest,
    coupling_local,
    top_couplings,
    top_target,
    top_source,
):
    leaves, _, rank = bases.shape
    half, pairs = leaves // 2, leaves // 2
    share = leaves // lax.axis_size("near")
    blocks, top_blocks = couplings.shape[0], top_couplings.shape[0]
    leaf_bits = list(range(lax.axis_size("leaf").bit_length() - 1))[::-1]
    quad_bits = [bit - 2 for bit in leaf_bits if bit >= 2]
    near_place, leaf_place = lax.axis_index("near"), lax.axis_index("leaf")
    parity = leaf_place % 2
    spot = jnp.stack([near_place, parity]).astype(jnp.int32)
    work = [pltpu.VMEM((8 * rank, 2 * rank), f32)]
    square = (rank, rank)
    wide = (rank, 2 * rank)

    source = place_of(coupling_dest[:, 0] ^ leaf_place, leaf_bits) * leaves + coupling_local
    top_left = top_target ^ (half * parity)
    top_right = place_of((top_source // leaves) ^ (leaf_place // 4), quad_bits) * leaves + (
        (top_source % leaves) ^ (half * parity)
    )

    top_other = swapped(top_transfer, "leaf", 1)
    low, low_pairs, piece, gram, inverse = call(
        leaf_kernel,
        [],
        [bases, leaf_transfer],
        [
            ((leaves, *square), bf16),
            ((pairs, *wide), bf16),
            ((leaves, *square), f32),
            ((pairs, *wide), f32),
            ((leaves, *square), f32),
        ],
        work,
    )
    gram_other = swapped(gram, "leaf", 1)
    halves, leaf_bases = call(
        half_kernel,
        [spot, coupling_target, source],
        [couplings, low, bases, inverse],
        [((blocks, *wide), bf16), ((share, *square), f32)],
    )
    table = gathered_by_xor(low_pairs, "leaf", leaf_bits)
    leaf_transfers, up, up_gram = call(
        middle_kernel,
        [spot],
        [gram, gram_other, piece, top_transfer, top_other],
        [((leaves, *square), f32), ((half, *square), f32), ((pairs, *wide), f32)],
        work,
    )
    up_other = swapped(up_gram, "leaf", 2)
    top_transfers, top_pairs = call(
        top_kernel,
        [],
        [up_gram, up_other, up],
        [((half, *square), f32), ((pairs, *wide), bf16)],
        work,
    )
    top_table = gathered_by_xor(top_pairs, "leaf", [bit + 2 for bit in quad_bits])
    (new_couplings,) = call(
        full_kernel, [source], [halves, table], [((blocks, *square), bf16)]
    )
    (new_top_couplings,) = call(
        top_project_kernel,
        [top_left, top_right],
        [top_couplings, top_table],
        [((top_blocks, *square), bf16)],
    )
    return (leaf_bases, leaf_transfers, top_transfers, new_couplings, new_top_couplings)


def solution(mesh):
    in_specs = (
        P("leaf", None, None),
        P("leaf", None, None),
        P("leaf", None, None),
        P(("leaf", "near"), None, None),
        P(("leaf", "near")),
        P(("leaf", "near"), None),
        P(("leaf", "near")),
        P(("leaf", "near"), None, None),
        P(("leaf", "near")),
        P(("leaf", "near")),
    )
    out_specs = (
        P(("leaf", "near"), None, None),
        P("leaf", None, None),
        P("leaf", None, None),
        P(("leaf", "near"), None, None),
        P(("leaf", "near"), None, None),
    )
    return jax.shard_map(
        on_device, mesh=mesh, in_specs=in_specs, out_specs=out_specs, check_vma=False
    )
```

time: 258 us -> 61.5 us (0.24)
  other arithmetic: 152 us -> 2.53 us
  blocking collectives: 71.2 us -> 0 us
  Pallas kernels: 0 us -> 31.3 us
  matrix products: 14.3 us -> 0 us
  starting transfers between devices: 1.7 us -> 13.2 us
  local copies, waits for them, and re-layouts: 12.7 us -> 9.63 us
    another operation x16 -> x1, other arithmetic: 152 us -> 0.07 us  [on_device(): spot = jnp.stack([near_place, parity]).astype(jnp.int32)]
    all_gather x3 -> x0, blocking collectives: 71.2 us -> none  [the longest x1 33.3 us: on_device(): every_factor = lax.all_gather(factor_low, 'leaf', axis=0, tiled=True)]
    pallas_call x0 -> x6, Pallas kernels: none -> 31.3 us  [call(): pl.pallas_call(kernel, out_shape=[jax.ShapeDtypeStruct(shape, dtype) for...]
    ppermute x2 -> x7, starting transfers between devices: 1.7 us -> 13.2 us  [swapped(): return lax.ppermute(value, axis, pairs)]
    dot_general x9 -> x0, matrix products: 10.6 us -> none  [the longest x1 4.67 us: on_device(): jnp.einsum('nkr,nlr->nkl', halves, source_rows, preferred_element_type=jn...]
    gather x4 -> x0, local copies, waits for them, and re-layouts: 5.47 us -> none  [the longest x1 2.17 us: on_device(): source_rows = every_factor[destination * leaves_here + coupling_local]]
    another operation x3 -> x0, matrix products: 3.71 us -> none  [single(): jax.scipy.linalg.solve_triangular(factor_one, block_one.T, lower=True)]
    unnamed x18, local copies, waits for them, and re-layouts: 6.78 us -> 9.63 us
  transfers between devices with their start and end apart: 2 -> 7, of which waited for: 1 -> 2; matrix products, arithmetic and copies ran while one was open for 11% -> 9% of each run, Pallas kernels for 0% -> 36%
where the time goes in v1:
time: 61.5 us; the launch traced here: 61.2 us
  Pallas kernels  31.3 us (51%)
  starting transfers between devices  13.2 us (21%)
  local copies, waits for them, and re-layouts  9.63 us (16%)
  waiting for transfers between devices  3.78 us (6%)
  other arithmetic  2.53 us (4%)
  between operations  0.73 us (1%)
    pallas_call x6, Pallas kernels, call(): pl.pallas_call(kernel, out_shape=[jax.ShapeDtypeStruct(shape, dtype) for...  31.3 us
    ppermute x7, starting transfers between devices, swapped(): return lax.ppermute(value, axis, pairs)  13.2 us
    unnamed x18, local copies, waits for them, and re-layouts  9.63 us
    ppermute x7, waiting for transfers between devices, swapped(): return lax.ppermute(value, axis, pairs)  3.78 us
    concatenate x4, other arithmetic, gathered_by_xor(): value = jnp.concatenate([value, swapped(value, axis, 1 << bit)], axis=0)  1.76 us
  transfers between devices with their start and end apart: 7, of which 2 were waited for; matrix products, arithmetic and copies ran while one was open for 9% of the time, Pallas kernels for 36%

profile of v1, /device:TPU:0, one launch (start us, length us, event | category | flops | bytes accessed | tf_op | source)
XLA Modules:
  0.0 61.2 jit_solution(12058503645292344373)
XLA Ops:
  0.6 0.0 copy-start
  0.6 0.9 %copy-done = f32[8,64,64]{2,1,0:T(8,128)S(1)} copy-done((f32[8,64,64]{2,1,0:T(8,128)S(1)}, f32[8,64,64]{2,1,0:T(8,128)}, u32[]{:S(2)}) %copy-start) | copy-done | bytes 131096
  1.6 0.9 %copy-done.3 = f32[8,64,64]{2,1,0:T(8,128)S(1)} copy-done((f32[8,64,64]{2,1,0:T(8,128)S(1)}, f32[8,64,64]{2,1,0:T(8,128)}, u32[]{:S(2)}) %copy-start.3) | copy-done | bytes 131096
  2.5 5.6 %shard_map.137 = (bf16[8,64,64]{2,1,0:T(8,128)(2,1)S(1)}, bf16[4,64,128]{2,1,0:T(8,128)(2,1)S(1)}, f32[8,64,64]{2,1,0:T(8,128)S(1)}, f32[4,64,128]{2,1,0:T(8,128)S(1)}, f32[8,64,64]{2,1,0:T(8,128)S(1)}) custom-call(f32[8,64,64]{2,1,0:T(8,128)S(1)} %copy-done, f32[8,64,64]{2,1,0:T(8,128)S(1)} %copy-done.3), custom_call_target="tpu_custom_call" | custom-call | tf_op jit(solution)/shard_map/pallas_call | solution.py:212
  8.1 3.0 %collective-permute-start = (f32[4,64,128]{2,1,0:T(8,128)S(1)}, f32[4,64,128]{2,1,0:T(8,128)S(1)}, u32[]{:S(2)}, u32[]{:S(2)}) collective-permute-start(f32[4,64,128]{2,1,0:T(8,128)S(1)} %get-tuple-element.20.mine), channel_id=1, source_target_pairs={{0,4},{4,0},{8,12},{12,8},{16,20},{20,16},{24,28},{28,24},{1,5},{5... | collective-permute-start | bytes 393224 | tf_op jit(solution)/shard_map/ppermute | solution.py:19
  11.2 0.1 collective-permute-start.1
  11.2 3.0 %collective-permute-start.3 = (bf16[4,64,128]{2,1,0:T(8,128)(2,1)S(1)}, bf16[4,64,128]{2,1,0:T(8,128)(2,1)S(1)}, u32[]{:S(2)}, u32[]{:S(2)}) collective-permute-start(bf16[4,64,128]{2,1,0:T(8,128)(2,1)S(1)} %get-tuple-element.27), channel_id=1, source_target_pairs={{0,16},{4,20},{8,24},{12,28},{16,0},{20,4},{24,8},{28,12},{1,17},{... | collective-permute-start | bytes 196616 | tf_op jit(solution)/shard_map/ppermute | solution.py:19
  14.2 0.1 pad_add_fusion.spot
  14.3 2.5 %collective-permute-done.3 = bf16[4,64,128]{2,1,0:T(8,128)(2,1)S(1)} collective-permute-done((bf16[4,64,128]{2,1,0:T(8,128)(2,1)S(1)}, bf16[4,64,128]{2,1,0:T(8,128)(2,1)S(1)}, u32[]{:S(2)}, u32[]{:S(2)}) %collective-permute-start.3) | collective-permute-done | bytes 65568 | tf_op jit(solution)/shard_map/ppermute | solution.py:19
  16.9 1.6 %collective-permute-start.4 = (bf16[8,64,128]{2,1,0:T(8,128)(2,1)S(1)}, bf16[8,64,128]{2,1,0:T(8,128)(2,1)S(1)}, u32[]{:S(2)}, u32[]{:S(2)}) collective-permute-start(bf16[8,64,128]{2,1,0:T(8,128)(2,1)S(1)} %pad_maximum_fusion.2), channel_id=1, source_target_pairs={{0,8},{4,12},{8,0},{12,4},{16,24},{20,28},{24,16},{28,20},{1,9},{5... | collective-permute-start | bytes 393224 | tf_op jit(solution)/shard_map/ppermute | solution.py:19
  18.5 0.0 collective-permute-done.1.top_other
  18.5 0.0 collective-permute-done.other
  18.5 0.9 %copy-done.4 = f32[4,64,64]{2,1,0:T(8,128)S(1)} copy-done((f32[4,64,64]{2,1,0:T(8,128)S(1)}, f32[4,64,64]{2,1,0:T(8,128)}, u32[]{:S(2)}) %copy-start.4) | copy-done | bytes 65560
  19.4 8.1 %shard_map.139 = (f32[8,64,64]{2,1,0:T(8,128)}, f32[4,64,64]{2,1,0:T(8,128)S(1)}, f32[4,64,128]{2,1,0:T(8,128)S(1)}) custom-call(s32[2]{0:T(128)S(1)} %pad_add_fusion.spot, f32[4,64,128]{2,1,0:T(8,128)S(1)} %get-tuple-element.20.mine, f32[4,64,128]{2,1,0:T(8,128)S(1)} %collective-permute-done.other, f32[8,64,64]{2,1,0:T(8,128)S(1)} %get-tuple-element.21.piece, ...), custom_call_target="tpu_custom_call" | custom-call | tf_op jit(solution)/shard_map/pallas_call | solution.py:212
  27.5 0.8 %collective-permute-start.2 = (f32[4,64,128]{2,1,0:T(8,128)S(1)}, f32[4,64,128]{2,1,0:T(8,128)S(1)}, u32[]{:S(2)}, u32[]{:S(2)}) collective-permute-start(f32[4,64,128]{2,1,0:T(8,128)S(1)} %get-tuple-element.23.mine), channel_id=1, source_target_pairs={{0,8},{4,12},{8,0},{12,4},{16,24},{20,28},{24,16},{28,20},{1,9},{5... | collective-permute-start | bytes 393224 | tf_op jit(solution)/shard_map/ppermute | solution.py:19
  28.3 0.7 %fusion.1 = (s32[16]{0:T(128)S(1)}, s32[16]{0:T(128)S(1)}) fusion(s32[16]{0:T(128)} %param.19, s32[]{:T(128)S(6)} %select_n.24, s32[]{:T(128)S(6)} %mul.15, s32[16]{0:T(128)} %param.18), kind=kLoop, calls=%fused_computation.10 | loop fusion | flops 432 | bytes 264 | tf_op jit(solution)/shard_map/add | solution.py:249
  29.0 0.0 collective-permute-done.4
  29.0 0.7 %pad_maximum_fusion.1 = bf16[16,64,128]{2,1,0:T(8,128)(2,1)} fusion(bf16[8,64,128]{2,1,0:T(8,128)(2,1)S(1)} %collective-permute-done.4, bf16[4,64,128]{2,1,0:T(8,128)(2,1)S(1)} %collective-permute-done.3, bf16[4,64,128]{2,1,0:T(8,128)(2,1)S(1)} %get-tuple-element.27), kind=kLoop, calls=%fused_computation.1 | loop fusion | flops 262144 | bytes 524288 | tf_op jit(solution)/shard_map/concatenate | solution.py:24
  29.7 1.5 %collective-permute-start.5 = (bf16[16,64,128]{2,1,0:T(8,128)(2,1)}, bf16[16,64,128]{2,1,0:T(8,128)(2,1)}, u32[]{:S(2)}, u32[]{:S(2)}) collective-permute-start(bf16[16,64,128]{2,1,0:T(8,128)(2,1)} %pad_maximum_fusion.1), channel_id=1, source_target_pairs={{0,4},{4,0},{8,12},{12,8},{16,20},{20,16},{24,28},{28,24},{1,5},{5... | collective-permute-start | bytes 786440 | tf_op jit(solution)/shard_map/ppermute | solution.py:19
  31.2 1.3 %collective-permute-done.2.other = f32[4,64,128]{2,1,0:T(8,128)S(1)} collective-permute-done((f32[4,64,128]{2,1,0:T(8,128)S(1)}, f32[4,64,128]{2,1,0:T(8,128)S(1)}, u32[]{:S(2)}, u32[]{:S(2)}) %collective-permute-start.2) | collective-permute-done | bytes 131104 | tf_op jit(solution)/shard_map/ppermute | solution.py:19
  32.5 5.6 %shard_map.140 = (f32[4,64,64]{2,1,0:T(8,128)}, bf16[4,64,128]{2,1,0:T(8,128)(2,1)S(1)}) custom-call(f32[4,64,128]{2,1,0:T(8,128)S(1)} %get-tuple-element.23.mine, f32[4,64,128]{2,1,0:T(8,128)S(1)} %collective-permute-done.2.other, f32[4,64,64]{2,1,0:T(8,128)S(1)} %get-tuple-element.24.up), custom_call_target="tpu_custom_call" | custom-call | tf_op jit(solution)/shard_map/pallas_call | solution.py:212
  38.1 3.2 %collective-permute-start.6 = (bf16[4,64,128]{2,1,0:T(8,128)(2,1)S(1)}, bf16[4,64,128]{2,1,0:T(8,128)(2,1)S(1)}, u32[]{:S(2)}, u32[]{:S(2)}) collective-permute-start(bf16[4,64,128]{2,1,0:T(8,128)(2,1)S(1)} %get-tuple-element.28), channel_id=1, source_target_pairs={{0,16},{4,20},{8,24},{12,28},{16,0},{20,4},{24,8},{28,12},{1,17},{... | collective-permute-start | bytes 196616 | tf_op jit(solution)/shard_map/ppermute | solution.py:19
  41.3 0.0 copy-done.6
  41.3 3.9 %copy.15.couplings = bf16[128,64,64]{2,1,0:T(8,128)(2,1)S(1)} copy(bf16[128,64,64]{0,2,1:T(8,128)(2,1)} %param.13) | data formatting | bytes 2097152 | tf_op args[3]
  45.2 0.0 copy-start.2
  45.2 5.7 %shard_map.138 = (bf16[128,64,128]{2,1,0:T(8,128)(2,1)S(1)}, f32[2,64,64]{2,1,0:T(8,128)}) custom-call(s32[2]{0:T(128)S(1)} %pad_add_fusion.spot, s32[128]{0:T(128)S(1)} %copy-done.5, s32[128]{0:T(128)S(1)} %bitcast_add_fusion.source, bf16[128,64,64]{2,1,0:T(8,128)(2,1)S(1)} %copy.15.couplings, bf16[8,64,64]{2,1,0:T(8,128)(2,1)S(1)} %get-tuple-element.17.low, ...), custom_call_target="tpu_custom_call" | custom-call | tf_op jit(solution)/shard_map/pallas_call | solution.py:212
  50.9 0.0 collective-permute-done.6
  50.9 2.5 %shard_map.142 = bf16[16,64,64]{2,1,0:T(8,128)(2,1)} custom-call(s32[16]{0:T(128)S(1)} %get-tuple-element.35.target, s32[16]{0:T(128)S(1)} %get-tuple-element.34.source, bf16[16,64,64]{2,1,0:T(8,128)(2,1)S(1)} %copy-done.2, bf16[8,64,128]{2,1,0:T(8,128)(2,1)S(1)} %pad_maximum_fusion.3.table), custom_call_target="tpu_custom_call" | custom-call | tf_op jit(solution)/shard_map/pallas_call | solution.py:212
  53.4 0.0 collective-permute-done.5
  53.4 1.0 %pad_maximum_fusion.table = bf16[32,64,128]{2,1,0:T(8,128)(2,1)S(1)} fusion(bf16[16,64,128]{2,1,0:T(8,128)(2,1)} %collective-permute-done.5, bf16[8,64,128]{2,1,0:T(8,128)(2,1)S(1)} %collective-permute-done.4, bf16[4,64,128]{2,1,0:T(8,128)(2,1)S(1)} %collective-permute-done.3, bf16[4,64,128]{2,1,0:T(8,128)(2,1)S(1)} %get-tuple-element.27), kind=kLoop, calls=%fused_computation | loop fusion | flops 786432 | bytes 1048576 | tf_op jit(solution)/shard_map/concatenate | solution.py:24
  54.5 3.8 %shard_map.141 = bf16[128,64,64]{2,1,0:T(8,128)(2,1)S(1)} custom-call(s32[128]{0:T(128)S(1)} %bitcast_add_fusion.source, bf16[128,64,128]{2,1,0:T(8,128)(2,1)S(1)} %get-tuple-element.26.halves, bf16[32,64,128]{2,1,0:T(8,128)(2,1)S(1)} %pad_maximum_fusion.table), custom_call_target="tpu_custom_call" | custom-call | tf_op jit(solution)/shard_map/pallas_call | solution.py:212
  58.3 2.9 %copy.16 = bf16[128,64,64]{0,2,1:T(8,128)(2,1)} copy(bf16[128,64,64]{2,1,0:T(8,128)(2,1)S(1)} %shard_map.141) | data formatting | bytes 2097152
  (13 shorter events, 0.1 us)
Async XLA Ops:
  0.6 1.0 %copy-start = (f32[8,64,64]{2,1,0:T(8,128)S(1)}, f32[8,64,64]{2,1,0:T(8,128)}, u32[]{:S(2)}) copy-start(f32[8,64,64]{2,1,0:T(8,128)} %bases.3) | copy-start | bytes 393220
  1.6 0.9 %copy-start.3 = (f32[8,64,64]{2,1,0:T(8,128)S(1)}, f32[8,64,64]{2,1,0:T(8,128)}, u32[]{:S(2)}) copy-start(f32[8,64,64]{2,1,0:T(8,128)} %transfer.1) | copy-start | bytes 393220
  2.5 38.8 %copy-start.6 = (s32[128]{0:T(128)S(1)}, s32[128]{0:T(128)}, u32[]{:S(2)}) copy-start(s32[128]{0:T(128)} %param.16) | copy-start | bytes 1540
  2.5 38.8 %copy-start.7 = (s32[128,1]{0,1:T(1,128)S(1)}, s32[128,1]{0,1:T(1,128)}, u32[]{:S(2)}) copy-start(s32[128,1]{0,1:T(1,128)} %param.15) | copy-start | bytes 1540
  8.1 10.4 %collective-permute-start = (f32[4,64,128]{2,1,0:T(8,128)S(1)}, f32[4,64,128]{2,1,0:T(8,128)S(1)}, u32[]{:S(2)}, u32[]{:S(2)}) collective-permute-start(f32[4,64,128]{2,1,0:T(8,128)S(1)} %get-tuple-element.20.mine), channel_id=1, source_target_pairs={{0,4},{4,0},{8,12},{12,8},{16,20},{20,16},{24,28},{28,24},{1,5},{5... | collective-permute-start | bytes 393224 | tf_op jit(solution)/shard_map/ppermute | solution.py:19
  11.2 7.3 %collective-permute-start.1 = (f32[4,64,64]{2,1,0:T(8,128)}, f32[4,64,64]{2,1,0:T(8,128)S(1)}, u32[]{:S(2)}, u32[]{:S(2)}) collective-permute-start(f32[4,64,64]{2,1,0:T(8,128)} %top_mine.1), channel_id=1, source_target_pairs={{0,4},{4,0},{8,12},{12,8},{16,20},{20,16},{24,28},{28,24},{1,5},{5... | collective-permute-start | bytes 196616 | tf_op jit(solution)/shard_map/ppermute | solution.py:19
  11.2 5.6 %collective-permute-start.3 = (bf16[4,64,128]{2,1,0:T(8,128)(2,1)S(1)}, bf16[4,64,128]{2,1,0:T(8,128)(2,1)S(1)}, u32[]{:S(2)}, u32[]{:S(2)}) collective-permute-start(bf16[4,64,128]{2,1,0:T(8,128)(2,1)S(1)} %get-tuple-element.27), channel_id=1, source_target_pairs={{0,16},{4,20},{8,24},{12,28},{16,0},{20,4},{24,8},{28,12},{1,17},{... | collective-permute-start | bytes 196616 | tf_op jit(solution)/shard_map/ppermute | solution.py:19
  16.9 12.1 %collective-permute-start.4 = (bf16[8,64,128]{2,1,0:T(8,128)(2,1)S(1)}, bf16[8,64,128]{2,1,0:T(8,128)(2,1)S(1)}, u32[]{:S(2)}, u32[]{:S(2)}) collective-permute-start(bf16[8,64,128]{2,1,0:T(8,128)(2,1)S(1)} %pad_maximum_fusion.2), channel_id=1, source_target_pairs={{0,8},{4,12},{8,0},{12,4},{16,24},{20,28},{24,16},{28,20},{1,9},{5... | collective-permute-start | bytes 393224 | tf_op jit(solution)/shard_map/ppermute | solution.py:19
  18.5 0.9 %copy-start.4 = (f32[4,64,64]{2,1,0:T(8,128)S(1)}, f32[4,64,64]{2,1,0:T(8,128)}, u32[]{:S(2)}) copy-start(f32[4,64,64]{2,1,0:T(8,128)} %top_mine.1) | copy-start | bytes 196612
  27.5 17.7 %copy-start.1 = (f32[8,64,64]{2,1,0:T(8,128)S(1)}, f32[8,64,64]{2,1,0:T(8,128)}, u32[]{:S(2)}) copy-start(f32[8,64,64]{2,1,0:T(8,128)} %bases.3) | copy-start | bytes 393220
  27.5 17.7 %copy-start.5 = (s32[128]{0:T(128)S(1)}, s32[128]{0:T(128)}, u32[]{:S(2)}) copy-start(s32[128]{0:T(128)} %target.1) | copy-start | bytes 1540
  27.5 5.0 %collective-permute-start.2 = (f32[4,64,128]{2,1,0:T(8,128)S(1)}, f32[4,64,128]{2,1,0:T(8,128)S(1)}, u32[]{:S(2)}, u32[]{:S(2)}) collective-permute-start(f32[4,64,128]{2,1,0:T(8,128)S(1)} %get-tuple-element.23.mine), channel_id=1, source_target_pairs={{0,8},{4,12},{8,0},{12,4},{16,24},{20,28},{24,16},{28,20},{1,9},{5... | collective-permute-start | bytes 393224 | tf_op jit(solution)/shard_map/ppermute | solution.py:19
  29.7 23.7 %collective-permute-start.5 = (bf16[16,64,128]{2,1,0:T(8,128)(2,1)}, bf16[16,64,128]{2,1,0:T(8,128)(2,1)}, u32[]{:S(2)}, u32[]{:S(2)}) collective-permute-start(bf16[16,64,128]{2,1,0:T(8,128)(2,1)} %pad_maximum_fusion.1), channel_id=1, source_target_pairs={{0,4},{4,0},{8,12},{12,8},{16,20},{20,16},{24,28},{28,24},{1,5},{5... | collective-permute-start | bytes 786440 | tf_op jit(solution)/shard_map/ppermute | solution.py:19
  38.1 12.8 %collective-permute-start.6 = (bf16[4,64,128]{2,1,0:T(8,128)(2,1)S(1)}, bf16[4,64,128]{2,1,0:T(8,128)(2,1)S(1)}, u32[]{:S(2)}, u32[]{:S(2)}) collective-permute-start(bf16[4,64,128]{2,1,0:T(8,128)(2,1)S(1)} %get-tuple-element.28), channel_id=1, source_target_pairs={{0,16},{4,20},{8,24},{12,28},{16,0},{20,4},{24,8},{28,12},{1,17},{... | collective-permute-start | bytes 196616 | tf_op jit(solution)/shard_map/ppermute | solution.py:19
  45.2 5.7 %copy-start.2 = (bf16[16,64,64]{2,1,0:T(8,128)(2,1)S(1)}, bf16[16,64,64]{2,1,0:T(8,128)(2,1)}, u32[]{:S(2)}) copy-start(bf16[16,64,64]{2,1,0:T(8,128)(2,1)} %couplings.2) | copy-start | bytes 393220

commit v2 on v0

v2 whole, which is shorter than its diff:
```python
import functools

import jax
import jax.numpy as jnp
from jax import lax
from jax.experimental import pallas as pl
from jax.experimental.pallas import tpu as pltpu
from jax.sharding import PartitionSpec as P

exact = lax.Precision.HIGHEST
f32 = jnp.float32
bf16 = jnp.bfloat16
BLOCK = 8
GROUP = 4
PITCH_EXTRA = 8
VMEM_LIMIT = 48 * 2**20


def swapped(value, axis, mask):
    pairs = [(source, source ^ mask) for source in range(lax.axis_size(axis))]
    return lax.ppermute(value, axis, pairs)


def gathered_by_xor(value, axis, bits):
    values = [value]
    for bit in bits:
        values = values + [swapped(one, axis, 1 << bit) for one in values]
    return values


def place_of(difference, bits):
    place = jnp.zeros_like(difference)
    for order, bit in enumerate(bits):
        place = place | (((difference >> bit) & 1) << order)
    return place


def dot_nn(a, b):
    return jnp.dot(a, b, precision=exact, preferred_element_type=f32)


def dot_tn(a, b):
    return lax.dot_general(a, b, (((0,), (0,)), ((), ())), precision=exact, preferred_element_type=f32)


def dot_nt(a, b):
    return lax.dot_general(a, b, (((1,), (1,)), ((), ())), precision=exact, preferred_element_type=f32)


def low_nn(a, b):
    return jnp.dot(a, b, preferred_element_type=f32)


def low_nt(a, b):
    return lax.dot_general(a, b, (((1,), (1,)), ((), ())), preferred_element_type=f32)


def eliminate(work, factor, inverse):
    rank = work.shape[1] // 2
    shape = (2 * GROUP, 2 * rank)
    lanes = lax.broadcasted_iota(jnp.int32, shape, 1)
    odd = lax.broadcasted_iota(jnp.int32, shape, 0) // GROUP
    upper = odd == 0
    column = lanes % rank
    side = lanes - column

    def pick(rows, index):
        return jnp.take_along_axis(rows, index, axis=1)

    def span(pair):
        return pl.ds(2 * GROUP * pair, 2 * GROUP)

    for start in range(0, rank, BLOCK):
        inside = (column >= start) & (column < start + BLOCK)
        rows = []
        for pair in range(start // 2, (start + BLOCK) // 2):
            both = work[span(pair), :]
            turned = pltpu.roll(both, GROUP, axis=0)
            rows += [jnp.where(upper, both, turned), jnp.where(upper, turned, both)]
        done = [(column == start + a).astype(f32) for a in range(BLOCK)]
        entry = [[pick(rows[a], side + (start + b)) if b >= a else None for b in range(BLOCK)] for a in range(BLOCK)]
        scaled = []
        for a in range(BLOCK):
            pivot = pltpu.reciprocal(entry[a][a], approx=True)
            scaled.append(rows[a] * pivot)
            for b in range(a + 1, BLOCK):
                share = entry[a][b] * pivot
                for c in range(b, BLOCK):
                    entry[b][c] = entry[b][c] - share * entry[a][c]
                rows[b] = rows[b] - share * rows[a]
                done[b] = done[b] - share * done[a]
        mixed = [jnp.where(inside, done[a], rows[a]) for a in range(BLOCK)]
        for pair in range((start + BLOCK) // 2, rank // 2):
            total = jnp.where(inside, 0.0, work[span(pair), :])
            index = side + odd + 2 * pair
            for a in range(BLOCK):
                total = total - pick(scaled[a], index) * mixed[a]
            work[span(pair), :] = total
        for a in range(0, BLOCK, 2):
            pair = (start + a) // 2
            row = odd + 2 * pair
            scale = lax.rsqrt(jnp.where(upper, entry[a][a], entry[a + 1][a + 1]))
            factor[span(pair), :] = jnp.where(
                column >= row, jnp.where(upper, rows[a], rows[a + 1]) * scale, 0.0
            )
            inverse[span(pair), :] = jnp.where(
                column <= row, jnp.where(upper, mixed[a], mixed[a + 1]) * scale, 0.0
            )


def matrix_pair(work, group):
    return pl.ds(group, work.shape[1] // 2, stride=GROUP)


def side_by_side(left, right):
    return jnp.concatenate([left, right], axis=1)


def leaf_kernel(bases_far, transfer_far, low, piece, gram, inverse_out, bases, transfer, work, factor, inverse, arrived):
    rank = bases.shape[2]
    first = pltpu.make_async_copy(bases_far, bases, arrived.at[0])
    second = pltpu.make_async_copy(transfer_far, transfer, arrived.at[1])
    first.start()
    second.start()
    first.wait()
    for g in range(GROUP):
        left, right = bases[g], bases[g + GROUP]
        work[matrix_pair(work, g), :] = side_by_side(dot_tn(left, left), dot_tn(right, right))
    eliminate(work, factor, inverse)
    second.wait()
    for g in range(GROUP):
        both = factor[matrix_pair(work, g), :]
        left = dot_nn(both[:, :rank], transfer[g])
        right = dot_nn(both[:, rank:], transfer[g + GROUP])
        piece[g] = left
        piece[g + GROUP] = right
        gram[g] = side_by_side(dot_tn(left, left), dot_tn(right, right))
        low[g] = both.astype(bf16)
        inverse_out[g] = inverse[matrix_pair(work, g), :]


def middle_kernel(spot, mine, other, top_mine, top_other, after, up, gram, inverse_out, work, factor, inverse):
    rank = top_mine.shape[2]
    for g in range(GROUP):
        work[matrix_pair(work, g), :] = mine[g] + other[g]
    eliminate(work, factor, inverse)
    for g in range(GROUP):
        both = factor[matrix_pair(work, g), :]
        both = jnp.where(spot[1] == 0, both, pltpu.roll(both, rank, axis=1))
        left = dot_nn(both[:, :rank], top_mine[g])
        right = dot_nn(both[:, rank:], top_other[g])
        up[g] = left
        gram[g] = side_by_side(dot_tn(left, left), dot_tn(right, right))
        inverse_out[g] = inverse[matrix_pair(work, g), :]


def top_kernel(mine, other, after, low, inverse_out, work, factor, inverse):
    for g in range(GROUP):
        work[matrix_pair(work, g), :] = mine[g] + other[g]
    eliminate(work, factor, inverse)
    for g in range(GROUP):
        low[g] = factor[matrix_pair(work, g), :].astype(bf16)
        inverse_out[g] = inverse[matrix_pair(work, g), :]


def half_kernel(target, couplings, low, halves, turned, table):
    rank, _, count = couplings.shape
    pitch = turned.shape[0] // rank
    for g in range(GROUP):
        both = low[g]
        table[g] = both[:, :rank]
        table[g + GROUP] = both[:, rank:]
    for m in range(rank):
        turned[m * pitch : m * pitch + count, :] = couplings[m].astype(f32).T
    for r in range(count):
        block = turned[pl.ds(r, rank, stride=pitch), :].astype(bf16)
        halves[r] = low_nn(table[target[r]], block).astype(bf16)


def leaf_output_kernel(spot, bases, inverse, piece, middle_inverse, leaf_bases, leaf_transfers):
    rank = bases.shape[2]
    share = leaf_bases.shape[0]
    for k in range(share):
        place = spot[0] * share + k
        both = inverse[place % GROUP]
        both = jnp.where(place < GROUP, both[:, :rank], both[:, rank:])
        leaf_bases[k] = dot_nt(bases[place], both)
    for g in range(GROUP):
        both = middle_inverse[g]
        leaf_transfers[g] = dot_nt(piece[g], both[:, :rank])
        leaf_transfers[g + GROUP] = dot_nt(piece[g + GROUP], both[:, rank:])


def unpack(packed, table, base):
    rank = table.shape[2]
    for g in range(GROUP):
        both = packed[g]
        table[base + g] = both[:, :rank]
        table[base + g + GROUP] = both[:, rank:]


def full_kernel(source, halves, up, inverse, *rest):
    packed, (out, top_transfers, turned, table) = rest[:-4], rest[-4:]
    count, rank, _ = halves.shape
    pitch = turned.shape[0] // rank
    for place, one in enumerate(packed):
        unpack(one, table, 2 * GROUP * place)
    for r in range(count):
        turned[pl.ds(r, rank, stride=pitch), :] = low_nt(halves[r], table[source[r]])
    for g in range(GROUP):
        top_transfers[g] = dot_nt(up[g], inverse[g][:, :rank])
    for k in range(rank):
        out[k] = turned[k * pitch : k * pitch + count, :].T.astype(bf16)


def top_project_kernel(target, source, couplings, after, *rest):
    packed, (out, table) = rest[:-2], rest[-2:]
    count, rank, _ = couplings.shape
    for place, one in enumerate(packed):
        unpack(one, table, 2 * GROUP * place)
    for r in range(count):
        part = low_nn(table[target[r]], couplings[r]).astype(bf16)
        out[r] = low_nt(part, table[source[r]]).astype(bf16)


vmem = pl.BlockSpec(memory_space=pltpu.VMEM)
smem = pl.BlockSpec(memory_space=pltpu.SMEM)
anywhere = pl.BlockSpec(memory_space=pl.ANY)


def call(kernel, outs, scalars=(), arrays=(), after=(), tables=(), scratch=(), far=()):
    return pl.pallas_call(
        kernel,
        out_shape=[jax.ShapeDtypeStruct(shape, dtype) for shape, dtype in outs],
        in_specs=[smem] * len(scalars)
        + [anywhere] * len(far)
        + [vmem] * len(arrays)
        + [anywhere] * len(after)
        + [vmem] * len(tables),
        out_specs=[vmem] * len(outs),
        scratch_shapes=list(scratch),
        compiler_params=pltpu.CompilerParams(vmem_limit_bytes=VMEM_LIMIT),
    )(*scalars, *far, *arrays, *after, *tables)


def on_device(
    bases,
    leaf_transfer,
    top_transfer,
    couplings,
    coupling_target,
    coupling_dest,
    coupling_local,
    top_couplings,
    top_target,
    top_source,
):
    leaves, _, rank = bases.shape
    share = leaves // lax.axis_size("near")
    blocks, top_blocks = couplings.shape[0], top_couplings.shape[0]
    leaf_bits = list(range(lax.axis_size("leaf").bit_length() - 1))[::-1]
    quad_bits = [bit - 2 for bit in leaf_bits if bit >= 2]
    near_place, leaf_place = lax.axis_index("near"), lax.axis_index("leaf")
    parity = leaf_place % 2
    spot = jnp.stack([near_place, parity]).astype(jnp.int32)
    square = (rank, rank)
    packed = (GROUP, rank, 2 * rank)
    work = [pltpu.VMEM((rank * GROUP, 2 * rank), f32)] * 3
    turned = pltpu.VMEM((rank * (blocks + PITCH_EXTRA), rank), f32)

    source = place_of(coupling_dest[:, 0] ^ leaf_place, leaf_bits) * leaves + coupling_local
    top_left = top_target ^ (GROUP * parity)
    top_right = place_of((top_source // leaves) ^ (leaf_place // 4), quad_bits) * leaves + (
        (top_source % leaves) ^ (GROUP * parity)
    )

    top_other = swapped(top_transfer, "leaf", 1)
    low, piece, gram, inverse = call(
        leaf_kernel,
        [(packed, bf16), ((leaves, *square), f32), (packed, f32), (packed, f32)],
        far=[bases, leaf_transfer],
        scratch=[pltpu.VMEM(bases.shape, f32), pltpu.VMEM(leaf_transfer.shape, f32), *work, pltpu.SemaphoreType.DMA((2,))],
    )
    gram_other = swapped(gram, "leaf", 1)
    (halves,) = call(
        half_kernel,
        [((blocks, *square), bf16)],
        scalars=[coupling_target],
        arrays=[jnp.transpose(couplings, (1, 2, 0)), low],
        scratch=[turned, pltpu.VMEM((leaves, *square), bf16)],
    )
    tables = gathered_by_xor(low, "leaf", leaf_bits)
    up, up_gram, middle_inverse = call(
        middle_kernel,
        [((GROUP, *square), f32), (packed, f32), (packed, f32)],
        scalars=[spot],
        arrays=[gram, gram_other, top_transfer, top_other],
        after=[halves],
        scratch=work,
    )
    up_other = swapped(up_gram, "leaf", 2)
    leaf_bases, leaf_transfers = call(
        leaf_output_kernel,
        [((share, *square), f32), ((leaves, *square), f32)],
        scalars=[spot],
        arrays=[bases, inverse, piece, middle_inverse],
    )
    top_low, top_inverse = call(
        top_kernel,
        [(packed, bf16), (packed, f32)],
        arrays=[up_gram, up_other],
        after=[leaf_transfers],
        scratch=work,
    )
    top_tables = gathered_by_xor(top_low, "leaf", [bit + 2 for bit in quad_bits])
    new_couplings, top_transfers = call(
        full_kernel,
        [((rank, rank, blocks), bf16), ((GROUP, *square), f32)],
        scalars=[source],
        arrays=[halves, up, top_inverse],
        tables=tables,
        scratch=[turned, pltpu.VMEM((len(tables) * leaves, *square), bf16)],
    )
    (new_top_couplings,) = call(
        top_project_kernel,
        [((top_blocks, *square), bf16)],
        scalars=[top_left, top_right],
        arrays=[top_couplings],
        after=[new_couplings],
        tables=top_tables,
        scratch=[pltpu.VMEM((len(top_tables) * leaves, *square), bf16)],
    )
    new_couplings = jnp.transpose(new_couplings, (2, 0, 1))
    return (leaf_bases, leaf_transfers, top_transfers, new_couplings, new_top_couplings)


def solution(mesh):
    in_specs = (
        P("leaf", None, None),
        P("leaf", None, None),
        P("leaf", None, None),
        P(("leaf", "near"), None, None),
        P(("leaf", "near")),
        P(("leaf", "near"), None),
        P(("leaf", "near")),
        P(("leaf", "near"), None, None),
        P(("leaf", "near")),
        P(("leaf", "near")),
    )
    out_specs = (
        P(("leaf", "near"), None, None),
        P("leaf", None, None),
        P("leaf", None, None),
        P(("leaf", "near"), None, None),
        P(("leaf", "near"), None, None),
    )
    return jax.shard_map(
        on_device, mesh=mesh, in_specs=in_specs, out_specs=out_specs, check_vma=False
    )
```

time: 258 us -> 45.8 us (0.18)
  other arithmetic: 152 us -> 0.1 us
  blocking collectives: 71.2 us -> 0 us
  Pallas kernels: 0 us -> 22.5 us
  matrix products: 14.3 us -> 0 us
  starting transfers between devices: 1.7 us -> 14.7 us
  local copies, waits for them, and re-layouts: 12.7 us -> 5.99 us
  waiting for transfers between devices: 4.57 us -> 1.39 us
    another operation x16 -> x1, other arithmetic: 152 us -> 0.08 us  [on_device(): spot = jnp.stack([near_place, parity]).astype(jnp.int32)]
    all_gather x3 -> x0, blocking collectives: 71.2 us -> none  [the longest x1 33.3 us: on_device(): every_factor = lax.all_gather(factor_low, 'leaf', axis=0, tiled=True)]
    pallas_call x0 -> x7, Pallas kernels: none -> 22.5 us  [call(): pl.pallas_call(kernel, out_shape=[jax.ShapeDtypeStruct(shape, dtype) for...]
    ppermute x2 -> x11, starting transfers between devices: 1.7 us -> 14.7 us  [swapped(): return lax.ppermute(value, axis, pairs)]
    dot_general x9 -> x0, matrix products: 10.6 us -> none  [the longest x1 4.67 us: on_device(): jnp.einsum('nkr,nlr->nkl', halves, source_rows, preferred_element_type=jn...]
    gather x4 -> x0, local copies, waits for them, and re-layouts: 5.47 us -> none  [the longest x1 2.17 us: on_device(): source_rows = every_factor[destination * leaves_here + coupling_local]]
    another operation x3 -> x0, matrix products: 3.71 us -> none  [single(): jax.scipy.linalg.solve_triangular(factor_one, block_one.T, lower=True)]
    ppermute x2 -> x11, waiting for transfers between devices: 4.57 us -> 1.39 us  [swapped(): return lax.ppermute(value, axis, pairs)]
  transfers between devices with their start and end apart: 2 -> 11, of which waited for: 1 -> 1; matrix products, arithmetic and copies ran while one was open for 11% -> 0% of each run, Pallas kernels for 0% -> 33%
where the time goes in v2:
time: 45.8 us; the launch traced here: 45.5 us
  Pallas kernels  22.5 us (49%)
  starting transfers between devices  14.7 us (32%)
  local copies, waits for them, and re-layouts  5.99 us (13%)
  waiting for transfers between devices  1.39 us (3%)
  between operations  0.75 us (2%)
    pallas_call x7, Pallas kernels, call(): pl.pallas_call(kernel, out_shape=[jax.ShapeDtypeStruct(shape, dtype) for...  22.5 us
    ppermute x11, starting transfers between devices, swapped(): return lax.ppermute(value, axis, pairs)  14.7 us
    unnamed x26, local copies, waits for them, and re-layouts  5.99 us
    ppermute x11, waiting for transfers between devices, swapped(): return lax.ppermute(value, axis, pairs)  1.39 us
  transfers between devices with their start and end apart: 11, of which 1 were waited for; matrix products, arithmetic and copies ran while one was open for 0% of the time, Pallas kernels for 33%

profile of v2, /device:TPU:0, one launch (start us, length us, event | category | flops | bytes accessed | tf_op | source)
XLA Modules:
  0.0 45.5 jit_solution(1896905995245910933)
XLA Ops:
  0.6 0.0 copy-start.2
  0.6 0.9 %copy-done.2 = f32[8,64,64]{2,1,0:T(8,128)S(1)} copy-done((f32[8,64,64]{2,1,0:T(8,128)S(1)}, f32[8,64,64]{2,1,0:T(8,128)}, u32[]{:S(2)}) %copy-start.2) | copy-done | bytes 131096
  1.6 0.9 %copy-done.4 = f32[8,64,64]{2,1,0:T(8,128)S(1)} copy-done((f32[8,64,64]{2,1,0:T(8,128)S(1)}, f32[8,64,64]{2,1,0:T(8,128)}, u32[]{:S(2)}) %copy-start.4) | copy-done | bytes 131096
  2.5 5.0 %shard_map.137 = (bf16[4,64,128]{2,1,0:T(8,128)(2,1)S(1)}, f32[8,64,64]{2,1,0:T(8,128)S(1)}, f32[4,64,128]{2,1,0:T(8,128)S(1)}, f32[4,64,128]{2,1,0:T(8,128)S(1)}) custom-call(f32[8,64,64]{2,1,0:T(8,128)S(1)} %copy-done.2, f32[8,64,64]{2,1,0:T(8,128)S(1)} %copy-done.4), custom_call_target="tpu_custom_call" | custom-call | tf_op jit(solution)/shard_map/pallas_call | solution.py:232
  7.5 3.0 %collective-permute-start = (f32[4,64,128]{2,1,0:T(8,128)S(1)}, f32[4,64,128]{2,1,0:T(8,128)S(1)}, u32[]{:S(2)}, u32[]{:S(2)}) collective-permute-start(f32[4,64,128]{2,1,0:T(8,128)S(1)} %get-tuple-element.20.mine), channel_id=1, source_target_pairs={{0,4},{4,0},{8,12},{12,8},{16,20},{20,16},{24,28},{28,24},{1,5},{5... | collective-permute-start | bytes 393224 | tf_op jit(solution)/shard_map/ppermute | solution.py:21
  10.6 0.1 collective-permute-start.6
  10.7 2.0 %collective-permute-start.4 = (bf16[4,64,128]{2,1,0:T(8,128)(2,1)S(1)}, bf16[4,64,128]{2,1,0:T(8,128)(2,1)S(1)}, u32[]{:S(2)}, u32[]{:S(2)}) collective-permute-start(bf16[4,64,128]{2,1,0:T(8,128)(2,1)S(1)} %get-tuple-element.21.low.rest_0_), channel_id=1, source_target_pairs={{0,8},{4,12},{8,0},{12,4},{16,24},{20,28},{24,16},{28,20},{1,9},{5... | collective-permute-start | bytes 196616 | tf_op jit(solution)/shard_map/ppermute | solution.py:21
  12.7 2.6 %collective-permute-start.3 = (bf16[4,64,128]{2,1,0:T(8,128)(2,1)S(1)}, bf16[4,64,128]{2,1,0:T(8,128)(2,1)S(1)}, u32[]{:S(2)}, u32[]{:S(2)}) collective-permute-start(bf16[4,64,128]{2,1,0:T(8,128)(2,1)S(1)} %get-tuple-element.21.low.rest_0_), channel_id=1, source_target_pairs={{0,16},{4,20},{8,24},{12,28},{16,0},{20,4},{24,8},{28,12},{1,17},{... | collective-permute-start | bytes 196616 | tf_op jit(solution)/shard_map/ppermute | solution.py:21
  15.2 1.5 %collective-permute-start.1 = (f32[4,64,64]{2,1,0:T(8,128)}, f32[4,64,64]{2,1,0:T(8,128)S(1)}, u32[]{:S(2)}, u32[]{:S(2)}) collective-permute-start(f32[4,64,64]{2,1,0:T(8,128)} %top_mine.1), channel_id=1, source_target_pairs={{0,4},{4,0},{8,12},{12,8},{16,20},{20,16},{24,28},{28,24},{1,5},{5... | collective-permute-start | bytes 196616 | tf_op jit(solution)/shard_map/ppermute | solution.py:21
  16.8 1.2 %copy-done = bf16[128,64,64]{0,2,1:T(8,128)(2,1)S(1)} copy-done((bf16[128,64,64]{0,2,1:T(8,128)(2,1)S(1)}, bf16[128,64,64]{0,2,1:T(8,128)(2,1)}, u32[]{:S(2)}) %copy-start) | copy-done | bytes 1048600
  18.0 0.7 %copy-done.8 = s32[128]{0:T(128)S(1)} copy-done((s32[128]{0:T(128)S(1)}, s32[128]{0:T(128)}, u32[]{:S(2)}) %copy-start.8) | copy-done | bytes 536
  18.6 2.1 %shard_map.138.after.halves = bf16[128,64,64]{2,1,0:T(8,128)(2,1)S(1)} custom-call(s32[128]{0:T(128)S(1)} %copy-done.8, bf16[64,64,128]{2,1,0:T(8,128)(2,1)S(1)} %bitcast.6, bf16[4,64,128]{2,1,0:T(8,128)(2,1)S(1)} %get-tuple-element.21.low.rest_0_), custom_call_target="tpu_custom_call" | custom-call | tf_op jit(solution)/shard_map/pallas_call | solution.py:232
  20.8 0.0 copy-start.9
  20.8 0.0 copy-start.10
  20.8 0.0 copy-start.3
  20.8 0.0 copy-start.11
  20.8 0.0 copy-start.12
  20.8 0.1 pad_add_fusion.spot
  20.9 0.5 %collective-permute-start.5 = (bf16[4,64,128]{2,1,0:T(8,128)(2,1)S(1)}, bf16[4,64,128]{2,1,0:T(8,128)(2,1)S(1)}, u32[]{:S(2)}, u32[]{:S(2)}) collective-permute-start(bf16[4,64,128]{2,1,0:T(8,128)(2,1)S(1)} %collective-permute-done.3.rest_1_), channel_id=1, source_target_pairs={{0,8},{4,12},{8,0},{12,4},{16,24},{20,28},{24,16},{28,20},{1,9},{5... | collective-permute-start | bytes 196616 | tf_op jit(solution)/shard_map/ppermute | solution.py:21
  21.4 4.5 %shard_map.139 = (f32[4,64,64]{2,1,0:T(8,128)S(1)}, f32[4,64,128]{2,1,0:T(8,128)S(1)}, f32[4,64,128]{2,1,0:T(8,128)S(1)}) custom-call(s32[2]{0:T(128)S(1)} %pad_add_fusion.spot, f32[4,64,128]{2,1,0:T(8,128)S(1)} %get-tuple-element.20.mine, f32[4,64,128]{2,1,0:T(8,128)S(1)} %collective-permute-done.other, f32[4,64,64]{2,1,0:T(8,128)S(1)} %copy-done.7, ...), custom_call_target="tpu_custom_call" | custom-call | tf_op jit(solution)/shard_map/pallas_call | solution.py:232
  25.9 1.7 %collective-permute-start.2 = (f32[4,64,128]{2,1,0:T(8,128)S(1)}, f32[4,64,128]{2,1,0:T(8,128)S(1)}, u32[]{:S(2)}, u32[]{:S(2)}) collective-permute-start(f32[4,64,128]{2,1,0:T(8,128)S(1)} %get-tuple-element.26.mine), channel_id=1, source_target_pairs={{0,8},{4,12},{8,0},{12,4},{16,24},{20,28},{24,16},{28,20},{1,9},{5... | collective-permute-start | bytes 393224 | tf_op jit(solution)/shard_map/ppermute | solution.py:21
  27.6 0.6 %collective-permute-start.7 = (bf16[4,64,128]{2,1,0:T(8,128)(2,1)S(1)}, bf16[4,64,128]{2,1,0:T(8,128)(2,1)S(1)}, u32[]{:S(2)}, u32[]{:S(2)}) collective-permute-start(bf16[4,64,128]{2,1,0:T(8,128)(2,1)S(1)} %collective-permute-done.3.rest_1_), channel_id=1, source_target_pairs={{0,4},{4,0},{8,12},{12,8},{16,20},{20,16},{24,28},{28,24},{1,5},{5... | collective-permute-start | bytes 196616 | tf_op jit(solution)/shard_map/ppermute | solution.py:21
  28.2 1.5 %collective-permute-start.8 = (bf16[4,64,128]{2,1,0:T(8,128)(2,1)S(1)}, bf16[4,64,128]{2,1,0:T(8,128)(2,1)S(1)}, u32[]{:S(2)}, u32[]{:S(2)}) collective-permute-start(bf16[4,64,128]{2,1,0:T(8,128)(2,1)S(1)} %collective-permute-done.4.rest_2_), channel_id=1, source_target_pairs={{0,4},{4,0},{8,12},{12,8},{16,20},{20,16},{24,28},{28,24},{1,5},{5... | collective-permute-start | bytes 196616 | tf_op jit(solution)/shard_map/ppermute | solution.py:21
  29.7 2.0 %shard_map.140 = (f32[2,64,64]{2,1,0:T(8,128)}, f32[8,64,64]{2,1,0:T(8,128)}) custom-call(s32[2]{0:T(128)S(1)} %pad_add_fusion.spot, f32[8,64,64]{2,1,0:T(8,128)S(1)} %copy-done.3, f32[4,64,128]{2,1,0:T(8,128)S(1)} %get-tuple-element.18.inverse, f32[8,64,64]{2,1,0:T(8,128)S(1)} %get-tuple-element.19.piece, f32[4,64,128]{2,1,0:T(8,128)S(1)} %get-tuple-element.22.middle_inverse), custom_call_target="tpu_custom_call" | custom-call | tf_op jit(solution)/shard_map/pallas_call | solution.py:232
  31.7 0.5 %collective-permute-start.9 = (bf16[4,64,128]{2,1,0:T(8,128)(2,1)S(1)}, bf16[4,64,128]{2,1,0:T(8,128)(2,1)S(1)}, u32[]{:S(2)}, u32[]{:S(2)}) collective-permute-start(bf16[4,64,128]{2,1,0:T(8,128)(2,1)S(1)} %collective-permute-done.5.rest_3_), channel_id=1, source_target_pairs={{0,4},{4,0},{8,12},{12,8},{16,20},{20,16},{24,28},{28,24},{1,5},{5... | collective-permute-start | bytes 196616 | tf_op jit(solution)/shard_map/ppermute | solution.py:21
  32.2 0.9 %copy-done.5 = f32[8,64,64]{2,1,0:T(8,128)S(1)} copy-done((f32[8,64,64]{2,1,0:T(8,128)S(1)}, f32[8,64,64]{2,1,0:T(8,128)}, u32[]{:S(2)}) %copy-start.5) | copy-done | bytes 131096
  33.1 2.7 %shard_map.141 = (bf16[4,64,128]{2,1,0:T(8,128)(2,1)S(1)}, f32[4,64,128]{2,1,0:T(8,128)S(1)}) custom-call(f32[4,64,128]{2,1,0:T(8,128)S(1)} %get-tuple-element.26.mine, f32[4,64,128]{2,1,0:T(8,128)S(1)} %collective-permute-done.2.other, f32[8,64,64]{2,1,0:T(8,128)S(1)} %copy-done.5), custom_call_target="tpu_custom_call" | custom-call | tf_op jit(solution)/shard_map/pallas_call | solution.py:232
  35.8 0.8 %collective-permute-start.10 = (bf16[4,64,128]{2,1,0:T(8,128)(2,1)S(1)}, bf16[4,64,128]{2,1,0:T(8,128)(2,1)S(1)}, u32[]{:S(2)}, u32[]{:S(2)}) collective-permute-start(bf16[4,64,128]{2,1,0:T(8,128)(2,1)S(1)} %get-tuple-element.30.rest_0_), channel_id=1, source_target_pairs={{0,16},{4,20},{8,24},{12,28},{16,0},{20,4},{24,8},{28,12},{1,17},{... | collective-permute-start | bytes 196616 | tf_op jit(solution)/shard_map/ppermute | solution.py:21
  36.7 3.7 %shard_map.142 = (bf16[64,64,128]{2,1,0:T(8,128)(2,1)}, f32[4,64,64]{2,1,0:T(8,128)}) custom-call(s32[128]{0:T(128)S(1)} %bitcast_add_fusion.source, bf16[128,64,64]{2,1,0:T(8,128)(2,1)S(1)} %shard_map.138.after.halves, f32[4,64,64]{2,1,0:T(8,128)S(1)} %get-tuple-element.25.up, f32[4,64,128]{2,1,0:T(8,128)S(1)} %get-tuple-element.27.inverse, ...), custom_call_target="tpu_custom_call" | custom-call | tf_op jit(solution)/shard_map/pallas_call | solution.py:232
  40.3 1.4 %collective-permute-done.10.rest_1_ = bf16[4,64,128]{2,1,0:T(8,128)(2,1)S(1)} collective-permute-done((bf16[4,64,128]{2,1,0:T(8,128)(2,1)S(1)}, bf16[4,64,128]{2,1,0:T(8,128)(2,1)S(1)}, u32[]{:S(2)}, u32[]{:S(2)}) %collective-permute-start.10) | collective-permute-done | bytes 65568 | tf_op jit(solution)/shard_map/ppermute | solution.py:21
  41.7 1.2 %copy-done.1 = bf16[64,64,128]{2,1,0:T(8,128)(2,1)S(1)} copy-done((bf16[64,64,128]{2,1,0:T(8,128)(2,1)S(1)}, bf16[64,64,128]{2,1,0:T(8,128)(2,1)}, u32[]{:S(2)}) %copy-start.1) | copy-done | bytes 1048600
  42.9 2.5 %shard_map.143 = bf16[16,64,64]{2,1,0:T(8,128)(2,1)} custom-call(s32[16]{0:T(128)S(1)} %get-tuple-element.32.target, s32[16]{0:T(128)S(1)} %get-tuple-element.31.source, bf16[16,64,64]{2,1,0:T(8,128)(2,1)S(1)} %copy-done.6, bf16[64,64,128]{2,1,0:T(8,128)(2,1)S(1)} %copy-done.1, bf16[4,64,128]{2,1,0:T(8,128)(2,1)S(1)} %get-tuple-element.30.rest_0_, ...), custom_call_target="tpu_custom_call" | custom-call | tf_op jit(solution)/shard_map/pallas_call | solution.py:232
  (26 shorter events, 0.1 us)
Async XLA Ops:
  0.6 1.0 %copy-start.2 = (f32[8,64,64]{2,1,0:T(8,128)S(1)}, f32[8,64,64]{2,1,0:T(8,128)}, u32[]{:S(2)}) copy-start(f32[8,64,64]{2,1,0:T(8,128)} %bases.1) | copy-start | bytes 393220
  1.6 0.9 %copy-start.4 = (f32[8,64,64]{2,1,0:T(8,128)S(1)}, f32[8,64,64]{2,1,0:T(8,128)}, u32[]{:S(2)}) copy-start(f32[8,64,64]{2,1,0:T(8,128)} %transfer_far.1) | copy-start | bytes 393220
  2.5 18.8 %copy-start.7 = (f32[4,64,64]{2,1,0:T(8,128)S(1)}, f32[4,64,64]{2,1,0:T(8,128)}, u32[]{:S(2)}) copy-start(f32[4,64,64]{2,1,0:T(8,128)} %top_mine.1) | copy-start | bytes 196612
  7.5 13.8 %collective-permute-start = (f32[4,64,128]{2,1,0:T(8,128)S(1)}, f32[4,64,128]{2,1,0:T(8,128)S(1)}, u32[]{:S(2)}, u32[]{:S(2)}) collective-permute-start(f32[4,64,128]{2,1,0:T(8,128)S(1)} %get-tuple-element.20.mine), channel_id=1, source_target_pairs={{0,4},{4,0},{8,12},{12,8},{16,20},{20,16},{24,28},{28,24},{1,5},{5... | collective-permute-start | bytes 393224 | tf_op jit(solution)/shard_map/ppermute | solution.py:21
  10.6 26.1 %collective-permute-start.6 = (bf16[4,64,128]{2,1,0:T(8,128)(2,1)S(1)}, bf16[4,64,128]{2,1,0:T(8,128)(2,1)S(1)}, u32[]{:S(2)}, u32[]{:S(2)}) collective-permute-start(bf16[4,64,128]{2,1,0:T(8,128)(2,1)S(1)} %get-tuple-element.21.low.rest_0_), channel_id=1, source_target_pairs={{0,4},{4,0},{8,12},{12,8},{16,20},{20,16},{24,28},{28,24},{1,5},{5... | collective-permute-start | bytes 196616 | tf_op jit(solution)/shard_map/ppermute | solution.py:21
  10.7 17.5 %collective-permute-start.4 = (bf16[4,64,128]{2,1,0:T(8,128)(2,1)S(1)}, bf16[4,64,128]{2,1,0:T(8,128)(2,1)S(1)}, u32[]{:S(2)}, u32[]{:S(2)}) collective-permute-start(bf16[4,64,128]{2,1,0:T(8,128)(2,1)S(1)} %get-tuple-element.21.low.rest_0_), channel_id=1, source_target_pairs={{0,8},{4,12},{8,0},{12,4},{16,24},{20,28},{24,16},{28,20},{1,9},{5... | collective-permute-start | bytes 196616 | tf_op jit(solution)/shard_map/ppermute | solution.py:21
  12.7 8.2 %collective-permute-start.3 = (bf16[4,64,128]{2,1,0:T(8,128)(2,1)S(1)}, bf16[4,64,128]{2,1,0:T(8,128)(2,1)S(1)}, u32[]{:S(2)}, u32[]{:S(2)}) collective-permute-start(bf16[4,64,128]{2,1,0:T(8,128)(2,1)S(1)} %get-tuple-element.21.low.rest_0_), channel_id=1, source_target_pairs={{0,16},{4,20},{8,24},{12,28},{16,0},{20,4},{24,8},{28,12},{1,17},{... | collective-permute-start | bytes 196616 | tf_op jit(solution)/shard_map/ppermute | solution.py:21
  15.2 6.1 %collective-permute-start.1 = (f32[4,64,64]{2,1,0:T(8,128)}, f32[4,64,64]{2,1,0:T(8,128)S(1)}, u32[]{:S(2)}, u32[]{:S(2)}) collective-permute-start(f32[4,64,64]{2,1,0:T(8,128)} %top_mine.1), channel_id=1, source_target_pairs={{0,4},{4,0},{8,12},{12,8},{16,20},{20,16},{24,28},{28,24},{1,5},{5... | collective-permute-start | bytes 196616 | tf_op jit(solution)/shard_map/ppermute | solution.py:21
  16.8 1.2 %copy-start = (bf16[128,64,64]{0,2,1:T(8,128)(2,1)S(1)}, bf16[128,64,64]{0,2,1:T(8,128)(2,1)}, u32[]{:S(2)}) copy-start(bf16[128,64,64]{0,2,1:T(8,128)(2,1)} %param.13) | copy-start | bytes 3145732
  18.0 0.7 %copy-start.8 = (s32[128]{0:T(128)S(1)}, s32[128]{0:T(128)}, u32[]{:S(2)}) copy-start(s32[128]{0:T(128)} %target.1) | copy-start | bytes 1540
  20.8 6.8 %copy-start.9 = (s32[16]{0:T(128)S(1)}, s32[16]{0:T(128)}, u32[]{:S(2)}) copy-start(s32[16]{0:T(128)} %param.19) | copy-start | bytes 196
  20.8 6.8 %copy-start.10 = (s32[16]{0:T(128)S(1)}, s32[16]{0:T(128)}, u32[]{:S(2)}) copy-start(s32[16]{0:T(128)} %param.18) | copy-start | bytes 196
  20.8 8.9 %copy-start.3 = (f32[8,64,64]{2,1,0:T(8,128)S(1)}, f32[8,64,64]{2,1,0:T(8,128)}, u32[]{:S(2)}) copy-start(f32[8,64,64]{2,1,0:T(8,128)} %bases.1) | copy-start | bytes 393220
  20.8 15.8 %copy-start.11 = (s32[128]{0:T(128)S(1)}, s32[128]{0:T(128)}, u32[]{:S(2)}) copy-start(s32[128]{0:T(128)} %param.16) | copy-start | bytes 1540
  20.8 15.8 %copy-start.12 = (s32[128,1]{0,1:T(1,128)S(1)}, s32[128,1]{0,1:T(1,128)}, u32[]{:S(2)}) copy-start(s32[128,1]{0,1:T(1,128)} %param.15) | copy-start | bytes 1540
  20.9 10.8 %collective-permute-start.5 = (bf16[4,64,128]{2,1,0:T(8,128)(2,1)S(1)}, bf16[4,64,128]{2,1,0:T(8,128)(2,1)S(1)}, u32[]{:S(2)}, u32[]{:S(2)}) collective-permute-start(bf16[4,64,128]{2,1,0:T(8,128)(2,1)S(1)} %collective-permute-done.3.rest_1_), channel_id=1, source_target_pairs={{0,8},{4,12},{8,0},{12,4},{16,24},{20,28},{24,16},{28,20},{1,9},{5... | collective-permute-start | bytes 196616 | tf_op jit(solution)/shard_map/ppermute | solution.py:21
  25.9 6.3 %collective-permute-start.2 = (f32[4,64,128]{2,1,0:T(8,128)S(1)}, f32[4,64,128]{2,1,0:T(8,128)S(1)}, u32[]{:S(2)}, u32[]{:S(2)}) collective-permute-start(f32[4,64,128]{2,1,0:T(8,128)S(1)} %get-tuple-element.26.mine), channel_id=1, source_target_pairs={{0,8},{4,12},{8,0},{12,4},{16,24},{20,28},{24,16},{28,20},{1,9},{5... | collective-permute-start | bytes 393224 | tf_op jit(solution)/shard_map/ppermute | solution.py:21
  27.6 9.1 %collective-permute-start.7 = (bf16[4,64,128]{2,1,0:T(8,128)(2,1)S(1)}, bf16[4,64,128]{2,1,0:T(8,128)(2,1)S(1)}, u32[]{:S(2)}, u32[]{:S(2)}) collective-permute-start(bf16[4,64,128]{2,1,0:T(8,128)(2,1)S(1)} %collective-permute-done.3.rest_1_), channel_id=1, source_target_pairs={{0,4},{4,0},{8,12},{12,8},{16,20},{20,16},{24,28},{28,24},{1,5},{5... | collective-permute-start | bytes 196616 | tf_op jit(solution)/shard_map/ppermute | solution.py:21
  28.2 8.5 %collective-permute-start.8 = (bf16[4,64,128]{2,1,0:T(8,128)(2,1)S(1)}, bf16[4,64,128]{2,1,0:T(8,128)(2,1)S(1)}, u32[]{:S(2)}, u32[]{:S(2)}) collective-permute-start(bf16[4,64,128]{2,1,0:T(8,128)(2,1)S(1)} %collective-permute-done.4.rest_2_), channel_id=1, source_target_pairs={{0,4},{4,0},{8,12},{12,8},{16,20},{20,16},{24,28},{28,24},{1,5},{5... | collective-permute-start | bytes 196616 | tf_op jit(solution)/shard_map/ppermute | solution.py:21
  29.7 12.0 %copy-start.6 = (bf16[16,64,64]{2,1,0:T(8,128)(2,1)S(1)}, bf16[16,64,64]{2,1,0:T(8,128)(2,1)}, u32[]{:S(2)}) copy-start(bf16[16,64,64]{2,1,0:T(8,128)(2,1)} %couplings.1) | copy-start | bytes 393220
  31.7 5.0 %collective-permute-start.9 = (bf16[4,64,128]{2,1,0:T(8,128)(2,1)S(1)}, bf16[4,64,128]{2,1,0:T(8,128)(2,1)S(1)}, u32[]{:S(2)}, u32[]{:S(2)}) collective-permute-start(bf16[4,64,128]{2,1,0:T(8,128)(2,1)S(1)} %collective-permute-done.5.rest_3_), channel_id=1, source_target_pairs={{0,4},{4,0},{8,12},{12,8},{16,20},{20,16},{24,28},{28,24},{1,5},{5... | collective-permute-start | bytes 196616 | tf_op jit(solution)/shard_map/ppermute | solution.py:21
  32.2 1.0 %copy-start.5 = (f32[8,64,64]{2,1,0:T(8,128)S(1)}, f32[8,64,64]{2,1,0:T(8,128)}, u32[]{:S(2)}) copy-start(f32[8,64,64]{2,1,0:T(8,128)} %get-tuple-element.14.after) | copy-start | bytes 393220
  35.8 5.9 %collective-permute-start.10 = (bf16[4,64,128]{2,1,0:T(8,128)(2,1)S(1)}, bf16[4,64,128]{2,1,0:T(8,128)(2,1)S(1)}, u32[]{:S(2)}, u32[]{:S(2)}) collective-permute-start(bf16[4,64,128]{2,1,0:T(8,128)(2,1)S(1)} %get-tuple-element.30.rest_0_), channel_id=1, source_target_pairs={{0,16},{4,20},{8,24},{12,28},{16,0},{20,4},{24,8},{28,12},{1,17},{... | collective-permute-start | bytes 196616 | tf_op jit(solution)/shard_map/ppermute | solution.py:21
  41.7 1.2 %copy-start.1 = (bf16[64,64,128]{2,1,0:T(8,128)(2,1)S(1)}, bf16[64,64,128]{2,1,0:T(8,128)(2,1)}, u32[]{:S(2)}) copy-start(bf16[64,64,128]{2,1,0:T(8,128)(2,1)} %get-tuple-element.29.after) | copy-start | bytes 3145732

commit v3 on v2

--- a/solution.py
+++ b/solution.py
@@ -13,7 +13,9 @@
 BLOCK = 8
 GROUP = 4
 PITCH_EXTRA = 8
+CHUNKS = 4
 VMEM_LIMIT = 48 * 2**20
+FLOPS = 1e9
 
 
 def swapped(value, axis, mask):
@@ -22,10 +24,22 @@
 
 
 def gathered_by_xor(value, axis, bits):
-    values = [value]
-    for bit in bits:
-        values = values + [swapped(one, axis, 1 << bit) for one in values]
-    return values
+    for step, bit in enumerate(bits):
+        other = swapped(value, axis, 1 << bit)
+        if step == len(bits) - 1:
+            return [value, other]
+        value = joined(value, other)
+    return [value]
+
+
+def join_kernel(first, second, out):
+    out[: first.shape[0]] = first[...]
+    out[first.shape[0] :] = second[...]
+
+
+def joined(first, second):
+    shape = (first.shape[0] + second.shape[0], *first.shape[1:])
+    return call(join_kernel, [(shape, first.dtype)], 0.5, arrays=[first, second])[0]
 
 
 def place_of(difference, bits):
@@ -139,7 +153,7 @@
         inverse_out[g] = inverse[matrix_pair(work, g), :]
 
 
-def middle_kernel(spot, mine, other, top_mine, top_other, after, up, gram, inverse_out, work, factor, inverse):
+def middle_kernel(spot, mine, other, top_mine, top_other, token, up, gram, inverse_out, work, factor, inverse):
     rank = top_mine.shape[2]
     for g in range(GROUP):
         work[matrix_pair(work, g), :] = mine[g] + other[g]
@@ -154,7 +168,7 @@
         inverse_out[g] = inverse[matrix_pair(work, g), :]
 
 
-def top_kernel(mine, other, after, low, inverse_out, work, factor, inverse):
+def top_kernel(mine, other, token, low, inverse_out, work, factor, inverse):
     for g in range(GROUP):
         work[matrix_pair(work, g), :] = mine[g] + other[g]
     eliminate(work, factor, inverse)
@@ -163,84 +177,126 @@
         inverse_out[g] = inverse[matrix_pair(work, g), :]
 
 
-def half_kernel(target, couplings, low, halves, turned, table):
+def half_kernel(target, couplings_far, low, halves, token, couplings, turned, table, arrived):
     rank, _, count = couplings.shape
     pitch = turned.shape[0] // rank
+    token[...] = jnp.zeros_like(token)
+    chunk = rank // CHUNKS
+    copies = []
+    for k in range(CHUNKS):
+        part = pl.ds(k * chunk, chunk)
+        copies.append(pltpu.make_async_copy(couplings_far.at[part], couplings.at[part], arrived.at[k]))
+        copies[k].start()
     for g in range(GROUP):
         both = low[g]
         table[g] = both[:, :rank]
         table[g + GROUP] = both[:, rank:]
-    for m in range(rank):
-        turned[m * pitch : m * pitch + count, :] = couplings[m].astype(f32).T
+    for k in range(CHUNKS):
+        copies[k].wait()
+        for m in range(k * chunk, (k + 1) * chunk):
+            turned[m * pitch : m * pitch + count, :] = couplings[m].astype(f32).T
     for r in range(count):
         block = turned[pl.ds(r, rank, stride=pitch), :].astype(bf16)
         halves[r] = low_nn(table[target[r]], block).astype(bf16)
 
 
-def leaf_output_kernel(spot, bases, inverse, piece, middle_inverse, leaf_bases, leaf_transfers):
-    rank = bases.shape[2]
-    share = leaf_bases.shape[0]
+def leaf_output_kernel(spot, bases_far, inverse, piece, middle_inverse, leaf_bases, leaf_transfers, token, bases, arrived):
+    share, _, rank = bases.shape
+    token[...] = jnp.zeros_like(token)
+    copy = pltpu.make_async_copy(bases_far.at[pl.ds(spot[0] * share, share)], bases, arrived)
+    copy.start()
+    for g in range(GROUP):
+        both = middle_inverse[g]
+        leaf_transfers[g] = dot_nt(piece[g], both[:, :rank])
+        leaf_transfers[g + GROUP] = dot_nt(piece[g + GROUP], both[:, rank:])
+    copy.wait()
     for k in range(share):
         place = spot[0] * share + k
         both = inverse[place % GROUP]
         both = jnp.where(place < GROUP, both[:, :rank], both[:, rank:])
-        leaf_bases[k] = dot_nt(bases[place], both)
-    for g in range(GROUP):
-        both = middle_inverse[g]
-        leaf_transfers[g] = dot_nt(piece[g], both[:, :rank])
-        leaf_transfers[g + GROUP] = dot_nt(piece[g + GROUP], both[:, rank:])
+        leaf_bases[k] = dot_nt(bases[k], both)
 
 
 def unpack(packed, table, base):
-    rank = table.shape[2]
-    for g in range(GROUP):
-        both = packed[g]
-        table[base + g] = both[:, :rank]
-        table[base + g + GROUP] = both[:, rank:]
-
-
-def full_kernel(source, halves, up, inverse, *rest):
-    packed, (out, top_transfers, turned, table) = rest[:-4], rest[-4:]
+    count, rank = packed.shape[0], table.shape[2]
+
+    def step(n, carry):
+        both = packed[n]
+        place = base + 2 * GROUP * (n // GROUP) + n % GROUP
+        table[place] = both[:, :rank]
+        table[place + GROUP] = both[:, rank:]
+        return carry
+
+    lax.fori_loop(0, count, step, 0, unroll=min(count, 16))
+
+
+def full_kernel(
+    source,
+    target,
+    top_far,
+    halves,
+    up,
+    inverse,
+    top_low,
+    *rest,
+):
+    packed, rest = rest[:-11], rest[-11:]
+    out_far, top_transfers, top_halves, token = rest[:4]
+    out, turned, table, top_couplings, top_table, arrived, left = rest[4:]
     count, rank, _ = halves.shape
     pitch = turned.shape[0] // rank
-    for place, one in enumerate(packed):
-        unpack(one, table, 2 * GROUP * place)
+    token[...] = jnp.zeros_like(token)
+    copy = pltpu.make_async_copy(top_far, top_couplings, arrived)
+    copy.start()
+    base = 0
+    for one in packed:
+        unpack(one, table, base)
+        base += 2 * one.shape[0]
     for r in range(count):
         turned[pl.ds(r, rank, stride=pitch), :] = low_nt(halves[r], table[source[r]])
+    chunk = rank // CHUNKS
+    copies = []
+    for k in range(CHUNKS):
+        for m in range(k * chunk, (k + 1) * chunk):
+            out[m] = turned[m * pitch : m * pitch + count, :].T.astype(bf16)
+        part = pl.ds(k * chunk, chunk)
+        copies.append(pltpu.make_async_copy(out.at[part], out_far.at[part], left.at[k]))
+        copies[k].start()
+    unpack(top_low, top_table, 0)
     for g in range(GROUP):
         top_transfers[g] = dot_nt(up[g], inverse[g][:, :rank])
-    for k in range(rank):
-        out[k] = turned[k * pitch : k * pitch + count, :].T.astype(bf16)
-
-
-def top_project_kernel(target, source, couplings, after, *rest):
+    copy.wait()
+    for r in range(top_couplings.shape[0]):
+        top_halves[r] = low_nn(top_table[target[r]], top_couplings[r]).astype(bf16)
+    for copy in copies:
+        copy.wait()
+
+
+def top_project_kernel(source, halves, token, *rest):
     packed, (out, table) = rest[:-2], rest[-2:]
-    count, rank, _ = couplings.shape
-    for place, one in enumerate(packed):
-        unpack(one, table, 2 * GROUP * place)
-    for r in range(count):
-        part = low_nn(table[target[r]], couplings[r]).astype(bf16)
-        out[r] = low_nt(part, table[source[r]]).astype(bf16)
+    base = 0
+    for one in packed:
+        unpack(one, table, base)
+        base += 2 * one.shape[0]
+    for r in range(halves.shape[0]):
+        out[r] = low_nt(halves[r], table[source[r]]).astype(bf16)
 
 
 vmem = pl.BlockSpec(memory_space=pltpu.VMEM)
 smem = pl.BlockSpec(memory_space=pltpu.SMEM)
-anywhere = pl.BlockSpec(memory_space=pl.ANY)
-
-
-def call(kernel, outs, scalars=(), arrays=(), after=(), tables=(), scratch=(), far=()):
+hbm = pl.BlockSpec(memory_space=pltpu.HBM)
+
+
+def call(kernel, outs, microseconds, scalars=(), far=(), arrays=(), scratch=(), far_outs=0):
     return pl.pallas_call(
         kernel,
         out_shape=[jax.ShapeDtypeStruct(shape, dtype) for shape, dtype in outs],
-        in_specs=[smem] * len(scalars)
-        + [anywhere] * len(far)
-        + [vmem] * len(arrays)
-        + [anywhere] * len(after)
-        + [vmem] * len(tables),
-        out_specs=[vmem] * len(outs),
+        in_specs=[smem] * len(scalars) + [hbm] * len(far) + [vmem] * len(arrays),
+        out_specs=[hbm] * far_outs + [vmem] * (len(outs) - far_outs),
         scratch_shapes=list(scratch),
         compiler_params=pltpu.CompilerParams(vmem_limit_bytes=VMEM_LIMIT),
-    )(*scalars, *far, *arrays, *after, *tables)
+        cost_estimate=pl.CostEstimate(flops=int(microseconds * FLOPS), bytes_accessed=0, transcendentals=0),
+    )(*scalars, *far, *arrays)
 
 
 def on_device(
@@ -274,61 +330,79 @@
         (top_source % leaves) ^ (GROUP * parity)
     )
 
+    note = ((8, 2 * rank), f32)
+    dma = pltpu.SemaphoreType.DMA
+
     top_other = swapped(top_transfer, "leaf", 1)
     low, piece, gram, inverse = call(
         leaf_kernel,
         [(packed, bf16), ((leaves, *square), f32), (packed, f32), (packed, f32)],
+        4.5,
         far=[bases, leaf_transfer],
-        scratch=[pltpu.VMEM(bases.shape, f32), pltpu.VMEM(leaf_transfer.shape, f32), *work, pltpu.SemaphoreType.DMA((2,))],
+        scratch=[pltpu.VMEM(bases.shape, f32), pltpu.VMEM(leaf_transfer.shape, f32), *work, dma((2,))],
     )
     gram_other = swapped(gram, "leaf", 1)
-    (halves,) = call(
+    halves, token = call(
         half_kernel,
-        [((blocks, *square), bf16)],
+        [((blocks, *square), bf16), note],
+        2,
         scalars=[coupling_target],
-        arrays=[jnp.transpose(couplings, (1, 2, 0)), low],
-        scratch=[turned, pltpu.VMEM((leaves, *square), bf16)],
+        far=[jnp.transpose(couplings, (1, 2, 0))],
+        arrays=[low],
+        scratch=[pltpu.VMEM((rank, rank, blocks), bf16), turned, pltpu.VMEM((leaves, *square), bf16), dma((CHUNKS,))],
     )
     tables = gathered_by_xor(low, "leaf", leaf_bits)
     up, up_gram, middle_inverse = call(
         middle_kernel,
         [((GROUP, *square), f32), (packed, f32), (packed, f32)],
+        4.5,
         scalars=[spot],
-        arrays=[gram, gram_other, top_transfer, top_other],
-        after=[halves],
+        arrays=[gram, gram_other, top_transfer, top_other, token],
         scratch=work,
     )
     up_other = swapped(up_gram, "leaf", 2)
-    leaf_bases, leaf_transfers = call(
+    leaf_bases, leaf_transfers, token = call(
         leaf_output_kernel,
-        [((share, *square), f32), ((leaves, *square), f32)],
+        [((share, *square), f32), ((leaves, *square), f32), note],
+        2,
         scalars=[spot],
-        arrays=[bases, inverse, piece, middle_inverse],
+        far=[bases],
+        arrays=[inverse, piece, middle_inverse],
+        scratch=[pltpu.VMEM((share, *square), f32), dma],
     )
     top_low, top_inverse = call(
         top_kernel,
         [(packed, bf16), (packed, f32)],
-        arrays=[up_gram, up_other],
-        after=[leaf_transfers],
+        2.7,
+        arrays=[up_gram, up_other, token],
         scratch=work,
     )
     top_tables = gathered_by_xor(top_low, "leaf", [bit + 2 for bit in quad_bits])
-    new_couplings, top_transfers = call(
+    new_couplings, top_transfers, top_halves, token = call(
         full_kernel,
-        [((rank, rank, blocks), bf16), ((GROUP, *square), f32)],
-        scalars=[source],
-        arrays=[halves, up, top_inverse],
-        tables=tables,
-        scratch=[turned, pltpu.VMEM((len(tables) * leaves, *square), bf16)],
+        [((rank, rank, blocks), bf16), ((GROUP, *square), f32), ((top_blocks, *square), bf16), note],
+        3.5,
+        scalars=[source, top_left],
+        far=[top_couplings],
+        arrays=[halves, up, top_inverse, top_low, *tables],
+        scratch=[
+            pltpu.VMEM((rank, rank, blocks), bf16),
+            turned,
+            pltpu.VMEM((2 * sum(one.shape[0] for one in tables), *square), bf16),
+            pltpu.VMEM(top_couplings.shape, bf16),
+            pltpu.VMEM((leaves, *square), bf16),
+            dma,
+            dma((CHUNKS,)),
+        ],
+        far_outs=1,
     )
     (new_top_couplings,) = call(
         top_project_kernel,
         [((top_blocks, *square), bf16)],
-        scalars=[top_left, top_right],
-        arrays=[top_couplings],
-        after=[new_couplings],
-        tables=top_tables,
-        scratch=[pltpu.VMEM((len(top_tables) * leaves, *square), bf16)],
+        1.5,
+        scalars=[top_right],
+        arrays=[top_halves, token, *top_tables],
+        scratch=[pltpu.VMEM((2 * sum(one.shape[0] for one in top_tables), *square), bf16)],
     )
     new_couplings = jnp.transpose(new_couplings, (2, 0, 1))
     return (leaf_bases, leaf_transfers, top_transfers, new_couplings, new_top_couplings)

time: 45.8 us -> 39.2 us (0.86)
  local copies, waits for them, and re-layouts: 5.99 us -> 1.94 us
  starting transfers between devices: 14.7 us -> 12.6 us
  waiting for transfers between devices: 1.39 us -> 0.73 us
    unnamed x26 -> x22, local copies, waits for them, and re-layouts: 5.99 us -> 1.94 us
    ppermute x11 -> x7, starting transfers between devices: 14.7 us -> 12.6 us  [swapped(): return lax.ppermute(value, axis, pairs)]
    ppermute x11 -> x7, waiting for transfers between devices: 1.39 us -> 0.73 us  [swapped(): return lax.ppermute(value, axis, pairs)]
    pallas_call x7 -> x9, Pallas kernels: 22.5 us -> 22.9 us  [call(): pl.pallas_call(kernel, out_shape=[jax.ShapeDtypeStruct(shape, dtype) for...]
  transfers between devices with their start and end apart: 11 -> 7, of which waited for: 1 -> 2; matrix products, arithmetic and copies ran while one was open for 0% -> 0% of each run, Pallas kernels for 33% -> 54%
where the time goes in v3:
time: 39.2 us; the launch traced here: 39 us
  Pallas kernels  22.9 us (58%)
  starting transfers between devices  12.6 us (32%)
  local copies, waits for them, and re-layouts  1.94 us (5%)
  between operations  0.77 us (2%)
  waiting for transfers between devices  0.73 us (2%)
    pallas_call x9, Pallas kernels, call(): pl.pallas_call(kernel, out_shape=[jax.ShapeDtypeStruct(shape, dtype) for...  22.9 us
    ppermute x7, starting transfers between devices, swapped(): return lax.ppermute(value, axis, pairs)  12.6 us
    unnamed x22, local copies, waits for them, and re-layouts  1.94 us
  transfers between devices with their start and end apart: 7, of which 2 were waited for; matrix products, arithmetic and copies ran while one was open for 0% of the time, Pallas kernels for 54%

profile of v3, /device:TPU:0, one launch (start us, length us, event | category | flops | bytes accessed | tf_op | source)
XLA Modules:
  0.0 39.0 jit_solution(11423893139650359386)
XLA Ops:
  0.6 0.0 copy-start
  0.6 3.0 %collective-permute-start.1 = (f32[4,64,64]{2,1,0:T(8,128)}, f32[4,64,64]{2,1,0:T(8,128)S(1)}, u32[]{:S(2)}, u32[]{:S(2)}) collective-permute-start(f32[4,64,64]{2,1,0:T(8,128)} %top_mine.1), channel_id=1, source_target_pairs={{0,4},{4,0},{8,12},{12,8},{16,20},{20,16},{24,28},{28,24},{1,5},{5... | collective-permute-start | bytes 196616 | tf_op jit(solution)/shard_map/ppermute | solution.py:23
  3.7 0.9 %copy-done.1 = f32[8,64,64]{2,1,0:T(8,128)S(1)} copy-done((f32[8,64,64]{2,1,0:T(8,128)S(1)}, f32[8,64,64]{2,1,0:T(8,128)}, u32[]{:S(2)}) %copy-start.1) | copy-done | bytes 131096
  4.6 0.9 %copy-done.2 = f32[8,64,64]{2,1,0:T(8,128)S(1)} copy-done((f32[8,64,64]{2,1,0:T(8,128)S(1)}, f32[8,64,64]{2,1,0:T(8,128)}, u32[]{:S(2)}) %copy-start.2) | copy-done | bytes 131096
  5.6 0.0 copy-start.6
  5.6 5.0 %shard_map.137 = (bf16[4,64,128]{2,1,0:T(8,128)(2,1)S(1)}, f32[8,64,64]{2,1,0:T(8,128)S(1)}, f32[4,64,128]{2,1,0:T(8,128)S(1)}, f32[4,64,128]{2,1,0:T(8,128)S(1)}) custom-call(f32[8,64,64]{2,1,0:T(8,128)S(1)} %copy-done.2, f32[8,64,64]{2,1,0:T(8,128)S(1)} %copy-done.1), custom_call_target="tpu_custom_call" | custom-call | flops 4499999744 | tf_op jit(solution)/shard_map/pallas_call | solution.py:291
  10.6 2.7 %collective-permute-start.3 = (bf16[4,64,128]{2,1,0:T(8,128)(2,1)S(1)}, bf16[4,64,128]{2,1,0:T(8,128)(2,1)S(1)}, u32[]{:S(2)}, u32[]{:S(2)}) collective-permute-start(bf16[4,64,128]{2,1,0:T(8,128)(2,1)S(1)} %get-tuple-element.26.low.first), channel_id=1, source_target_pairs={{0,16},{4,20},{8,24},{12,28},{16,0},{20,4},{24,8},{28,12},{1,17},{... | collective-permute-start | bytes 196616 | tf_op jit(solution)/shard_map/ppermute | solution.py:23
  13.3 0.5 %collective-permute-start = (f32[4,64,128]{2,1,0:T(8,128)S(1)}, f32[4,64,128]{2,1,0:T(8,128)S(1)}, u32[]{:S(2)}, u32[]{:S(2)}) collective-permute-start(f32[4,64,128]{2,1,0:T(8,128)S(1)} %get-tuple-element.25.mine), channel_id=1, source_target_pairs={{0,4},{4,0},{8,12},{12,8},{16,20},{20,16},{24,28},{28,24},{1,5},{5... | collective-permute-start | bytes 393224 | tf_op jit(solution)/shard_map/ppermute | solution.py:23
  13.8 0.0 copy-done.10
  13.8 0.0 copy-done.7
  13.8 0.0 copy-done.8
  13.8 0.0 copy-done.9
  13.8 0.0 copy-start.5
  13.9 2.5 %shard_map.138 = (bf16[128,64,64]{2,1,0:T(8,128)(2,1)S(1)}, f32[8,128]{1,0:T(8,128)S(1)}) custom-call(s32[128]{0:T(128)S(1)} %copy-done.6, bf16[64,64,128]{2,1,0:T(8,128)(2,1)S(1)} %bitcast.6, bf16[4,64,128]{2,1,0:T(8,128)(2,1)S(1)} %get-tuple-element.26.low.first), custom_call_target="tpu_custom_call" | custom-call | flops 2000000000 | tf_op jit(solution)/shard_map/pallas_call | solution.py:291
  16.4 0.1 pad_add_fusion.spot
  16.4 0.0 collective-permute-done.3.second
  16.5 1.6 %collective-permute-start.4 = (bf16[8,64,128]{2,1,0:T(8,128)(2,1)S(1)}, bf16[8,64,128]{2,1,0:T(8,128)(2,1)S(1)}, u32[]{:S(2)}, u32[]{:S(2)}) collective-permute-start(bf16[8,64,128]{2,1,0:T(8,128)(2,1)S(1)} %shard_map.142.first), channel_id=1, source_target_pairs={{0,8},{4,12},{8,0},{12,4},{16,24},{20,28},{24,16},{28,20},{1,9},{5... | collective-permute-start | bytes 393224 | tf_op jit(solution)/shard_map/ppermute | solution.py:23
  18.1 0.0 collective-permute-done.1.top_other
  18.1 0.1 collective-permute-done.other
  18.2 4.5 %shard_map.139 = (f32[4,64,64]{2,1,0:T(8,128)S(1)}, f32[4,64,128]{2,1,0:T(8,128)S(1)}, f32[4,64,128]{2,1,0:T(8,128)S(1)}) custom-call(s32[2]{0:T(128)S(1)} %pad_add_fusion.spot, f32[4,64,128]{2,1,0:T(8,128)S(1)} %get-tuple-element.25.mine, f32[4,64,128]{2,1,0:T(8,128)S(1)} %collective-permute-done.other, f32[4,64,64]{2,1,0:T(8,128)S(1)} %copy-done.5, ...), custom_call_target="tpu_custom_call" | custom-call | flops 4499999744 | tf_op jit(solution)/shard_map/pallas_call | solution.py:291
  22.8 1.7 %collective-permute-start.2 = (f32[4,64,128]{2,1,0:T(8,128)S(1)}, f32[4,64,128]{2,1,0:T(8,128)S(1)}, u32[]{:S(2)}, u32[]{:S(2)}) collective-permute-start(f32[4,64,128]{2,1,0:T(8,128)S(1)} %get-tuple-element.33.mine), channel_id=1, source_target_pairs={{0,8},{4,12},{8,0},{12,4},{16,24},{20,28},{24,16},{28,20},{1,9},{5... | collective-permute-start | bytes 393224 | tf_op jit(solution)/shard_map/ppermute | solution.py:23
  24.4 0.0 collective-permute-done.4.second
  24.5 0.6 %collective-permute-start.5 = (bf16[16,64,128]{2,1,0:T(8,128)(2,1)S(1)}, bf16[16,64,128]{2,1,0:T(8,128)(2,1)S(1)}, u32[]{:S(2)}, u32[]{:S(2)}) collective-permute-start(bf16[16,64,128]{2,1,0:T(8,128)(2,1)S(1)} %shard_map.143.rest_0_), channel_id=1, source_target_pairs={{0,4},{4,0},{8,12},{12,8},{16,20},{20,16},{24,28},{28,24},{1,5},{5... | collective-permute-start | bytes 786440 | tf_op jit(solution)/shard_map/ppermute | solution.py:23
  25.0 2.2 %shard_map.140 = (f32[2,64,64]{2,1,0:T(8,128)}, f32[8,64,64]{2,1,0:T(8,128)}, f32[8,128]{1,0:T(8,128)S(1)}) custom-call(s32[2]{0:T(128)S(1)} %pad_add_fusion.spot, f32[8,64,64]{2,1,0:T(8,128)S(1)} %copy-done.3, f32[4,64,128]{2,1,0:T(8,128)S(1)} %get-tuple-element.23.inverse, f32[8,64,64]{2,1,0:T(8,128)S(1)} %get-tuple-element.24.piece, ...), custom_call_target="tpu_custom_call" | custom-call | flops 2000000000 | tf_op jit(solution)/shard_map/pallas_call | solution.py:291
  27.2 0.6 %collective-permute-done.2.other = f32[4,64,128]{2,1,0:T(8,128)S(1)} collective-permute-done((f32[4,64,128]{2,1,0:T(8,128)S(1)}, f32[4,64,128]{2,1,0:T(8,128)S(1)}, u32[]{:S(2)}, u32[]{:S(2)}) %collective-permute-start.2) | collective-permute-done | bytes 131104 | tf_op jit(solution)/shard_map/ppermute | solution.py:23
  27.8 2.7 %shard_map.141 = (bf16[4,64,128]{2,1,0:T(8,128)(2,1)S(1)}, f32[4,64,128]{2,1,0:T(8,128)S(1)}) custom-call(f32[4,64,128]{2,1,0:T(8,128)S(1)} %get-tuple-element.33.mine, f32[4,64,128]{2,1,0:T(8,128)S(1)} %collective-permute-done.2.other, f32[8,128]{1,0:T(8,128)S(1)} %get-tuple-element.34.token), custom_call_target="tpu_custom_call" | custom-call | flops 2700000000 | tf_op jit(solution)/shard_map/pallas_call | solution.py:291
  30.5 2.5 %collective-permute-start.6 = (bf16[4,64,128]{2,1,0:T(8,128)(2,1)S(1)}, bf16[4,64,128]{2,1,0:T(8,128)(2,1)S(1)}, u32[]{:S(2)}, u32[]{:S(2)}) collective-permute-start(bf16[4,64,128]{2,1,0:T(8,128)(2,1)S(1)} %get-tuple-element.36.top_low.rest_0_), channel_id=1, source_target_pairs={{0,16},{4,20},{8,24},{12,28},{16,0},{20,4},{24,8},{28,12},{1,17},{... | collective-permute-start | bytes 196616 | tf_op jit(solution)/shard_map/ppermute | solution.py:23
  33.1 0.0 collective-permute-done.5.rest_1_
  33.1 0.0 copy-done.4
  33.1 4.3 %shard_map.144 = (bf16[64,64,128]{2,1,0:T(8,128)(2,1)}, f32[4,64,64]{2,1,0:T(8,128)}, bf16[16,64,64]{2,1,0:T(8,128)(2,1)S(1)}, f32[8,128]{1,0:T(8,128)S(1)}) custom-call(s32[128]{0:T(128)S(1)} %bitcast_add_fusion.source, s32[16]{0:T(128)S(1)} %broadcast_xor_fusion.target, bf16[16,64,64]{2,1,0:T(8,128)(2,1)S(1)} %copy-done.4, ...), custom_call_target="tpu_custom_call" | custom-call | flops 3500000000 | tf_op jit(solution)/shard_map/pallas_call | solution.py:291
  37.3 0.0 collective-permute-done.6.rest_1_
  37.4 1.6 %shard_map.145 = bf16[16,64,64]{2,1,0:T(8,128)(2,1)} custom-call(s32[16]{0:T(128)S(1)} %fusion.1.source, bf16[16,64,64]{2,1,0:T(8,128)(2,1)S(1)} %get-tuple-element.39.halves, f32[8,128]{1,0:T(8,128)S(1)} %get-tuple-element.40.token, bf16[4,64,128]{2,1,0:T(8,128)(2,1)S(1)} %get-tuple-element.36.top_low.rest_0_, ...), custom_call_target="tpu_custom_call" | custom-call | flops 1500000000 | tf_op jit(solution)/shard_map/pallas_call | solution.py:291
  (17 shorter events, 0.1 us)
Async XLA Ops:
  0.6 13.2 %copy-start = (bf16[128,64,64]{0,2,1:T(8,128)(2,1)S(1)}, bf16[128,64,64]{0,2,1:T(8,128)(2,1)}, u32[]{:S(2)}) copy-start(bf16[128,64,64]{0,2,1:T(8,128)(2,1)} %param.13) | copy-start | bytes 3145732
  0.6 17.5 %collective-permute-start.1 = (f32[4,64,64]{2,1,0:T(8,128)}, f32[4,64,64]{2,1,0:T(8,128)S(1)}, u32[]{:S(2)}, u32[]{:S(2)}) collective-permute-start(f32[4,64,64]{2,1,0:T(8,128)} %top_mine.1), channel_id=1, source_target_pairs={{0,4},{4,0},{8,12},{12,8},{16,20},{20,16},{24,28},{28,24},{1,5},{5... | collective-permute-start | bytes 196616 | tf_op jit(solution)/shard_map/ppermute | solution.py:23
  3.7 0.9 %copy-start.1 = (f32[8,64,64]{2,1,0:T(8,128)S(1)}, f32[8,64,64]{2,1,0:T(8,128)}, u32[]{:S(2)}) copy-start(f32[8,64,64]{2,1,0:T(8,128)} %transfer_far.1) | copy-start | bytes 393220
  4.6 0.9 %copy-start.2 = (f32[8,64,64]{2,1,0:T(8,128)S(1)}, f32[8,64,64]{2,1,0:T(8,128)}, u32[]{:S(2)}) copy-start(f32[8,64,64]{2,1,0:T(8,128)} %bases_far.3) | copy-start | bytes 393220
  5.6 8.2 %copy-start.10 = (s32[16]{0:T(128)S(1)}, s32[16]{0:T(128)}, u32[]{:S(2)}) copy-start(s32[16]{0:T(128)} %param.18) | copy-start | bytes 196
  5.6 8.2 %copy-start.7 = (s32[16]{0:T(128)S(1)}, s32[16]{0:T(128)}, u32[]{:S(2)}) copy-start(s32[16]{0:T(128)} %param.19) | copy-start | bytes 196
  5.6 8.2 %copy-start.8 = (s32[128]{0:T(128)S(1)}, s32[128]{0:T(128)}, u32[]{:S(2)}) copy-start(s32[128]{0:T(128)} %param.16) | copy-start | bytes 1540
  5.6 8.2 %copy-start.9 = (s32[128,1]{0,1:T(1,128)S(1)}, s32[128,1]{0,1:T(1,128)}, u32[]{:S(2)}) copy-start(s32[128,1]{0,1:T(1,128)} %param.15) | copy-start | bytes 1540
  5.6 8.3 %copy-start.6 = (s32[128]{0:T(128)S(1)}, s32[128]{0:T(128)}, u32[]{:S(2)}) copy-start(s32[128]{0:T(128)} %target.1) | copy-start | bytes 1540
  10.6 5.8 %collective-permute-start.3 = (bf16[4,64,128]{2,1,0:T(8,128)(2,1)S(1)}, bf16[4,64,128]{2,1,0:T(8,128)(2,1)S(1)}, u32[]{:S(2)}, u32[]{:S(2)}) collective-permute-start(bf16[4,64,128]{2,1,0:T(8,128)(2,1)S(1)} %get-tuple-element.26.low.first), channel_id=1, source_target_pairs={{0,16},{4,20},{8,24},{12,28},{16,0},{20,4},{24,8},{28,12},{1,17},{... | collective-permute-start | bytes 196616 | tf_op jit(solution)/shard_map/ppermute | solution.py:23
  13.3 5.0 %collective-permute-start = (f32[4,64,128]{2,1,0:T(8,128)S(1)}, f32[4,64,128]{2,1,0:T(8,128)S(1)}, u32[]{:S(2)}, u32[]{:S(2)}) collective-permute-start(f32[4,64,128]{2,1,0:T(8,128)S(1)} %get-tuple-element.25.mine), channel_id=1, source_target_pairs={{0,4},{4,0},{8,12},{12,8},{16,20},{20,16},{24,28},{28,24},{1,5},{5... | collective-permute-start | bytes 393224 | tf_op jit(solution)/shard_map/ppermute | solution.py:23
  13.8 4.4 %copy-start.5 = (f32[4,64,64]{2,1,0:T(8,128)S(1)}, f32[4,64,64]{2,1,0:T(8,128)}, u32[]{:S(2)}) copy-start(f32[4,64,64]{2,1,0:T(8,128)} %top_mine.1) | copy-start | bytes 196612
  16.5 8.0 %collective-permute-start.4 = (bf16[8,64,128]{2,1,0:T(8,128)(2,1)S(1)}, bf16[8,64,128]{2,1,0:T(8,128)(2,1)S(1)}, u32[]{:S(2)}, u32[]{:S(2)}) collective-permute-start(bf16[8,64,128]{2,1,0:T(8,128)(2,1)S(1)} %shard_map.142.first), channel_id=1, source_target_pairs={{0,8},{4,12},{8,0},{12,4},{16,24},{20,28},{24,16},{28,20},{1,9},{5... | collective-permute-start | bytes 393224 | tf_op jit(solution)/shard_map/ppermute | solution.py:23
  18.2 6.8 %copy-start.3 = (f32[8,64,64]{2,1,0:T(8,128)S(1)}, f32[8,64,64]{2,1,0:T(8,128)}, u32[]{:S(2)}) copy-start(f32[8,64,64]{2,1,0:T(8,128)} %bases_far.3) | copy-start | bytes 393220
  22.8 5.1 %collective-permute-start.2 = (f32[4,64,128]{2,1,0:T(8,128)S(1)}, f32[4,64,128]{2,1,0:T(8,128)S(1)}, u32[]{:S(2)}, u32[]{:S(2)}) collective-permute-start(f32[4,64,128]{2,1,0:T(8,128)S(1)} %get-tuple-element.33.mine), channel_id=1, source_target_pairs={{0,8},{4,12},{8,0},{12,4},{16,24},{20,28},{24,16},{28,20},{1,9},{5... | collective-permute-start | bytes 393224 | tf_op jit(solution)/shard_map/ppermute | solution.py:23
  24.5 8.6 %collective-permute-start.5 = (bf16[16,64,128]{2,1,0:T(8,128)(2,1)S(1)}, bf16[16,64,128]{2,1,0:T(8,128)(2,1)S(1)}, u32[]{:S(2)}, u32[]{:S(2)}) collective-permute-start(bf16[16,64,128]{2,1,0:T(8,128)(2,1)S(1)} %shard_map.143.rest_0_), channel_id=1, source_target_pairs={{0,4},{4,0},{8,12},{12,8},{16,20},{20,16},{24,28},{28,24},{1,5},{5... | collective-permute-start | bytes 786440 | tf_op jit(solution)/shard_map/ppermute | solution.py:23
  27.8 5.2 %copy-start.4 = (bf16[16,64,64]{2,1,0:T(8,128)(2,1)S(1)}, bf16[16,64,64]{2,1,0:T(8,128)(2,1)}, u32[]{:S(2)}) copy-start(bf16[16,64,64]{2,1,0:T(8,128)(2,1)} %top_far.1) | copy-start | bytes 393220
  30.5 6.8 %collective-permute-start.6 = (bf16[4,64,128]{2,1,0:T(8,128)(2,1)S(1)}, bf16[4,64,128]{2,1,0:T(8,128)(2,1)S(1)}, u32[]{:S(2)}, u32[]{:S(2)}) collective-permute-start(bf16[4,64,128]{2,1,0:T(8,128)(2,1)S(1)} %get-tuple-element.36.top_low.rest_0_), channel_id=1, source_target_pairs={{0,16},{4,20},{8,24},{12,28},{16,0},{20,4},{24,8},{28,12},{1,17},{... | collective-permute-start | bytes 196616 | tf_op jit(solution)/shard_map/ppermute | solution.py:23

commit v4 on v3

--- a/solution.py
+++ b/solution.py
@@ -23,23 +23,25 @@
     return lax.ppermute(value, axis, pairs)
 
 
-def gathered_by_xor(value, axis, bits):
-    for step, bit in enumerate(bits):
-        other = swapped(value, axis, 1 << bit)
-        if step == len(bits) - 1:
-            return [value, other]
-        value = joined(value, other)
-    return [value]
-
-
-def join_kernel(first, second, out):
+def join_kernel(first, second, after, out):
     out[: first.shape[0]] = first[...]
     out[first.shape[0] :] = second[...]
 
 
-def joined(first, second):
-    shape = (first.shape[0] + second.shape[0], *first.shape[1:])
-    return call(join_kernel, [(shape, first.dtype)], 0.5, arrays=[first, second])[0]
+def hold_kernel(value, after, out):
+    out[...] = value[...]
+
+
+def held(value, after):
+    return call(hold_kernel, [(value.shape, value.dtype)], 0.1, arrays=[value, after])[0]
+
+
+def joined_by_xor(value, axis, bits, after):
+    for bit in bits:
+        other = swapped(value, axis, 1 << bit)
+        shape = (2 * value.shape[0], *value.shape[1:])
+        (value,) = call(join_kernel, [(shape, value.dtype)], 0.2, arrays=[value, other, after])
+    return value
 
 
 def place_of(difference, bits):
@@ -130,51 +132,51 @@
     return jnp.concatenate([left, right], axis=1)
 
 
-def leaf_kernel(bases_far, transfer_far, low, piece, gram, inverse_out, bases, transfer, work, factor, inverse, arrived):
-    rank = bases.shape[2]
-    first = pltpu.make_async_copy(bases_far, bases, arrived.at[0])
-    second = pltpu.make_async_copy(transfer_far, transfer, arrived.at[1])
-    first.start()
-    second.start()
-    first.wait()
+def gram_kernel(bases, gram):
     for g in range(GROUP):
         left, right = bases[g], bases[g + GROUP]
-        work[matrix_pair(work, g), :] = side_by_side(dot_tn(left, left), dot_tn(right, right))
+        gram[g] = side_by_side(dot_tn(left, left), dot_tn(right, right))
+
+
+def congruent(gram, left, right):
+    rank = gram.shape[0]
+    first = dot_tn(left, dot_nn(gram[:, :rank], left))
+    second = dot_tn(right, dot_nn(gram[:, rank:], right))
+    return side_by_side(first, second)
+
+
+def child_kernel(gram, transfer, top, message, token):
+    token[...] = jnp.zeros_like(token)
+    for g in range(GROUP):
+        message[g] = congruent(gram[g], transfer[g], transfer[g + GROUP])
+    for n in range(GROUP // 2):
+        message[GROUP + n] = side_by_side(top[2 * n], top[2 * n + 1])
+
+
+def middle_kernel(spot, mine, other, after, middle_gram, top_gram, token):
+    rank = middle_gram.shape[1]
+    token[...] = jnp.zeros_like(token)
+    for g in range(GROUP):
+        both = mine[g] + other[g]
+        middle_gram[g] = both
+        both = jnp.where(spot[1] == 0, both, pltpu.roll(both, rank, axis=1))
+        lanes = slice(g % 2 * rank, (g % 2 + 1) * rank)
+        top_gram[g] = congruent(both, mine[GROUP + g // 2][:, lanes], other[GROUP + g // 2][:, lanes])
+
+
+def factor_kernel(terms, has_factor, has_low, *refs):
+    grams, refs = refs[:terms], refs[terms + 1 :]
+    outs, (work, factor, inverse) = refs[:-3], refs[-3:]
+    for g in range(GROUP):
+        work[matrix_pair(work, g), :] = grams[0][g] if terms == 1 else grams[0][g] + grams[1][g]
     eliminate(work, factor, inverse)
-    second.wait()
     for g in range(GROUP):
         both = factor[matrix_pair(work, g), :]
-        left = dot_nn(both[:, :rank], transfer[g])
-        right = dot_nn(both[:, rank:], transfer[g + GROUP])
-        piece[g] = left
-        piece[g + GROUP] = right
-        gram[g] = side_by_side(dot_tn(left, left), dot_tn(right, right))
-        low[g] = both.astype(bf16)
-        inverse_out[g] = inverse[matrix_pair(work, g), :]
-
-
-def middle_kernel(spot, mine, other, top_mine, top_other, token, up, gram, inverse_out, work, factor, inverse):
-    rank = top_mine.shape[2]
-    for g in range(GROUP):
-        work[matrix_pair(work, g), :] = mine[g] + other[g]
-    eliminate(work, factor, inverse)
-    for g in range(GROUP):
-        both = factor[matrix_pair(work, g), :]
-        both = jnp.where(spot[1] == 0, both, pltpu.roll(both, rank, axis=1))
-        left = dot_nn(both[:, :rank], top_mine[g])
-        right = dot_nn(both[:, rank:], top_other[g])
-        up[g] = left
-        gram[g] = side_by_side(dot_tn(left, left), dot_tn(right, right))
-        inverse_out[g] = inverse[matrix_pair(work, g), :]
-
-
-def top_kernel(mine, other, token, low, inverse_out, work, factor, inverse):
-    for g in range(GROUP):
-        work[matrix_pair(work, g), :] = mine[g] + other[g]
-    eliminate(work, factor, inverse)
-    for g in range(GROUP):
-        low[g] = factor[matrix_pair(work, g), :].astype(bf16)
-        inverse_out[g] = inverse[matrix_pair(work, g), :]
+        outs[0][g] = inverse[matrix_pair(work, g), :]
+        if has_factor:
+            outs[1][g] = both
+        if has_low:
+            outs[-1][g] = both.astype(bf16)
 
 
 def half_kernel(target, couplings_far, low, halves, token, couplings, turned, table, arrived):
@@ -200,19 +202,39 @@
         halves[r] = low_nn(table[target[r]], block).astype(bf16)
 
 
-def leaf_output_kernel(spot, bases_far, inverse, piece, middle_inverse, leaf_bases, leaf_transfers, token, bases, arrived):
+def output_kernel(
+    spot,
+    bases_far,
+    after,
+    leaf_factor,
+    leaf_inverse,
+    leaf_transfer,
+    middle_factor,
+    middle_inverse,
+    top_transfer,
+    top_inverse,
+    leaf_bases,
+    leaf_transfers,
+    top_transfers,
+    token,
+    bases,
+    arrived,
+):
     share, _, rank = bases.shape
     token[...] = jnp.zeros_like(token)
     copy = pltpu.make_async_copy(bases_far.at[pl.ds(spot[0] * share, share)], bases, arrived)
     copy.start()
     for g in range(GROUP):
-        both = middle_inverse[g]
-        leaf_transfers[g] = dot_nt(piece[g], both[:, :rank])
-        leaf_transfers[g + GROUP] = dot_nt(piece[g + GROUP], both[:, rank:])
+        for place, lanes in ((g, slice(0, rank)), (g + GROUP, slice(rank, 2 * rank))):
+            piece = dot_nn(leaf_factor[g][:, lanes], leaf_transfer[place])
+            leaf_transfers[place] = dot_nt(piece, middle_inverse[g][:, lanes])
+        both = middle_factor[g]
+        piece = dot_nn(jnp.where(spot[1] == 0, both[:, :rank], both[:, rank:]), top_transfer[g])
+        top_transfers[g] = dot_nt(piece, top_inverse[g][:, :rank])
     copy.wait()
     for k in range(share):
         place = spot[0] * share + k
-        both = inverse[place % GROUP]
+        both = leaf_inverse[place % GROUP]
         both = jnp.where(place < GROUP, both[:, :rank], both[:, rank:])
         leaf_bases[k] = dot_nt(bases[k], both)
 
@@ -230,28 +252,18 @@
     lax.fori_loop(0, count, step, 0, unroll=min(count, 16))
 
 
-def full_kernel(
-    source,
-    target,
-    top_far,
-    halves,
-    up,
-    inverse,
-    top_low,
-    *rest,
-):
-    packed, rest = rest[:-11], rest[-11:]
-    out_far, top_transfers, top_halves, token = rest[:4]
-    out, turned, table, top_couplings, top_table, arrived, left = rest[4:]
-    count, rank, _ = halves.shape
-    pitch = turned.shape[0] // rank
-    token[...] = jnp.zeros_like(token)
-    copy = pltpu.make_async_copy(top_far, top_couplings, arrived)
-    copy.start()
+def unpack_all(packed, table):
     base = 0
     for one in packed:
         unpack(one, table, base)
         base += 2 * one.shape[0]
+
+
+def full_kernel(source, halves, token, *rest):
+    packed, (out_far, out, turned, table, left) = rest[:-5], rest[-5:]
+    count, rank, _ = halves.shape
+    pitch = turned.shape[0] // rank
+    unpack_all(packed, table)
     for r in range(count):
         turned[pl.ds(r, rank, stride=pitch), :] = low_nt(halves[r], table[source[r]])
     chunk = rank // CHUNKS
@@ -262,24 +274,17 @@
         part = pl.ds(k * chunk, chunk)
         copies.append(pltpu.make_async_copy(out.at[part], out_far.at[part], left.at[k]))
         copies[k].start()
-    unpack(top_low, top_table, 0)
-    for g in range(GROUP):
-        top_transfers[g] = dot_nt(up[g], inverse[g][:, :rank])
-    copy.wait()
-    for r in range(top_couplings.shape[0]):
-        top_halves[r] = low_nn(top_table[target[r]], top_couplings[r]).astype(bf16)
     for copy in copies:
         copy.wait()
 
 
-def top_project_kernel(source, halves, token, *rest):
-    packed, (out, table) = rest[:-2], rest[-2:]
-    base = 0
-    for one in packed:
-        unpack(one, table, base)
-        base += 2 * one.shape[0]
-    for r in range(halves.shape[0]):
-        out[r] = low_nt(halves[r], table[source[r]]).astype(bf16)
+def top_project_kernel(target, source, couplings, after, *rest):
+    packed, (out, token, table) = rest[:-3], rest[-3:]
+    token[...] = jnp.zeros_like(token)
+    unpack_all(packed, table)
+    for r in range(couplings.shape[0]):
+        half = low_nn(table[target[r]], couplings[r]).astype(bf16)
+        out[r] = low_nt(half, table[source[r]]).astype(bf16)
 
 
 vmem = pl.BlockSpec(memory_space=pltpu.VMEM)
@@ -333,76 +338,88 @@
     note = ((8, 2 * rank), f32)
     dma = pltpu.SemaphoreType.DMA
 
-    top_other = swapped(top_transfer, "leaf", 1)
-    low, piece, gram, inverse = call(
-        leaf_kernel,
-        [(packed, bf16), ((leaves, *square), f32), (packed, f32), (packed, f32)],
-        4.5,
-        far=[bases, leaf_transfer],
-        scratch=[pltpu.VMEM(bases.shape, f32), pltpu.VMEM(leaf_transfer.shape, f32), *work, dma((2,))],
-    )
-    gram_other = swapped(gram, "leaf", 1)
-    halves, token = call(
+
+    def factored(grams, after, has_factor, has_low):
+        return call(
+            functools.partial(factor_kernel, len(grams), has_factor, has_low),
+            [(packed, f32)] * (1 + has_factor) + [(packed, bf16)] * has_low,
+            2.6,
+            arrays=[*grams, after],
+            scratch=work,
+        )
+
+    (gram,) = call(gram_kernel, [(packed, f32)], 0.6, arrays=[bases])
+    message, token = call(
+        child_kernel,
+        [((GROUP + GROUP // 2, *packed[1:]), f32), note],
+        0.8,
+        arrays=[gram, leaf_transfer, top_transfer],
+    )
+    message_other = swapped(message, "leaf", 1)
+    leaf_inverse, leaf_factor, low = factored([gram], token, True, True)
+    halves, half_token = call(
         half_kernel,
         [((blocks, *square), bf16), note],
-        2,
+        2.7,
         scalars=[coupling_target],
         far=[jnp.transpose(couplings, (1, 2, 0))],
         arrays=[low],
         scratch=[pltpu.VMEM((rank, rank, blocks), bf16), turned, pltpu.VMEM((leaves, *square), bf16), dma((CHUNKS,))],
     )
-    tables = gathered_by_xor(low, "leaf", leaf_bits)
-    up, up_gram, middle_inverse = call(
+    middle_gram, top_gram, token = call(
         middle_kernel,
-        [((GROUP, *square), f32), (packed, f32), (packed, f32)],
-        4.5,
+        [(packed, f32), (packed, f32), note],
+        1.4,
         scalars=[spot],
-        arrays=[gram, gram_other, top_transfer, top_other, token],
-        scratch=work,
-    )
-    up_other = swapped(up_gram, "leaf", 2)
-    leaf_bases, leaf_transfers, token = call(
-        leaf_output_kernel,
-        [((share, *square), f32), ((leaves, *square), f32), note],
-        2,
+        arrays=[message, message_other, half_token],
+    )
+    top_gram_other = swapped(top_gram, "leaf", 2)
+    middle_inverse, middle_factor = factored([middle_gram], token, True, False)
+    table = joined_by_xor(held(low, half_token), "leaf", leaf_bits[:1], middle_inverse)
+    top_inverse, top_low = factored([top_gram, top_gram_other], table, False, True)
+    top_table = joined_by_xor(top_low, "leaf", [bit + 2 for bit in quad_bits[:-1]], top_inverse)
+    top_tables = [top_table, swapped(top_table, "leaf", 4 << quad_bits[-1])]
+    table = joined_by_xor(table, "leaf", leaf_bits[1:-1], top_inverse)
+    tables = [table, swapped(table, "leaf", 1 << leaf_bits[-1])]
+    leaf_bases, leaf_transfers, top_transfers, token = call(
+        output_kernel,
+        [((share, *square), f32), ((leaves, *square), f32), ((GROUP, *square), f32), note],
+        2.4,
         scalars=[spot],
         far=[bases],
-        arrays=[inverse, piece, middle_inverse],
+        arrays=[
+            table,
+            leaf_factor,
+            leaf_inverse,
+            leaf_transfer,
+            middle_factor,
+            middle_inverse,
+            top_transfer,
+            top_inverse,
+        ],
         scratch=[pltpu.VMEM((share, *square), f32), dma],
     )
-    top_low, top_inverse = call(
-        top_kernel,
-        [(packed, bf16), (packed, f32)],
-        2.7,
-        arrays=[up_gram, up_other, token],
-        scratch=work,
-    )
-    top_tables = gathered_by_xor(top_low, "leaf", [bit + 2 for bit in quad_bits])
-    new_couplings, top_transfers, top_halves, token = call(
+    new_top_couplings, token = call(
+        top_project_kernel,
+        [((top_blocks, *square), bf16), note],
+        1.5,
+        scalars=[top_left, top_right],
+        arrays=[top_couplings, token, *top_tables],
+        scratch=[pltpu.VMEM((2 * sum(one.shape[0] for one in top_tables), *square), bf16)],
+    )
+    (new_couplings,) = call(
         full_kernel,
-        [((rank, rank, blocks), bf16), ((GROUP, *square), f32), ((top_blocks, *square), bf16), note],
+        [((rank, rank, blocks), bf16)],
         3.5,
-        scalars=[source, top_left],
-        far=[top_couplings],
-        arrays=[halves, up, top_inverse, top_low, *tables],
+        scalars=[source],
+        arrays=[halves, token, *tables],
         scratch=[
             pltpu.VMEM((rank, rank, blocks), bf16),
             turned,
             pltpu.VMEM((2 * sum(one.shape[0] for one in tables), *square), bf16),
-            pltpu.VMEM(top_couplings.shape, bf16),
-            pltpu.VMEM((leaves, *square), bf16),
-            dma,
             dma((CHUNKS,)),
         ],
         far_outs=1,
-    )
-    (new_top_couplings,) = call(
-        top_project_kernel,
-        [((top_blocks, *square), bf16)],
-        1.5,
-        scalars=[top_right],
-        arrays=[top_halves, token, *top_tables],
-        scratch=[pltpu.VMEM((2 * sum(one.shape[0] for one in top_tables), *square), bf16)],
     )
     new_couplings = jnp.transpose(new_couplings, (2, 0, 1))
     return (leaf_bases, leaf_transfers, top_transfers, new_couplings, new_top_couplings)

time: 39.2 us -> 35.7 us (0.911)
  starting transfers between devices: 12.6 us -> 9.66 us
  local copies, waits for them, and re-layouts: 1.94 us -> 1.49 us
    ppermute x7 -> x6, starting transfers between devices: 12.6 us -> 9.66 us  [swapped(): return lax.ppermute(value, axis, pairs)]
    unnamed x22, local copies, waits for them, and re-layouts: 1.94 us -> 1.49 us
    pallas_call x9 -> x13, Pallas kernels: 22.9 us -> 22.7 us  [call(): pl.pallas_call(kernel, out_shape=[jax.ShapeDtypeStruct(shape, dtype) for...]
  transfers between devices with their start and end apart: 7 -> 6, of which waited for: 2 -> 2; matrix products, arithmetic and copies ran while one was open for 0% -> 0% of each run, Pallas kernels for 54% -> 51%
where the time goes in v4:
time: 35.7 us; the launch traced here: 35.6 us
  Pallas kernels  22.7 us (64%)
  starting transfers between devices  9.66 us (27%)
  local copies, waits for them, and re-layouts  1.49 us (4%)
  between operations  0.97 us (3%)
  waiting for transfers between devices  0.59 us (2%)
    pallas_call x13, Pallas kernels, call(): pl.pallas_call(kernel, out_shape=[jax.ShapeDtypeStruct(shape, dtype) for...  22.7 us
    ppermute x6, starting transfers between devices, swapped(): return lax.ppermute(value, axis, pairs)  9.66 us
    unnamed x22, local copies, waits for them, and re-layouts  1.49 us
  transfers between devices with their start and end apart: 6, of which 2 were waited for; matrix products, arithmetic and copies ran while one was open for 0% of the time, Pallas kernels for 51%

profile of v4, /device:TPU:0, one launch (start us, length us, event | category | flops | bytes accessed | tf_op | source)
XLA Modules:
  0.0 35.6 jit_solution(13967402672564911766)
XLA Ops:
  0.6 0.0 copy-start.1
  0.6 0.9 %copy-done.1 = f32[8,64,64]{2,1,0:T(8,128)S(1)} copy-done((f32[8,64,64]{2,1,0:T(8,128)S(1)}, f32[8,64,64]{2,1,0:T(8,128)}, u32[]{:S(2)}) %copy-start.1) | copy-done | bytes 131096
  1.6 0.5 %shard_map.137.gram.refs_0_ = f32[4,64,128]{2,1,0:T(8,128)S(1)} custom-call(f32[8,64,64]{2,1,0:T(8,128)S(1)} %copy-done.1), custom_call_target="tpu_custom_call" | custom-call | flops 600000000 | tf_op jit(solution)/shard_map/pallas_call | solution.py:296
  2.1 0.5 %copy-done.3 = f32[8,64,64]{2,1,0:T(8,128)S(1)} copy-done((f32[8,64,64]{2,1,0:T(8,128)S(1)}, f32[8,64,64]{2,1,0:T(8,128)}, u32[]{:S(2)}) %copy-start.3) | copy-done | bytes 131096
  2.5 0.0 copy-done.5
  2.6 0.8 %shard_map.138 = (f32[6,64,128]{2,1,0:T(8,128)S(1)}, f32[8,128]{1,0:T(8,128)S(1)}) custom-call(f32[4,64,128]{2,1,0:T(8,128)S(1)} %shard_map.137.gram.refs_0_, f32[8,64,64]{2,1,0:T(8,128)S(1)} %copy-done.3, f32[4,64,64]{2,1,0:T(8,128)S(1)} %copy-done.5), custom_call_target="tpu_custom_call" | custom-call | flops 800000000 | tf_op jit(solution)/shard_map/pallas_call | solution.py:296
  3.4 3.0 %collective-permute-start.1 = (f32[6,64,128]{2,1,0:T(8,128)S(1)}, f32[6,64,128]{2,1,0:T(8,128)S(1)}, u32[]{:S(2)}, u32[]{:S(2)}) collective-permute-start(f32[6,64,128]{2,1,0:T(8,128)S(1)} %get-tuple-element.28.mine), channel_id=1, source_target_pairs={{0,4},{4,0},{8,12},{12,8},{16,20},{20,16},{24,28},{28,24},{1,5},{5... | collective-permute-start | bytes 589832 | tf_op jit(solution)/shard_map/ppermute | solution.py:23
  6.4 2.7 %shard_map.139 = (f32[4,64,128]{2,1,0:T(8,128)S(1)}, f32[4,64,128]{2,1,0:T(8,128)S(1)}, bf16[4,64,128]{2,1,0:T(8,128)(2,1)S(1)}) custom-call(f32[4,64,128]{2,1,0:T(8,128)S(1)} %shard_map.137.gram.refs_0_, f32[8,128]{1,0:T(8,128)S(1)} %get-tuple-element.25.refs_1_), custom_call_target="tpu_custom_call" | custom-call | flops 2600000000 | tf_op jit(solution)/shard_map/pallas_call | solution.py:296
  9.1 0.0 copy-start.7
  9.1 0.0 copy-start.8
  9.1 0.0 copy-start.9
  9.1 0.0 copy-start.10
  9.2 2.7 %shard_map.140 = (bf16[128,64,64]{2,1,0:T(8,128)(2,1)S(1)}, f32[8,128]{1,0:T(8,128)S(1)}) custom-call(s32[128]{0:T(128)S(1)} %copy-done.6, bf16[64,64,128]{2,1,0:T(8,128)(2,1)S(1)} %bitcast.6, bf16[4,64,128]{2,1,0:T(8,128)(2,1)S(1)} %get-tuple-element.26.low.value), custom_call_target="tpu_custom_call" | custom-call | flops 2700000000 | tf_op jit(solution)/shard_map/pallas_call | solution.py:296
  11.9 2.7 %collective-permute-start = (bf16[4,64,128]{2,1,0:T(8,128)(2,1)S(1)}, bf16[4,64,128]{2,1,0:T(8,128)(2,1)S(1)}, u32[]{:S(2)}, u32[]{:S(2)}) collective-permute-start(bf16[4,64,128]{2,1,0:T(8,128)(2,1)S(1)} %shard_map.141.first), channel_id=1, source_target_pairs={{0,16},{4,20},{8,24},{12,28},{16,0},{20,4},{24,8},{28,12},{1,17},{... | collective-permute-start | bytes 196616 | tf_op jit(solution)/shard_map/ppermute | solution.py:23
  14.5 0.1 pad_add_fusion.spot
  14.6 0.0 collective-permute-done.1.other
  14.7 1.4 %shard_map.142 = (f32[4,64,128]{2,1,0:T(8,128)S(1)}, f32[4,64,128]{2,1,0:T(8,128)S(1)}, f32[8,128]{1,0:T(8,128)S(1)}) custom-call(s32[2]{0:T(128)S(1)} %pad_add_fusion.spot, f32[6,64,128]{2,1,0:T(8,128)S(1)} %get-tuple-element.28.mine, f32[6,64,128]{2,1,0:T(8,128)S(1)} %collective-permute-done.1.other, f32[8,128]{1,0:T(8,128)S(1)} %get-tuple-element.27.after), custom_call_target="tpu_custom_call" | custom-call | flops 1400000000 | tf_op jit(solution)/shard_map/pallas_call | solution.py:296
  16.1 1.6 %collective-permute-start.3 = (f32[4,64,128]{2,1,0:T(8,128)S(1)}, f32[4,64,128]{2,1,0:T(8,128)S(1)}, u32[]{:S(2)}, u32[]{:S(2)}) collective-permute-start(f32[4,64,128]{2,1,0:T(8,128)S(1)} %get-tuple-element.32.refs_0_), channel_id=1, source_target_pairs={{0,8},{4,12},{8,0},{12,4},{16,24},{20,28},{24,16},{28,20},{1,9},{5... | collective-permute-start | bytes 393224 | tf_op jit(solution)/shard_map/ppermute | solution.py:23
  17.7 2.7 %shard_map.143 = (f32[4,64,128]{2,1,0:T(8,128)S(1)}, f32[4,64,128]{2,1,0:T(8,128)S(1)}) custom-call(f32[4,64,128]{2,1,0:T(8,128)S(1)} %get-tuple-element.29.refs_0_, f32[8,128]{1,0:T(8,128)S(1)} %get-tuple-element.30.refs_1_), custom_call_target="tpu_custom_call" | custom-call | flops 2600000000 | tf_op jit(solution)/shard_map/pallas_call | solution.py:296
  20.4 0.0 collective-permute-done.second
  20.4 0.0 copy-start.2
  20.4 0.5 %collective-permute-start.2 = (bf16[8,64,128]{2,1,0:T(8,128)(2,1)S(1)}, bf16[8,64,128]{2,1,0:T(8,128)(2,1)S(1)}, u32[]{:S(2)}, u32[]{:S(2)}) collective-permute-start(bf16[8,64,128]{2,1,0:T(8,128)(2,1)S(1)} %shard_map.144.refs_2_.first), channel_id=1, source_target_pairs={{0,8},{4,12},{8,0},{12,4},{16,24},{20,28},{24,16},{28,20},{1,9},{5... | collective-permute-start | bytes 393224 | tf_op jit(solution)/shard_map/ppermute | solution.py:23
  20.9 0.2 collective-permute-done.3.refs_1_
  21.1 2.7 %shard_map.145 = (f32[4,64,128]{2,1,0:T(8,128)S(1)}, bf16[4,64,128]{2,1,0:T(8,128)(2,1)S(1)}) custom-call(f32[4,64,128]{2,1,0:T(8,128)S(1)} %get-tuple-element.32.refs_0_, f32[4,64,128]{2,1,0:T(8,128)S(1)} %collective-permute-done.3.refs_1_, bf16[8,64,128]{2,1,0:T(8,128)(2,1)S(1)} %shard_map.144.refs_2_.first), custom_call_target="tpu_custom_call" | custom-call | flops 2600000000 | tf_op jit(solution)/shard_map/pallas_call | solution.py:296
  23.8 1.2 %collective-permute-start.4 = (bf16[4,64,128]{2,1,0:T(8,128)(2,1)S(1)}, bf16[4,64,128]{2,1,0:T(8,128)(2,1)S(1)}, u32[]{:S(2)}, u32[]{:S(2)}) collective-permute-start(bf16[4,64,128]{2,1,0:T(8,128)(2,1)S(1)} %get-tuple-element.42.rest_0_), channel_id=1, source_target_pairs={{0,16},{4,20},{8,24},{12,28},{16,0},{20,4},{24,8},{28,12},{1,17},{... | collective-permute-start | bytes 196616 | tf_op jit(solution)/shard_map/ppermute | solution.py:23
  25.0 0.4 %collective-permute-done.2.second = bf16[8,64,128]{2,1,0:T(8,128)(2,1)S(1)} collective-permute-done((bf16[8,64,128]{2,1,0:T(8,128)(2,1)S(1)}, bf16[8,64,128]{2,1,0:T(8,128)(2,1)S(1)}, u32[]{:S(2)}, u32[]{:S(2)}) %collective-permute-start.2) | collective-permute-done | bytes 131104 | tf_op jit(solution)/shard_map/ppermute | solution.py:23
  25.5 0.6 %collective-permute-start.5 = (bf16[16,64,128]{2,1,0:T(8,128)(2,1)S(1)}, bf16[16,64,128]{2,1,0:T(8,128)(2,1)S(1)}, u32[]{:S(2)}, u32[]{:S(2)}) collective-permute-start(bf16[16,64,128]{2,1,0:T(8,128)(2,1)S(1)} %shard_map.146.after.rest_0_), channel_id=1, source_target_pairs={{0,4},{4,0},{8,12},{12,8},{16,20},{20,16},{24,28},{28,24},{1,5},{5... | collective-permute-start | bytes 786440 | tf_op jit(solution)/shard_map/ppermute | solution.py:23
  26.1 3.3 %shard_map.147 = (f32[2,64,64]{2,1,0:T(8,128)}, f32[8,64,64]{2,1,0:T(8,128)}, f32[4,64,64]{2,1,0:T(8,128)}, f32[8,128]{1,0:T(8,128)S(1)}) custom-call(s32[2]{0:T(128)S(1)} %pad_add_fusion.spot, f32[8,64,64]{2,1,0:T(8,128)S(1)} %copy-done.2, bf16[16,64,128]{2,1,0:T(8,128)(2,1)S(1)} %shard_map.146.after.rest_0_, ...), custom_call_target="tpu_custom_call" | custom-call | flops 2400000000 | tf_op jit(solution)/shard_map/pallas_call | solution.py:296
  29.4 0.0 collective-permute-done.4.rest_1_
  29.4 2.5 %shard_map.148 = (bf16[16,64,64]{2,1,0:T(8,128)(2,1)}, f32[8,128]{1,0:T(8,128)S(1)}) custom-call(s32[16]{0:T(128)S(1)} %get-tuple-element.46.target, s32[16]{0:T(128)S(1)} %get-tuple-element.45.source, bf16[16,64,64]{2,1,0:T(8,128)(2,1)S(1)} %copy-done.4, f32[8,128]{1,0:T(8,128)S(1)} %get-tuple-element.41.after, ...), custom_call_target="tpu_custom_call" | custom-call | flops 1500000000 | tf_op jit(solution)/shard_map/pallas_call | solution.py:296
  31.9 0.0 collective-permute-done.5.rest_1_
  31.9 3.5 %shard_map.149 = bf16[64,64,128]{2,1,0:T(8,128)(2,1)} custom-call(s32[128]{0:T(128)S(1)} %bitcast_add_fusion.source, bf16[128,64,64]{2,1,0:T(8,128)(2,1)S(1)} %get-tuple-element.40.halves, f32[8,128]{1,0:T(8,128)S(1)} %get-tuple-element.43.token, bf16[16,64,128]{2,1,0:T(8,128)(2,1)S(1)} %shard_map.146.after.rest_0_, ...), custom_call_target="tpu_custom_call" | custom-call | flops 3500000000 | tf_op jit(solution)/shard_map/pallas_call | solution.py:296
  (18 shorter events, 0.1 us)
Async XLA Ops:
  0.6 1.0 %copy-start.1 = (f32[8,64,64]{2,1,0:T(8,128)S(1)}, f32[8,64,64]{2,1,0:T(8,128)}, u32[]{:S(2)}) copy-start(f32[8,64,64]{2,1,0:T(8,128)} %bases_far.1) | copy-start | bytes 393220
  1.6 0.9 %copy-start.3 = (f32[8,64,64]{2,1,0:T(8,128)S(1)}, f32[8,64,64]{2,1,0:T(8,128)}, u32[]{:S(2)}) copy-start(f32[8,64,64]{2,1,0:T(8,128)} %leaf_transfer.1) | copy-start | bytes 393220
  1.6 1.0 %copy-start.5 = (f32[4,64,64]{2,1,0:T(8,128)S(1)}, f32[4,64,64]{2,1,0:T(8,128)}, u32[]{:S(2)}) copy-start(f32[4,64,64]{2,1,0:T(8,128)} %top_transfer.1) | copy-start | bytes 196612
  3.4 11.3 %collective-permute-start.1 = (f32[6,64,128]{2,1,0:T(8,128)S(1)}, f32[6,64,128]{2,1,0:T(8,128)S(1)}, u32[]{:S(2)}, u32[]{:S(2)}) collective-permute-start(f32[6,64,128]{2,1,0:T(8,128)S(1)} %get-tuple-element.28.mine), channel_id=1, source_target_pairs={{0,4},{4,0},{8,12},{12,8},{16,20},{20,16},{24,28},{28,24},{1,5},{5... | collective-permute-start | bytes 589832 | tf_op jit(solution)/shard_map/ppermute | solution.py:23
  6.4 2.7 %copy-start = (bf16[128,64,64]{0,2,1:T(8,128)(2,1)S(1)}, bf16[128,64,64]{0,2,1:T(8,128)(2,1)}, u32[]{:S(2)}) copy-start(bf16[128,64,64]{0,2,1:T(8,128)(2,1)} %param.13) | copy-start | bytes 3145732
  6.4 2.7 %copy-start.6 = (s32[128]{0:T(128)S(1)}, s32[128]{0:T(128)}, u32[]{:S(2)}) copy-start(s32[128]{0:T(128)} %target.1) | copy-start | bytes 1540
  9.1 5.5 %copy-start.7 = (s32[16]{0:T(128)S(1)}, s32[16]{0:T(128)}, u32[]{:S(2)}) copy-start(s32[16]{0:T(128)} %param.19) | copy-start | bytes 196
  9.1 5.5 %copy-start.8 = (s32[16]{0:T(128)S(1)}, s32[16]{0:T(128)}, u32[]{:S(2)}) copy-start(s32[16]{0:T(128)} %param.18) | copy-start | bytes 196
  9.1 5.5 %copy-start.9 = (s32[128]{0:T(128)S(1)}, s32[128]{0:T(128)}, u32[]{:S(2)}) copy-start(s32[128]{0:T(128)} %param.16) | copy-start | bytes 1540
  9.1 5.5 %copy-start.10 = (s32[128,1]{0,1:T(1,128)S(1)}, s32[128,1]{0,1:T(1,128)}, u32[]{:S(2)}) copy-start(s32[128,1]{0,1:T(1,128)} %param.15) | copy-start | bytes 1540
  11.9 8.5 %collective-permute-start = (bf16[4,64,128]{2,1,0:T(8,128)(2,1)S(1)}, bf16[4,64,128]{2,1,0:T(8,128)(2,1)S(1)}, u32[]{:S(2)}, u32[]{:S(2)}) collective-permute-start(bf16[4,64,128]{2,1,0:T(8,128)(2,1)S(1)} %shard_map.141.first), channel_id=1, source_target_pairs={{0,16},{4,20},{8,24},{12,28},{16,0},{20,4},{24,8},{28,12},{1,17},{... | collective-permute-start | bytes 196616 | tf_op jit(solution)/shard_map/ppermute | solution.py:23
  16.1 5.0 %collective-permute-start.3 = (f32[4,64,128]{2,1,0:T(8,128)S(1)}, f32[4,64,128]{2,1,0:T(8,128)S(1)}, u32[]{:S(2)}, u32[]{:S(2)}) collective-permute-start(f32[4,64,128]{2,1,0:T(8,128)S(1)} %get-tuple-element.32.refs_0_), channel_id=1, source_target_pairs={{0,8},{4,12},{8,0},{12,4},{16,24},{20,28},{24,16},{28,20},{1,9},{5... | collective-permute-start | bytes 393224 | tf_op jit(solution)/shard_map/ppermute | solution.py:23
  20.4 5.6 %copy-start.2 = (f32[8,64,64]{2,1,0:T(8,128)S(1)}, f32[8,64,64]{2,1,0:T(8,128)}, u32[]{:S(2)}) copy-start(f32[8,64,64]{2,1,0:T(8,128)} %bases_far.1) | copy-start | bytes 393220
  20.4 5.0 %collective-permute-start.2 = (bf16[8,64,128]{2,1,0:T(8,128)(2,1)S(1)}, bf16[8,64,128]{2,1,0:T(8,128)(2,1)S(1)}, u32[]{:S(2)}, u32[]{:S(2)}) collective-permute-start(bf16[8,64,128]{2,1,0:T(8,128)(2,1)S(1)} %shard_map.144.refs_2_.first), channel_id=1, source_target_pairs={{0,8},{4,12},{8,0},{12,4},{16,24},{20,28},{24,16},{28,20},{1,9},{5... | collective-permute-start | bytes 393224 | tf_op jit(solution)/shard_map/ppermute | solution.py:23
  23.8 5.6 %collective-permute-start.4 = (bf16[4,64,128]{2,1,0:T(8,128)(2,1)S(1)}, bf16[4,64,128]{2,1,0:T(8,128)(2,1)S(1)}, u32[]{:S(2)}, u32[]{:S(2)}) collective-permute-start(bf16[4,64,128]{2,1,0:T(8,128)(2,1)S(1)} %get-tuple-element.42.rest_0_), channel_id=1, source_target_pairs={{0,16},{4,20},{8,24},{12,28},{16,0},{20,4},{24,8},{28,12},{1,17},{... | collective-permute-start | bytes 196616 | tf_op jit(solution)/shard_map/ppermute | solution.py:23
  25.5 6.5 %collective-permute-start.5 = (bf16[16,64,128]{2,1,0:T(8,128)(2,1)S(1)}, bf16[16,64,128]{2,1,0:T(8,128)(2,1)S(1)}, u32[]{:S(2)}, u32[]{:S(2)}) collective-permute-start(bf16[16,64,128]{2,1,0:T(8,128)(2,1)S(1)} %shard_map.146.after.rest_0_), channel_id=1, source_target_pairs={{0,4},{4,0},{8,12},{12,8},{16,20},{20,16},{24,28},{28,24},{1,5},{5... | collective-permute-start | bytes 786440 | tf_op jit(solution)/shard_map/ppermute | solution.py:23
  26.1 3.3 %copy-start.4 = (bf16[16,64,64]{2,1,0:T(8,128)(2,1)S(1)}, bf16[16,64,64]{2,1,0:T(8,128)(2,1)}, u32[]{:S(2)}) copy-start(bf16[16,64,64]{2,1,0:T(8,128)(2,1)} %couplings.1) | copy-start | bytes 393220

commit v5 on v4

--- a/solution.py
+++ b/solution.py
@@ -73,6 +73,7 @@
 
 def eliminate(work, factor, inverse):
     rank = work.shape[1] // 2
+    middle = rank // 2
     shape = (2 * GROUP, 2 * rank)
     lanes = lax.broadcasted_iota(jnp.int32, shape, 1)
     odd = lax.broadcasted_iota(jnp.int32, shape, 0) // GROUP
@@ -106,7 +107,7 @@
                 rows[b] = rows[b] - share * rows[a]
                 done[b] = done[b] - share * done[a]
         mixed = [jnp.where(inside, done[a], rows[a]) for a in range(BLOCK)]
-        for pair in range((start + BLOCK) // 2, rank // 2):
+        for pair in range((start + BLOCK) // 2, (middle if start < middle else rank) // 2):
             total = jnp.where(inside, 0.0, work[span(pair), :])
             index = side + odd + 2 * pair
             for a in range(BLOCK):
@@ -122,6 +123,23 @@
             inverse[span(pair), :] = jnp.where(
                 column <= row, jnp.where(upper, mixed[a], mixed[a + 1]) * scale, 0.0
             )
+        if start + BLOCK == middle:
+            update_second_half(work, factor, inverse)
+
+
+def update_second_half(work, factor, inverse):
+    rank = work.shape[1] // 2
+    middle = rank // 2
+    shape = (middle, 2 * rank)
+    lanes = lax.broadcasted_iota(jnp.int32, shape, 1)
+    early = lanes % rank < middle
+    for g in range(GROUP):
+        above = pl.ds(g, middle, stride=GROUP)
+        below = pl.ds(GROUP * middle + g, middle, stride=GROUP)
+        rows = jnp.where(early, inverse[above, :], factor[above, :])
+        product = dot_tn(rows, rows)
+        taken = jnp.where(lanes < rank, product[middle:rank, :], product[rank + middle :, :])
+        work[below, :] = jnp.where(early, 0.0, work[below, :]) - taken
 
 
 def matrix_pair(work, group):
@@ -156,12 +174,13 @@
 def middle_kernel(spot, mine, other, after, middle_gram, top_gram, token):
     rank = middle_gram.shape[1]
     token[...] = jnp.zeros_like(token)
-    for g in range(GROUP):
+    first = spot[1] == 0
+    for g in range(GROUP):
+        lanes = slice(g % 2 * rank, (g % 2 + 1) * rank)
+        own, sibling = mine[GROUP + g // 2][:, lanes], other[GROUP + g // 2][:, lanes]
         both = mine[g] + other[g]
         middle_gram[g] = both
-        both = jnp.where(spot[1] == 0, both, pltpu.roll(both, rank, axis=1))
-        lanes = slice(g % 2 * rank, (g % 2 + 1) * rank)
-        top_gram[g] = congruent(both, mine[GROUP + g // 2][:, lanes], other[GROUP + g // 2][:, lanes])
+        top_gram[g] = congruent(both, jnp.where(first, own, sibling), jnp.where(first, sibling, own))
 
 
 def factor_kernel(terms, has_factor, has_low, *refs):
@@ -179,24 +198,16 @@
             outs[-1][g] = both.astype(bf16)
 
 
-def half_kernel(target, couplings_far, low, halves, token, couplings, turned, table, arrived):
+def half_kernel(target, couplings, low, halves, token, turned, table):
     rank, _, count = couplings.shape
     pitch = turned.shape[0] // rank
     token[...] = jnp.zeros_like(token)
-    chunk = rank // CHUNKS
-    copies = []
-    for k in range(CHUNKS):
-        part = pl.ds(k * chunk, chunk)
-        copies.append(pltpu.make_async_copy(couplings_far.at[part], couplings.at[part], arrived.at[k]))
-        copies[k].start()
     for g in range(GROUP):
         both = low[g]
         table[g] = both[:, :rank]
         table[g + GROUP] = both[:, rank:]
-    for k in range(CHUNKS):
-        copies[k].wait()
-        for m in range(k * chunk, (k + 1) * chunk):
-            turned[m * pitch : m * pitch + count, :] = couplings[m].astype(f32).T
+    for m in range(rank):
+        turned[m * pitch : m * pitch + count, :] = couplings[m].astype(f32).T
     for r in range(count):
         block = turned[pl.ds(r, rank, stride=pitch), :].astype(bf16)
         halves[r] = low_nn(table[target[r]], block).astype(bf16)
@@ -204,7 +215,7 @@
 
 def output_kernel(
     spot,
-    bases_far,
+    bases,
     after,
     leaf_factor,
     leaf_inverse,
@@ -217,71 +228,80 @@
     leaf_transfers,
     top_transfers,
     token,
-    bases,
-    arrived,
 ):
-    share, _, rank = bases.shape
+    rank = bases.shape[2]
+    share = leaf_bases.shape[0]
     token[...] = jnp.zeros_like(token)
-    copy = pltpu.make_async_copy(bases_far.at[pl.ds(spot[0] * share, share)], bases, arrived)
-    copy.start()
-    for g in range(GROUP):
-        for place, lanes in ((g, slice(0, rank)), (g + GROUP, slice(rank, 2 * rank))):
+    for n, lanes in enumerate((slice(0, rank), slice(rank, 2 * rank))):
+        for g in range(GROUP):
+            place = n * GROUP + g
             piece = dot_nn(leaf_factor[g][:, lanes], leaf_transfer[place])
             leaf_transfers[place] = dot_nt(piece, middle_inverse[g][:, lanes])
-        both = middle_factor[g]
-        piece = dot_nn(jnp.where(spot[1] == 0, both[:, :rank], both[:, rank:]), top_transfer[g])
-        top_transfers[g] = dot_nt(piece, top_inverse[g][:, :rank])
-    copy.wait()
+    for g in range(GROUP):
+        left, right = (jnp.where(spot[1] == 0, both[:, :rank], both[:, rank:]) for both in (middle_factor[g], top_inverse[g]))
+        top_transfers[g] = dot_nt(dot_nn(left, top_transfer[g]), right)
     for k in range(share):
         place = spot[0] * share + k
         both = leaf_inverse[place % GROUP]
         both = jnp.where(place < GROUP, both[:, :rank], both[:, rank:])
-        leaf_bases[k] = dot_nt(bases[k], both)
-
-
-def unpack(packed, table, base):
+        leaf_bases[k] = dot_nt(bases[place], both)
+
+
+def shares(count, steps):
+    edges = [count * k // steps for k in range(steps + 1)]
+    return [range(low, high) for low, high in zip(edges[:-1], edges[1:])]
+
+
+def unpack(packed, table, base, turn):
     count, rank = packed.shape[0], table.shape[2]
 
     def step(n, carry):
         both = packed[n]
         place = base + 2 * GROUP * (n // GROUP) + n % GROUP
-        table[place] = both[:, :rank]
-        table[place + GROUP] = both[:, rank:]
+        if turn:
+            both = both.T
+            table[place] = both[:rank]
+            table[place + GROUP] = both[rank:]
+        else:
+            table[place] = both[:, :rank]
+            table[place + GROUP] = both[:, rank:]
         return carry
 
     lax.fori_loop(0, count, step, 0, unroll=min(count, 16))
 
 
-def unpack_all(packed, table):
+def unpack_all(packed, table, turn):
     base = 0
     for one in packed:
-        unpack(one, table, base)
+        unpack(one, table, base, turn)
         base += 2 * one.shape[0]
 
 
-def full_kernel(source, halves, token, *rest):
+def full_kernel(ready, source, halves, *rest):
+    near, rest = rest[:ready], rest[ready:]
+    far, rest = rest[-5 - ready : -5], rest[: -5 - ready] + rest[-5:]
     packed, (out_far, out, turned, table, left) = rest[:-5], rest[-5:]
     count, rank, _ = halves.shape
     pitch = turned.shape[0] // rank
-    unpack_all(packed, table)
+    copies = [pltpu.make_async_copy(near[n], far[n], left.at[n]) for n in range(ready)]
+    for copy in copies:
+        copy.start()
+    unpack_all(packed, table, True)
     for r in range(count):
-        turned[pl.ds(r, rank, stride=pitch), :] = low_nt(halves[r], table[source[r]])
-    chunk = rank // CHUNKS
-    copies = []
-    for k in range(CHUNKS):
-        for m in range(k * chunk, (k + 1) * chunk):
+        turned[pl.ds(r, rank, stride=pitch), :] = low_nn(halves[r], table[source[r]])
+    for k, part in enumerate(shares(rank, CHUNKS)):
+        for m in part:
             out[m] = turned[m * pitch : m * pitch + count, :].T.astype(bf16)
-        part = pl.ds(k * chunk, chunk)
-        copies.append(pltpu.make_async_copy(out.at[part], out_far.at[part], left.at[k]))
-        copies[k].start()
+        place = pl.ds(part.start, len(part))
+        copies.append(pltpu.make_async_copy(out.at[place], out_far.at[place], left.at[ready + k]))
+        copies[-1].start()
     for copy in copies:
         copy.wait()
 
 
 def top_project_kernel(target, source, couplings, after, *rest):
-    packed, (out, token, table) = rest[:-3], rest[-3:]
-    token[...] = jnp.zeros_like(token)
-    unpack_all(packed, table)
+    packed, (out, table) = rest[:-2], rest[-2:]
+    unpack_all(packed, table, False)
     for r in range(couplings.shape[0]):
         half = low_nn(table[target[r]], couplings[r]).astype(bf16)
         out[r] = low_nt(half, table[source[r]]).astype(bf16)
@@ -330,11 +350,7 @@
     turned = pltpu.VMEM((rank * (blocks + PITCH_EXTRA), rank), f32)
 
     source = place_of(coupling_dest[:, 0] ^ leaf_place, leaf_bits) * leaves + coupling_local
-    top_left = top_target ^ (GROUP * parity)
-    top_right = place_of((top_source // leaves) ^ (leaf_place // 4), quad_bits) * leaves + (
-        (top_source % leaves) ^ (GROUP * parity)
-    )
-
+    top_right = place_of((top_source // leaves) ^ (leaf_place // 4), quad_bits) * leaves + top_source % leaves
     note = ((8, 2 * rank), f32)
     dma = pltpu.SemaphoreType.DMA
 
@@ -348,7 +364,7 @@
             scratch=work,
         )
 
-    (gram,) = call(gram_kernel, [(packed, f32)], 0.6, arrays=[bases])
+    (gram,) = call(gram_kernel, [(packed, f32)], 1.0, arrays=[bases])
     message, token = call(
         child_kernel,
         [((GROUP + GROUP // 2, *packed[1:]), f32), note],
@@ -362,9 +378,8 @@
         [((blocks, *square), bf16), note],
         2.7,
         scalars=[coupling_target],
-        far=[jnp.transpose(couplings, (1, 2, 0))],
-        arrays=[low],
-        scratch=[pltpu.VMEM((rank, rank, blocks), bf16), turned, pltpu.VMEM((leaves, *square), bf16), dma((CHUNKS,))],
+        arrays=[jnp.transpose(couplings, (1, 2, 0)), low],
+        scratch=[turned, pltpu.VMEM((leaves, *square), bf16)],
     )
     middle_gram, top_gram, token = call(
         middle_kernel,
@@ -386,8 +401,8 @@
         [((share, *square), f32), ((leaves, *square), f32), ((GROUP, *square), f32), note],
         2.4,
         scalars=[spot],
-        far=[bases],
         arrays=[
+            bases,
             table,
             leaf_factor,
             leaf_inverse,
@@ -397,29 +412,29 @@
             top_transfer,
             top_inverse,
         ],
-        scratch=[pltpu.VMEM((share, *square), f32), dma],
-    )
-    new_top_couplings, token = call(
+    )
+    (new_top_couplings,) = call(
         top_project_kernel,
-        [((top_blocks, *square), bf16), note],
+        [((top_blocks, *square), bf16)],
         1.5,
-        scalars=[top_left, top_right],
+        scalars=[top_target, top_right],
         arrays=[top_couplings, token, *top_tables],
         scratch=[pltpu.VMEM((2 * sum(one.shape[0] for one in top_tables), *square), bf16)],
     )
-    (new_couplings,) = call(
-        full_kernel,
-        [((rank, rank, blocks), bf16)],
+    ready = [leaf_bases, leaf_transfers, top_transfers, new_top_couplings]
+    leaf_bases, leaf_transfers, top_transfers, new_top_couplings, new_couplings = call(
+        functools.partial(full_kernel, len(ready)),
+        [(one.shape, one.dtype) for one in ready] + [((rank, rank, blocks), bf16)],
         3.5,
         scalars=[source],
-        arrays=[halves, token, *tables],
+        arrays=[halves, *ready, *tables],
         scratch=[
             pltpu.VMEM((rank, rank, blocks), bf16),
             turned,
             pltpu.VMEM((2 * sum(one.shape[0] for one in tables), *square), bf16),
-            dma((CHUNKS,)),
+            dma((len(ready) + CHUNKS,)),
         ],
-        far_outs=1,
+        far_outs=len(ready) + 1,
     )
     new_couplings = jnp.transpose(new_couplings, (2, 0, 1))
     return (leaf_bases, leaf_transfers, top_transfers, new_couplings, new_top_couplings)

time: 35.7 us -> 33.9 us (0.950)
  Pallas kernels: 22.7 us -> 19 us
  waiting for transfers between devices: 0.59 us -> 2.47 us
    pallas_call x13, Pallas kernels: 22.7 us -> 19 us  [call(): pl.pallas_call(kernel, out_shape=[jax.ShapeDtypeStruct(shape, dtype) for...]
    ppermute x6, waiting for transfers between devices: 0.59 us -> 2.47 us  [swapped(): return lax.ppermute(value, axis, pairs)]
  transfers between devices with their start and end apart: 6 -> 6, of which waited for: 2 -> 4; matrix products, arithmetic and copies ran while one was open for 0% -> 0% of each run, Pallas kernels for 51% -> 43%
where the time goes in v5:
time: 33.9 us; the launch traced here: 33.7 us
  Pallas kernels  19 us (56%)
  starting transfers between devices  9.84 us (29%)
  waiting for transfers between devices  2.47 us (7%)
  local copies, waits for them, and re-layouts  1.49 us (4%)
  between operations  0.77 us (2%)
    pallas_call x13, Pallas kernels, call(): pl.pallas_call(kernel, out_shape=[jax.ShapeDtypeStruct(shape, dtype) for...  19 us
    ppermute x6, starting transfers between devices, swapped(): return lax.ppermute(value, axis, pairs)  9.84 us
    ppermute x6, waiting for transfers between devices, swapped(): return lax.ppermute(value, axis, pairs)  2.47 us
    unnamed x22, local copies, waits for them, and re-layouts  1.49 us
  transfers between devices with their start and end apart: 6, of which 4 were waited for; matrix products, arithmetic and copies ran while one was open for 0% of the time, Pallas kernels for 43%

profile of v5, /device:TPU:0, one launch (start us, length us, event | category | flops | bytes accessed | tf_op | source)
XLA Modules:
  0.0 33.7 jit_solution(12108240321988489217)
XLA Ops:
  0.6 0.0 copy-start.1
  0.6 0.9 %copy-done.1 = f32[8,64,64]{2,1,0:T(8,128)S(1)} copy-done((f32[8,64,64]{2,1,0:T(8,128)S(1)}, f32[8,64,64]{2,1,0:T(8,128)}, u32[]{:S(2)}) %copy-start.1) | copy-done | bytes 131096
  1.6 0.5 %shard_map.137.gram.refs_0_ = f32[4,64,128]{2,1,0:T(8,128)S(1)} custom-call(f32[8,64,64]{2,1,0:T(8,128)S(1)} %copy-done.1), custom_call_target="tpu_custom_call" | custom-call | flops 1000000000 | tf_op jit(solution)/shard_map/pallas_call | solution.py:316
  2.1 0.5 %copy-done.3 = f32[8,64,64]{2,1,0:T(8,128)S(1)} copy-done((f32[8,64,64]{2,1,0:T(8,128)S(1)}, f32[8,64,64]{2,1,0:T(8,128)}, u32[]{:S(2)}) %copy-start.3) | copy-done | bytes 131096
  2.5 0.0 copy-done.5
  2.6 0.8 %shard_map.138 = (f32[6,64,128]{2,1,0:T(8,128)S(1)}, f32[8,128]{1,0:T(8,128)S(1)}) custom-call(f32[4,64,128]{2,1,0:T(8,128)S(1)} %shard_map.137.gram.refs_0_, f32[8,64,64]{2,1,0:T(8,128)S(1)} %copy-done.3, f32[4,64,64]{2,1,0:T(8,128)S(1)} %copy-done.5), custom_call_target="tpu_custom_call" | custom-call | flops 800000000 | tf_op jit(solution)/shard_map/pallas_call | solution.py:316
  3.4 3.0 %collective-permute-start.1 = (f32[6,64,128]{2,1,0:T(8,128)S(1)}, f32[6,64,128]{2,1,0:T(8,128)S(1)}, u32[]{:S(2)}, u32[]{:S(2)}) collective-permute-start(f32[6,64,128]{2,1,0:T(8,128)S(1)} %get-tuple-element.32.mine), channel_id=1, source_target_pairs={{0,4},{4,0},{8,12},{12,8},{16,20},{20,16},{24,28},{28,24},{1,5},{5... | collective-permute-start | bytes 589832 | tf_op jit(solution)/shard_map/ppermute | solution.py:23
  6.4 2.3 %shard_map.139 = (f32[4,64,128]{2,1,0:T(8,128)S(1)}, f32[4,64,128]{2,1,0:T(8,128)S(1)}, bf16[4,64,128]{2,1,0:T(8,128)(2,1)S(1)}) custom-call(f32[4,64,128]{2,1,0:T(8,128)S(1)} %shard_map.137.gram.refs_0_, f32[8,128]{1,0:T(8,128)S(1)} %get-tuple-element.28.refs_1_), custom_call_target="tpu_custom_call" | custom-call | flops 2600000000 | tf_op jit(solution)/shard_map/pallas_call | solution.py:316
  8.7 0.0 copy-done
  8.7 0.0 copy-start.8
  8.7 0.0 copy-start.9
  8.8 0.0 copy-start.10
  8.8 2.1 %shard_map.140 = (bf16[128,64,64]{2,1,0:T(8,128)(2,1)S(1)}, f32[8,128]{1,0:T(8,128)S(1)}) custom-call(s32[128]{0:T(128)S(1)} %copy-done.6, bf16[64,64,128]{2,1,0:T(8,128)(2,1)S(1)} %bitcast.6, bf16[4,64,128]{2,1,0:T(8,128)(2,1)S(1)} %get-tuple-element.29.low.value), custom_call_target="tpu_custom_call" | custom-call | flops 2700000000 | tf_op jit(solution)/shard_map/pallas_call | solution.py:316
  10.9 2.7 %collective-permute-start = (bf16[4,64,128]{2,1,0:T(8,128)(2,1)S(1)}, bf16[4,64,128]{2,1,0:T(8,128)(2,1)S(1)}, u32[]{:S(2)}, u32[]{:S(2)}) collective-permute-start(bf16[4,64,128]{2,1,0:T(8,128)(2,1)S(1)} %shard_map.141.first), channel_id=1, source_target_pairs={{0,16},{4,20},{8,24},{12,28},{16,0},{20,4},{24,8},{28,12},{1,17},{... | collective-permute-start | bytes 196616 | tf_op jit(solution)/shard_map/ppermute | solution.py:23
  13.6 0.1 pad_add_fusion.spot
  13.7 0.0 collective-permute-done.1.other
  13.7 1.3 %shard_map.142 = (f32[4,64,128]{2,1,0:T(8,128)S(1)}, f32[4,64,128]{2,1,0:T(8,128)S(1)}, f32[8,128]{1,0:T(8,128)S(1)}) custom-call(s32[2]{0:T(128)S(1)} %pad_add_fusion.spot, f32[6,64,128]{2,1,0:T(8,128)S(1)} %get-tuple-element.32.mine, f32[6,64,128]{2,1,0:T(8,128)S(1)} %collective-permute-done.1.other, f32[8,128]{1,0:T(8,128)S(1)} %get-tuple-element.31.after), custom_call_target="tpu_custom_call" | custom-call | flops 1400000000 | tf_op jit(solution)/shard_map/pallas_call | solution.py:316
  15.0 1.6 %collective-permute-start.3 = (f32[4,64,128]{2,1,0:T(8,128)S(1)}, f32[4,64,128]{2,1,0:T(8,128)S(1)}, u32[]{:S(2)}, u32[]{:S(2)}) collective-permute-start(f32[4,64,128]{2,1,0:T(8,128)S(1)} %get-tuple-element.36.refs_0_), channel_id=1, source_target_pairs={{0,8},{4,12},{8,0},{12,4},{16,24},{20,28},{24,16},{28,20},{1,9},{5... | collective-permute-start | bytes 393224 | tf_op jit(solution)/shard_map/ppermute | solution.py:23
  16.6 2.3 %shard_map.143 = (f32[4,64,128]{2,1,0:T(8,128)S(1)}, f32[4,64,128]{2,1,0:T(8,128)S(1)}) custom-call(f32[4,64,128]{2,1,0:T(8,128)S(1)} %get-tuple-element.33.refs_0_, f32[8,128]{1,0:T(8,128)S(1)} %get-tuple-element.34.refs_1_), custom_call_target="tpu_custom_call" | custom-call | flops 2600000000 | tf_op jit(solution)/shard_map/pallas_call | solution.py:316
  18.9 0.0 collective-permute-done.second
  18.9 0.0 copy-start.2
  19.0 0.5 %collective-permute-start.2 = (bf16[8,64,128]{2,1,0:T(8,128)(2,1)S(1)}, bf16[8,64,128]{2,1,0:T(8,128)(2,1)S(1)}, u32[]{:S(2)}, u32[]{:S(2)}) collective-permute-start(bf16[8,64,128]{2,1,0:T(8,128)(2,1)S(1)} %shard_map.144.refs_2_.first), channel_id=1, source_target_pairs={{0,8},{4,12},{8,0},{12,4},{16,24},{20,28},{24,16},{28,20},{1,9},{5... | collective-permute-start | bytes 393224 | tf_op jit(solution)/shard_map/ppermute | solution.py:23
  19.5 0.6 %collective-permute-done.3.refs_1_ = f32[4,64,128]{2,1,0:T(8,128)S(1)} collective-permute-done((f32[4,64,128]{2,1,0:T(8,128)S(1)}, f32[4,64,128]{2,1,0:T(8,128)S(1)}, u32[]{:S(2)}, u32[]{:S(2)}) %collective-permute-start.3) | collective-permute-done | bytes 131104 | tf_op jit(solution)/shard_map/ppermute | solution.py:23
  20.0 2.3 %shard_map.145 = (f32[4,64,128]{2,1,0:T(8,128)S(1)}, bf16[4,64,128]{2,1,0:T(8,128)(2,1)S(1)}) custom-call(f32[4,64,128]{2,1,0:T(8,128)S(1)} %get-tuple-element.36.refs_0_, f32[4,64,128]{2,1,0:T(8,128)S(1)} %collective-permute-done.3.refs_1_, bf16[8,64,128]{2,1,0:T(8,128)(2,1)S(1)} %shard_map.144.refs_2_.first), custom_call_target="tpu_custom_call" | custom-call | flops 2600000000 | tf_op jit(solution)/shard_map/pallas_call | solution.py:316
  22.3 1.3 %collective-permute-start.4 = (bf16[4,64,128]{2,1,0:T(8,128)(2,1)S(1)}, bf16[4,64,128]{2,1,0:T(8,128)(2,1)S(1)}, u32[]{:S(2)}, u32[]{:S(2)}) collective-permute-start(bf16[4,64,128]{2,1,0:T(8,128)(2,1)S(1)} %get-tuple-element.45.rest_0_), channel_id=1, source_target_pairs={{0,16},{4,20},{8,24},{12,28},{16,0},{20,4},{24,8},{28,12},{1,17},{... | collective-permute-start | bytes 196616 | tf_op jit(solution)/shard_map/ppermute | solution.py:23
  23.7 0.3 collective-permute-done.2.second
  24.0 0.7 %collective-permute-start.5 = (bf16[16,64,128]{2,1,0:T(8,128)(2,1)S(1)}, bf16[16,64,128]{2,1,0:T(8,128)(2,1)S(1)}, u32[]{:S(2)}, u32[]{:S(2)}) collective-permute-start(bf16[16,64,128]{2,1,0:T(8,128)(2,1)S(1)} %shard_map.146.after.rest_4_), channel_id=1, source_target_pairs={{0,4},{4,0},{8,12},{12,8},{16,20},{20,16},{24,28},{28,24},{1,5},{5... | collective-permute-start | bytes 786440 | tf_op jit(solution)/shard_map/ppermute | solution.py:23
  24.7 2.3 %shard_map.147 = (f32[2,64,64]{2,1,0:T(8,128)S(1)}, f32[8,64,64]{2,1,0:T(8,128)S(1)}, f32[4,64,64]{2,1,0:T(8,128)S(1)}, f32[8,128]{1,0:T(8,128)S(1)}) custom-call(s32[2]{0:T(128)S(1)} %pad_add_fusion.spot, f32[8,64,64]{2,1,0:T(8,128)S(1)} %copy-done.2, bf16[16,64,128]{2,1,0:T(8,128)(2,1)S(1)} %shard_map.146.after.rest_4_, ...), custom_call_target="tpu_custom_call" | custom-call | flops 2400000000 | tf_op jit(solution)/shard_map/pallas_call | solution.py:316
  27.0 0.6 %collective-permute-done.4.rest_1_ = bf16[4,64,128]{2,1,0:T(8,128)(2,1)S(1)} collective-permute-done((bf16[4,64,128]{2,1,0:T(8,128)(2,1)S(1)}, bf16[4,64,128]{2,1,0:T(8,128)(2,1)S(1)}, u32[]{:S(2)}, u32[]{:S(2)}) %collective-permute-start.4) | collective-permute-done | bytes 65568 | tf_op jit(solution)/shard_map/ppermute | solution.py:23
  27.6 1.8 %shard_map.148.rest_3_ = bf16[16,64,64]{2,1,0:T(8,128)(2,1)S(1)} custom-call(s32[16]{0:T(128)S(1)} %copy-done.7, s32[16]{0:T(128)S(1)} %fusion.source, bf16[16,64,64]{2,1,0:T(8,128)(2,1)S(1)} %copy-done.4, f32[8,128]{1,0:T(8,128)S(1)} %get-tuple-element.44.after, bf16[4,64,128]{2,1,0:T(8,128)(2,1)S(1)} %get-tuple-element.45.rest_0_, ...), custom_call_target="tpu_custom_call" | custom-call | flops 1500000000 | tf_op jit(solution)/shard_map/pallas_call | solution.py:316
  29.4 1.0 %collective-permute-done.5.rest_5_ = bf16[16,64,128]{2,1,0:T(8,128)(2,1)S(1)} collective-permute-done((bf16[16,64,128]{2,1,0:T(8,128)(2,1)S(1)}, bf16[16,64,128]{2,1,0:T(8,128)(2,1)S(1)}, u32[]{:S(2)}, u32[]{:S(2)}) %collective-permute-start.5) | collective-permute-done | bytes 262176 | tf_op jit(solution)/shard_map/ppermute | solution.py:23
  30.4 3.3 %shard_map.149 = (f32[2,64,64]{2,1,0:T(8,128)}, f32[8,64,64]{2,1,0:T(8,128)}, f32[4,64,64]{2,1,0:T(8,128)}, bf16[16,64,64]{2,1,0:T(8,128)(2,1)}, bf16[64,64,128]{2,1,0:T(8,128)(2,1)}) custom-call(s32[128]{0:T(128)S(1)} %bitcast_add_fusion.source, bf16[128,64,64]{2,1,0:T(8,128)(2,1)S(1)} %get-tuple-element.30.halves, ...), custom_call_target="tpu_custom_call" | custom-call | flops 3500000000 | tf_op jit(solution)/shard_map/pallas_call | solution.py:316
  (18 shorter events, 0.1 us)
Async XLA Ops:
  0.6 1.0 %copy-start.1 = (f32[8,64,64]{2,1,0:T(8,128)S(1)}, f32[8,64,64]{2,1,0:T(8,128)}, u32[]{:S(2)}) copy-start(f32[8,64,64]{2,1,0:T(8,128)} %bases.3) | copy-start | bytes 393220
  1.6 0.9 %copy-start.3 = (f32[8,64,64]{2,1,0:T(8,128)S(1)}, f32[8,64,64]{2,1,0:T(8,128)}, u32[]{:S(2)}) copy-start(f32[8,64,64]{2,1,0:T(8,128)} %leaf_transfer.1) | copy-start | bytes 393220
  1.6 1.0 %copy-start.5 = (f32[4,64,64]{2,1,0:T(8,128)S(1)}, f32[4,64,64]{2,1,0:T(8,128)}, u32[]{:S(2)}) copy-start(f32[4,64,64]{2,1,0:T(8,128)} %top_transfer.1) | copy-start | bytes 196612
  3.4 10.3 %collective-permute-start.1 = (f32[6,64,128]{2,1,0:T(8,128)S(1)}, f32[6,64,128]{2,1,0:T(8,128)S(1)}, u32[]{:S(2)}, u32[]{:S(2)}) collective-permute-start(f32[6,64,128]{2,1,0:T(8,128)S(1)} %get-tuple-element.32.mine), channel_id=1, source_target_pairs={{0,4},{4,0},{8,12},{12,8},{16,20},{20,16},{24,28},{28,24},{1,5},{5... | collective-permute-start | bytes 589832 | tf_op jit(solution)/shard_map/ppermute | solution.py:23
  6.4 2.3 %copy-start = (bf16[128,64,64]{0,2,1:T(8,128)(2,1)S(1)}, bf16[128,64,64]{0,2,1:T(8,128)(2,1)}, u32[]{:S(2)}) copy-start(bf16[128,64,64]{0,2,1:T(8,128)(2,1)} %param.13) | copy-start | bytes 3145732
  6.4 2.3 %copy-start.6 = (s32[128]{0:T(128)S(1)}, s32[128]{0:T(128)}, u32[]{:S(2)}) copy-start(s32[128]{0:T(128)} %target.2) | copy-start | bytes 1540
  8.7 4.9 %copy-start.8 = (s32[128]{0:T(128)S(1)}, s32[128]{0:T(128)}, u32[]{:S(2)}) copy-start(s32[128]{0:T(128)} %param.16) | copy-start | bytes 1540
  8.7 4.9 %copy-start.9 = (s32[128,1]{0,1:T(1,128)S(1)}, s32[128,1]{0,1:T(1,128)}, u32[]{:S(2)}) copy-start(s32[128,1]{0,1:T(1,128)} %param.15) | copy-start | bytes 1540
  8.8 4.9 %copy-start.10 = (s32[16]{0:T(128)S(1)}, s32[16]{0:T(128)}, u32[]{:S(2)}) copy-start(s32[16]{0:T(128)} %param.19) | copy-start | bytes 196
  10.9 8.0 %collective-permute-start = (bf16[4,64,128]{2,1,0:T(8,128)(2,1)S(1)}, bf16[4,64,128]{2,1,0:T(8,128)(2,1)S(1)}, u32[]{:S(2)}, u32[]{:S(2)}) collective-permute-start(bf16[4,64,128]{2,1,0:T(8,128)(2,1)S(1)} %shard_map.141.first), channel_id=1, source_target_pairs={{0,16},{4,20},{8,24},{12,28},{16,0},{20,4},{24,8},{28,12},{1,17},{... | collective-permute-start | bytes 196616 | tf_op jit(solution)/shard_map/ppermute | solution.py:23
  15.0 5.0 %collective-permute-start.3 = (f32[4,64,128]{2,1,0:T(8,128)S(1)}, f32[4,64,128]{2,1,0:T(8,128)S(1)}, u32[]{:S(2)}, u32[]{:S(2)}) collective-permute-start(f32[4,64,128]{2,1,0:T(8,128)S(1)} %get-tuple-element.36.refs_0_), channel_id=1, source_target_pairs={{0,8},{4,12},{8,0},{12,4},{16,24},{20,28},{24,16},{28,20},{1,9},{5... | collective-permute-start | bytes 393224 | tf_op jit(solution)/shard_map/ppermute | solution.py:23
  18.9 5.7 %copy-start.2 = (f32[8,64,64]{2,1,0:T(8,128)S(1)}, f32[8,64,64]{2,1,0:T(8,128)}, u32[]{:S(2)}) copy-start(f32[8,64,64]{2,1,0:T(8,128)} %bases.3) | copy-start | bytes 393220
  19.0 5.0 %collective-permute-start.2 = (bf16[8,64,128]{2,1,0:T(8,128)(2,1)S(1)}, bf16[8,64,128]{2,1,0:T(8,128)(2,1)S(1)}, u32[]{:S(2)}, u32[]{:S(2)}) collective-permute-start(bf16[8,64,128]{2,1,0:T(8,128)(2,1)S(1)} %shard_map.144.refs_2_.first), channel_id=1, source_target_pairs={{0,8},{4,12},{8,0},{12,4},{16,24},{20,28},{24,16},{28,20},{1,9},{5... | collective-permute-start | bytes 393224 | tf_op jit(solution)/shard_map/ppermute | solution.py:23
  22.3 5.2 %collective-permute-start.4 = (bf16[4,64,128]{2,1,0:T(8,128)(2,1)S(1)}, bf16[4,64,128]{2,1,0:T(8,128)(2,1)S(1)}, u32[]{:S(2)}, u32[]{:S(2)}) collective-permute-start(bf16[4,64,128]{2,1,0:T(8,128)(2,1)S(1)} %get-tuple-element.45.rest_0_), channel_id=1, source_target_pairs={{0,16},{4,20},{8,24},{12,28},{16,0},{20,4},{24,8},{28,12},{1,17},{... | collective-permute-start | bytes 196616 | tf_op jit(solution)/shard_map/ppermute | solution.py:23
  24.0 6.4 %collective-permute-start.5 = (bf16[16,64,128]{2,1,0:T(8,128)(2,1)S(1)}, bf16[16,64,128]{2,1,0:T(8,128)(2,1)S(1)}, u32[]{:S(2)}, u32[]{:S(2)}) collective-permute-start(bf16[16,64,128]{2,1,0:T(8,128)(2,1)S(1)} %shard_map.146.after.rest_4_), channel_id=1, source_target_pairs={{0,4},{4,0},{8,12},{12,8},{16,20},{20,16},{24,28},{28,24},{1,5},{5... | collective-permute-start | bytes 786440 | tf_op jit(solution)/shard_map/ppermute | solution.py:23
  24.7 2.9 %copy-start.4 = (bf16[16,64,64]{2,1,0:T(8,128)(2,1)S(1)}, bf16[16,64,64]{2,1,0:T(8,128)(2,1)}, u32[]{:S(2)}) copy-start(bf16[16,64,64]{2,1,0:T(8,128)(2,1)} %couplings.1) | copy-start | bytes 393220
  24.7 2.9 %copy-start.7 = (s32[16]{0:T(128)S(1)}, s32[16]{0:T(128)}, u32[]{:S(2)}) copy-start(s32[16]{0:T(128)} %target.3) | copy-start | bytes 196

commit v6 on v5

--- a/solution.py
+++ b/solution.py
@@ -150,6 +150,34 @@
     return jnp.concatenate([left, right], axis=1)
 
 
+def pack_upper(pairs, out):
+    rank = pairs[0].shape[0]
+    half = rank // 2
+    right = lax.broadcasted_iota(jnp.int32, (half, 2 * rank), 1) % rank >= half
+    for n in range(GROUP // 2):
+        first, second = pairs[2 * n], pairs[2 * n + 1]
+        start = 3 * half * n
+        out[start : start + half, :] = first[:half].astype(out.dtype)
+        out[start + half : start + 2 * half, :] = second[:half].astype(out.dtype)
+        turned = pltpu.roll(second[half:], 2 * rank - half, axis=1)
+        out[start + 2 * half : start + 3 * half, :] = jnp.where(right, first[half:], turned).astype(out.dtype)
+
+
+def unpack_upper(message):
+    rank = message.shape[-1] // 2
+    half = rank // 2
+    right = lax.broadcasted_iota(jnp.int32, (half, 2 * rank), 1) % rank >= half
+    pairs = []
+    for n in range(GROUP // 2):
+        start = 3 * half * n
+        shared = message[start + 2 * half : start + 3 * half, :].astype(f32)
+        for k, lower in enumerate((shared, pltpu.roll(shared, half, axis=1))):
+            upper = message[start + k * half : start + (k + 1) * half, :]
+            lower = jnp.where(right, lower, 0.0).astype(upper.dtype)
+            pairs.append(jnp.concatenate([upper, lower], axis=0))
+    return pairs
+
+
 def gram_kernel(bases, gram):
     for g in range(GROUP):
         left, right = bases[g], bases[g + GROUP]
@@ -171,31 +199,35 @@
         message[GROUP + n] = side_by_side(top[2 * n], top[2 * n + 1])
 
 
-def middle_kernel(spot, mine, other, after, middle_gram, top_gram, token):
+def middle_kernel(spot, mine, other, after, middle_gram, top_gram, message, token):
     rank = middle_gram.shape[1]
     token[...] = jnp.zeros_like(token)
     first = spot[1] == 0
+    grams = []
     for g in range(GROUP):
         lanes = slice(g % 2 * rank, (g % 2 + 1) * rank)
         own, sibling = mine[GROUP + g // 2][:, lanes], other[GROUP + g // 2][:, lanes]
         both = mine[g] + other[g]
         middle_gram[g] = both
-        top_gram[g] = congruent(both, jnp.where(first, own, sibling), jnp.where(first, sibling, own))
+        grams.append(congruent(both, jnp.where(first, own, sibling), jnp.where(first, sibling, own)))
+        top_gram[g] = grams[g]
+    pack_upper(grams, message)
 
 
 def factor_kernel(terms, has_factor, has_low, *refs):
     grams, refs = refs[:terms], refs[terms + 1 :]
     outs, (work, factor, inverse) = refs[:-3], refs[-3:]
-    for g in range(GROUP):
-        work[matrix_pair(work, g), :] = grams[0][g] if terms == 1 else grams[0][g] + grams[1][g]
+    more = unpack_upper(grams[1]) if terms == 2 else None
+    for g in range(GROUP):
+        work[matrix_pair(work, g), :] = grams[0][g] if more is None else grams[0][g] + more[g]
     eliminate(work, factor, inverse)
-    for g in range(GROUP):
-        both = factor[matrix_pair(work, g), :]
+    pairs = [factor[matrix_pair(work, g), :] for g in range(GROUP)]
+    if has_low:
+        pack_upper(pairs, outs[-1].at[0])
+    for g in range(GROUP):
         outs[0][g] = inverse[matrix_pair(work, g), :]
         if has_factor:
-            outs[1][g] = both
-        if has_low:
-            outs[-1][g] = both.astype(bf16)
+            outs[1][g] = pairs[g]
 
 
 def half_kernel(target, couplings, low, halves, token, turned, table):
@@ -203,7 +235,7 @@
     pitch = turned.shape[0] // rank
     token[...] = jnp.zeros_like(token)
     for g in range(GROUP):
-        both = low[g]
+        both = low[g].astype(bf16)
         table[g] = both[:, :rank]
         table[g + GROUP] = both[:, rank:]
     for m in range(rank):
@@ -215,8 +247,11 @@
 
 def output_kernel(
     spot,
+    target,
     bases,
     after,
+    top_couplings,
+    top_low,
     leaf_factor,
     leaf_inverse,
     leaf_transfer,
@@ -227,11 +262,14 @@
     leaf_bases,
     leaf_transfers,
     top_transfers,
-    token,
+    top_halves,
+    table,
 ):
     rank = bases.shape[2]
     share = leaf_bases.shape[0]
-    token[...] = jnp.zeros_like(token)
+    unpack(top_low, table, 0, False)
+    for r in range(top_couplings.shape[0]):
+        top_halves[r] = low_nn(table[target[r]], top_couplings[r]).astype(bf16)
     for n, lanes in enumerate((slice(0, rank), slice(rank, 2 * rank))):
         for g in range(GROUP):
             place = n * GROUP + g
@@ -256,25 +294,25 @@
     count, rank = packed.shape[0], table.shape[2]
 
     def step(n, carry):
-        both = packed[n]
-        place = base + 2 * GROUP * (n // GROUP) + n % GROUP
-        if turn:
-            both = both.T
-            table[place] = both[:rank]
-            table[place + GROUP] = both[rank:]
-        else:
-            table[place] = both[:, :rank]
-            table[place + GROUP] = both[:, rank:]
+        for g, both in enumerate(unpack_upper(packed.at[n])):
+            place = base + 2 * GROUP * n + g
+            if turn:
+                both = both.T
+                table[place] = both[:rank]
+                table[place + GROUP] = both[rank:]
+            else:
+                table[place] = both[:, :rank]
+                table[place + GROUP] = both[:, rank:]
         return carry
 
-    lax.fori_loop(0, count, step, 0, unroll=min(count, 16))
+    lax.fori_loop(0, count, step, 0, unroll=min(count, 4))
 
 
 def unpack_all(packed, table, turn):
     base = 0
     for one in packed:
         unpack(one, table, base, turn)
-        base += 2 * one.shape[0]
+        base += 2 * GROUP * one.shape[0]
 
 
 def full_kernel(ready, source, halves, *rest):
@@ -299,12 +337,11 @@
         copy.wait()
 
 
-def top_project_kernel(target, source, couplings, after, *rest):
+def top_project_kernel(source, halves, *rest):
     packed, (out, table) = rest[:-2], rest[-2:]
     unpack_all(packed, table, False)
-    for r in range(couplings.shape[0]):
-        half = low_nn(table[target[r]], couplings[r]).astype(bf16)
-        out[r] = low_nt(half, table[source[r]]).astype(bf16)
+    for r in range(halves.shape[0]):
+        out[r] = low_nt(halves[r], table[source[r]]).astype(bf16)
 
 
 vmem = pl.BlockSpec(memory_space=pltpu.VMEM)
@@ -355,10 +392,12 @@
     dma = pltpu.SemaphoreType.DMA
 
 
+    uppers = (GROUP // 2 * 3 * (rank // 2), 2 * rank)
+
     def factored(grams, after, has_factor, has_low):
         return call(
             functools.partial(factor_kernel, len(grams), has_factor, has_low),
-            [(packed, f32)] * (1 + has_factor) + [(packed, bf16)] * has_low,
+            [(packed, f32)] * (1 + has_factor) + [((1, *uppers), bf16)] * has_low,
             2.6,
             arrays=[*grams, after],
             scratch=work,
@@ -378,32 +417,34 @@
         [((blocks, *square), bf16), note],
         2.7,
         scalars=[coupling_target],
-        arrays=[jnp.transpose(couplings, (1, 2, 0)), low],
+        arrays=[jnp.transpose(couplings, (1, 2, 0)), leaf_factor],
         scratch=[turned, pltpu.VMEM((leaves, *square), bf16)],
     )
-    middle_gram, top_gram, token = call(
+    middle_gram, top_gram, top_message, token = call(
         middle_kernel,
-        [(packed, f32), (packed, f32), note],
+        [(packed, f32), (packed, f32), (uppers, f32), note],
         1.4,
         scalars=[spot],
         arrays=[message, message_other, half_token],
     )
-    top_gram_other = swapped(top_gram, "leaf", 2)
+    top_gram_other = swapped(top_message, "leaf", 2)
     middle_inverse, middle_factor = factored([middle_gram], token, True, False)
-    table = joined_by_xor(held(low, half_token), "leaf", leaf_bits[:1], middle_inverse)
+    table = joined_by_xor(held(low, half_token), "leaf", leaf_bits[:-2], middle_inverse)
+    tables = [table, swapped(table, "leaf", 1 << leaf_bits[-2])]
+    tables += [swapped(one, "leaf", 1 << leaf_bits[-1]) for one in tables]
     top_inverse, top_low = factored([top_gram, top_gram_other], table, False, True)
     top_table = joined_by_xor(top_low, "leaf", [bit + 2 for bit in quad_bits[:-1]], top_inverse)
     top_tables = [top_table, swapped(top_table, "leaf", 4 << quad_bits[-1])]
-    table = joined_by_xor(table, "leaf", leaf_bits[1:-1], top_inverse)
-    tables = [table, swapped(table, "leaf", 1 << leaf_bits[-1])]
-    leaf_bases, leaf_transfers, top_transfers, token = call(
+    leaf_bases, leaf_transfers, top_transfers, top_halves = call(
         output_kernel,
-        [((share, *square), f32), ((leaves, *square), f32), ((GROUP, *square), f32), note],
-        2.4,
-        scalars=[spot],
+        [((share, *square), f32), ((leaves, *square), f32), ((GROUP, *square), f32), ((top_blocks, *square), bf16)],
+        2.5,
+        scalars=[spot, top_target],
         arrays=[
             bases,
-            table,
+            tables[1],
+            top_couplings,
+            top_low,
             leaf_factor,
             leaf_inverse,
             leaf_transfer,
@@ -412,14 +453,15 @@
             top_transfer,
             top_inverse,
         ],
+        scratch=[pltpu.VMEM((leaves, *square), bf16)],
     )
     (new_top_couplings,) = call(
         top_project_kernel,
         [((top_blocks, *square), bf16)],
-        1.5,
-        scalars=[top_target, top_right],
-        arrays=[top_couplings, token, *top_tables],
-        scratch=[pltpu.VMEM((2 * sum(one.shape[0] for one in top_tables), *square), bf16)],
+        1.3,
+        scalars=[top_right],
+        arrays=[top_halves, *top_tables],
+        scratch=[pltpu.VMEM((leaves * sum(one.shape[0] for one in top_tables), *square), bf16)],
     )
     ready = [leaf_bases, leaf_transfers, top_transfers, new_top_couplings]
     leaf_bases, leaf_transfers, top_transfers, new_top_couplings, new_couplings = call(
@@ -431,7 +473,7 @@
         scratch=[
             pltpu.VMEM((rank, rank, blocks), bf16),
             turned,
-            pltpu.VMEM((2 * sum(one.shape[0] for one in tables), *square), bf16),
+            pltpu.VMEM((leaves * sum(one.shape[0] for one in tables), *square), bf16),
             dma((len(ready) + CHUNKS,)),
         ],
         far_outs=len(ready) + 1,

time: 33.9 us -> 32.8 us (0.968)
  waiting for transfers between devices: 2.47 us -> 0.41 us
  starting transfers between devices: 9.84 us -> 11.3 us
  Pallas kernels: 19 us -> 18.6 us
    ppermute x6 -> x7, waiting for transfers between devices: 2.47 us -> 0.41 us  [swapped(): return lax.ppermute(value, axis, pairs)]
    ppermute x6 -> x7, starting transfers between devices: 9.84 us -> 11.3 us  [swapped(): return lax.ppermute(value, axis, pairs)]
    pallas_call x13 -> x12, Pallas kernels: 19 us -> 18.6 us  [call(): pl.pallas_call(kernel, out_shape=[jax.ShapeDtypeStruct(shape, dtype) for...]
  transfers between devices with their start and end apart: 6 -> 7, of which waited for: 4 -> 1; matrix products, arithmetic and copies ran while one was open for 0% -> 0% of each run, Pallas kernels for 43% -> 43%
where the time goes in v6:
time: 32.8 us; the launch traced here: 32.6 us
  Pallas kernels  18.6 us (57%)
  starting transfers between devices  11.3 us (34%)
  local copies, waits for them, and re-layouts  1.49 us (5%)
  between operations  0.78 us (2%)
  waiting for transfers between devices  0.41 us (1%)
    pallas_call x12, Pallas kernels, call(): pl.pallas_call(kernel, out_shape=[jax.ShapeDtypeStruct(shape, dtype) for...  18.6 us
    ppermute x7, starting transfers between devices, swapped(): return lax.ppermute(value, axis, pairs)  11.3 us
    unnamed x22, local copies, waits for them, and re-layouts  1.49 us
  transfers between devices with their start and end apart: 7, of which 1 were waited for; matrix products, arithmetic and copies ran while one was open for 0% of the time, Pallas kernels for 43%

profile of v6, /device:TPU:0, one launch (start us, length us, event | category | flops | bytes accessed | tf_op | source)
XLA Modules:
  0.0 32.6 jit_solution(2487680777360558999)
XLA Ops:
  0.6 0.0 copy-start.1
  0.6 0.9 %copy-done.1 = f32[8,64,64]{2,1,0:T(8,128)S(1)} copy-done((f32[8,64,64]{2,1,0:T(8,128)S(1)}, f32[8,64,64]{2,1,0:T(8,128)}, u32[]{:S(2)}) %copy-start.1) | copy-done | bytes 131096
  1.6 0.5 %shard_map.137.gram.refs_0_ = f32[4,64,128]{2,1,0:T(8,128)S(1)} custom-call(f32[8,64,64]{2,1,0:T(8,128)S(1)} %copy-done.1), custom_call_target="tpu_custom_call" | custom-call | flops 1000000000 | tf_op jit(solution)/shard_map/pallas_call | solution.py:353
  2.1 0.5 %copy-done.3 = f32[8,64,64]{2,1,0:T(8,128)S(1)} copy-done((f32[8,64,64]{2,1,0:T(8,128)S(1)}, f32[8,64,64]{2,1,0:T(8,128)}, u32[]{:S(2)}) %copy-start.3) | copy-done | bytes 131096
  2.5 0.0 copy-done.5
  2.6 0.8 %shard_map.138 = (f32[6,64,128]{2,1,0:T(8,128)S(1)}, f32[8,128]{1,0:T(8,128)S(1)}) custom-call(f32[4,64,128]{2,1,0:T(8,128)S(1)} %shard_map.137.gram.refs_0_, f32[8,64,64]{2,1,0:T(8,128)S(1)} %copy-done.3, f32[4,64,64]{2,1,0:T(8,128)S(1)} %copy-done.5), custom_call_target="tpu_custom_call" | custom-call | flops 800000000 | tf_op jit(solution)/shard_map/pallas_call | solution.py:353
  3.4 3.0 %collective-permute-start.1 = (f32[6,64,128]{2,1,0:T(8,128)S(1)}, f32[6,64,128]{2,1,0:T(8,128)S(1)}, u32[]{:S(2)}, u32[]{:S(2)}) collective-permute-start(f32[6,64,128]{2,1,0:T(8,128)S(1)} %get-tuple-element.34.mine), channel_id=1, source_target_pairs={{0,4},{4,0},{8,12},{12,8},{16,20},{20,16},{24,28},{28,24},{1,5},{5... | collective-permute-start | bytes 589832 | tf_op jit(solution)/shard_map/ppermute | solution.py:23
  6.4 2.3 %shard_map.139 = (f32[4,64,128]{2,1,0:T(8,128)S(1)}, f32[4,64,128]{2,1,0:T(8,128)S(1)}, bf16[1,192,128]{2,1,0:T(8,128)(2,1)S(1)}) custom-call(f32[4,64,128]{2,1,0:T(8,128)S(1)} %shard_map.137.gram.refs_0_, f32[8,128]{1,0:T(8,128)S(1)} %get-tuple-element.29.refs_1_), custom_call_target="tpu_custom_call" | custom-call | flops 2600000000 | tf_op jit(solution)/shard_map/pallas_call | solution.py:353
  8.7 0.0 copy-done.6
  8.7 0.0 copy-start.8
  8.8 0.0 copy-start.9
  8.8 0.0 copy-start.10
  8.8 2.1 %shard_map.140 = (bf16[128,64,64]{2,1,0:T(8,128)(2,1)S(1)}, f32[8,128]{1,0:T(8,128)S(1)}) custom-call(s32[128]{0:T(128)S(1)} %copy-done.6, bf16[64,64,128]{2,1,0:T(8,128)(2,1)S(1)} %bitcast.6, f32[4,64,128]{2,1,0:T(8,128)S(1)} %get-tuple-element.30.low.leaf_factor), custom_call_target="tpu_custom_call" | custom-call | flops 2700000000 | tf_op jit(solution)/shard_map/pallas_call | solution.py:353
  10.9 2.7 %collective-permute-start = (bf16[1,192,128]{2,1,0:T(8,128)(2,1)S(1)}, bf16[1,192,128]{2,1,0:T(8,128)(2,1)S(1)}, u32[]{:S(2)}, u32[]{:S(2)}) collective-permute-start(bf16[1,192,128]{2,1,0:T(8,128)(2,1)S(1)} %shard_map.141.first), channel_id=1, source_target_pairs={{0,16},{4,20},{8,24},{12,28},{16,0},{20,4},{24,8},{28,12},{1,17},{... | collective-permute-start | bytes 147464 | tf_op jit(solution)/shard_map/ppermute | solution.py:23
  13.6 0.1 pad_add_fusion.spot
  13.7 0.0 collective-permute-done.1.other
  13.7 1.4 %shard_map.142 = (f32[4,64,128]{2,1,0:T(8,128)S(1)}, f32[4,64,128]{2,1,0:T(8,128)S(1)}, f32[192,128]{1,0:T(8,128)S(1)}, f32[8,128]{1,0:T(8,128)S(1)}) custom-call(s32[2]{0:T(128)S(1)} %pad_add_fusion.spot, f32[6,64,128]{2,1,0:T(8,128)S(1)} %get-tuple-element.34.mine, f32[6,64,128]{2,1,0:T(8,128)S(1)} %collective-permute-done.1.other, ...), custom_call_target="tpu_custom_call" | custom-call | flops 1400000000 | tf_op jit(solution)/shard_map/pallas_call | solution.py:353
  15.1 1.6 %collective-permute-start.3 = (f32[192,128]{1,0:T(8,128)S(1)}, f32[192,128]{1,0:T(8,128)S(1)}, u32[]{:S(2)}, u32[]{:S(2)}) collective-permute-start(f32[192,128]{1,0:T(8,128)S(1)} %get-tuple-element.39), channel_id=1, source_target_pairs={{0,8},{4,12},{8,0},{12,4},{16,24},{20,28},{24,16},{28,20},{1,9},{5... | collective-permute-start | bytes 294920 | tf_op jit(solution)/shard_map/ppermute | solution.py:23
  16.7 2.3 %shard_map.143 = (f32[4,64,128]{2,1,0:T(8,128)S(1)}, f32[4,64,128]{2,1,0:T(8,128)S(1)}) custom-call(f32[4,64,128]{2,1,0:T(8,128)S(1)} %get-tuple-element.35.refs_0_, f32[8,128]{1,0:T(8,128)S(1)} %get-tuple-element.36.refs_1_), custom_call_target="tpu_custom_call" | custom-call | flops 2600000000 | tf_op jit(solution)/shard_map/pallas_call | solution.py:353
  19.0 0.0 collective-permute-done.second
  19.0 0.6 %collective-permute-start.5 = (bf16[2,192,128]{2,1,0:T(8,128)(2,1)S(1)}, bf16[2,192,128]{2,1,0:T(8,128)(2,1)S(1)}, u32[]{:S(2)}, u32[]{:S(2)}) collective-permute-start(bf16[2,192,128]{2,1,0:T(8,128)(2,1)S(1)} %shard_map.144.refs_2_.rest_4_), channel_id=1, source_target_pairs={{0,4},{4,0},{8,12},{12,8},{16,20},{20,16},{24,28},{28,24},{1,5},{5... | collective-permute-start | bytes 294920 | tf_op jit(solution)/shard_map/ppermute | solution.py:23
  19.6 0.4 %collective-permute-start.2 = (bf16[2,192,128]{2,1,0:T(8,128)(2,1)S(1)}, bf16[2,192,128]{2,1,0:T(8,128)(2,1)S(1)}, u32[]{:S(2)}, u32[]{:S(2)}) collective-permute-start(bf16[2,192,128]{2,1,0:T(8,128)(2,1)S(1)} %shard_map.144.refs_2_.rest_4_), channel_id=1, source_target_pairs={{0,8},{4,12},{8,0},{12,4},{16,24},{20,28},{24,16},{28,20},{1,9},{5... | collective-permute-start | bytes 294920 | tf_op jit(solution)/shard_map/ppermute | solution.py:23
  20.0 0.0 collective-permute-done.3.refs_1_
  20.0 2.3 %shard_map.145 = (f32[4,64,128]{2,1,0:T(8,128)S(1)}, bf16[1,192,128]{2,1,0:T(8,128)(2,1)S(1)}) custom-call(f32[4,64,128]{2,1,0:T(8,128)S(1)} %get-tuple-element.38.refs_0_, f32[192,128]{1,0:T(8,128)S(1)} %collective-permute-done.3.refs_1_, bf16[2,192,128]{2,1,0:T(8,128)(2,1)S(1)} %shard_map.144.refs_2_.rest_4_), custom_call_target="tpu_custom_call" | custom-call | flops 2600000000 | tf_op jit(solution)/shard_map/pallas_call | solution.py:353
  22.3 1.4 %collective-permute-start.4 = (bf16[1,192,128]{2,1,0:T(8,128)(2,1)S(1)}, bf16[1,192,128]{2,1,0:T(8,128)(2,1)S(1)}, u32[]{:S(2)}, u32[]{:S(2)}) collective-permute-start(bf16[1,192,128]{2,1,0:T(8,128)(2,1)S(1)} %get-tuple-element.40.top_low.rest_0_), channel_id=1, source_target_pairs={{0,16},{4,20},{8,24},{12,28},{16,0},{20,4},{24,8},{28,12},{1,17},{... | collective-permute-start | bytes 147464 | tf_op jit(solution)/shard_map/ppermute | solution.py:23
  23.8 0.4 %collective-permute-done.2.after.rest_5_ = bf16[2,192,128]{2,1,0:T(8,128)(2,1)S(1)} collective-permute-done((bf16[2,192,128]{2,1,0:T(8,128)(2,1)S(1)}, bf16[2,192,128]{2,1,0:T(8,128)(2,1)S(1)}, u32[]{:S(2)}, u32[]{:S(2)}) %collective-permute-start.2) | collective-permute-done | bytes 98336 | tf_op jit(solution)/shard_map/ppermute | solution.py:23
  24.2 1.5 %collective-permute-start.6 = (bf16[2,192,128]{2,1,0:T(8,128)(2,1)S(1)}, bf16[2,192,128]{2,1,0:T(8,128)(2,1)S(1)}, u32[]{:S(2)}, u32[]{:S(2)}) collective-permute-start(bf16[2,192,128]{2,1,0:T(8,128)(2,1)S(1)} %collective-permute-done.2.after.rest_5_), channel_id=1, source_target_pairs={{0,4},{4,0},{8,12},{12,8},{16,20},{20,16},{24,28},{28,24},{1,5},{5... | collective-permute-start | bytes 294920 | tf_op jit(solution)/shard_map/ppermute | solution.py:23
  25.7 2.6 %shard_map.146 = (f32[2,64,64]{2,1,0:T(8,128)S(1)}, f32[8,64,64]{2,1,0:T(8,128)S(1)}, f32[4,64,64]{2,1,0:T(8,128)S(1)}, bf16[16,64,64]{2,1,0:T(8,128)(2,1)S(1)}) custom-call(s32[2]{0:T(128)S(1)} %pad_add_fusion.spot, s32[16]{0:T(128)S(1)} %copy-done.7, f32[8,64,64]{2,1,0:T(8,128)S(1)} %copy-done.2, ...), custom_call_target="tpu_custom_call" | custom-call | flops 2500000000 | tf_op jit(solution)/shard_map/pallas_call | solution.py:353
  28.3 0.0 collective-permute-done.4.rest_1_
  28.3 1.0 %shard_map.147.rest_3_ = bf16[16,64,64]{2,1,0:T(8,128)(2,1)S(1)} custom-call(s32[16]{0:T(128)S(1)} %fusion.source, bf16[16,64,64]{2,1,0:T(8,128)(2,1)S(1)} %get-tuple-element.47.halves, bf16[1,192,128]{2,1,0:T(8,128)(2,1)S(1)} %get-tuple-element.40.top_low.rest_0_, bf16[1,192,128]{2,1,0:T(8,128)(2,1)S(1)} %collective-permute-done.4.rest_1_), custom_call_target="tpu_custom_call" | custom-call | flops 1300000000 | tf_op jit(solution)/shard_map/pallas_call | solution.py:353
  29.3 0.0 collective-permute-done.5.rest_6_
  29.3 3.3 %shard_map.148 = (f32[2,64,64]{2,1,0:T(8,128)}, f32[8,64,64]{2,1,0:T(8,128)}, f32[4,64,64]{2,1,0:T(8,128)}, bf16[16,64,64]{2,1,0:T(8,128)(2,1)}, bf16[64,64,128]{2,1,0:T(8,128)(2,1)}) custom-call(s32[128]{0:T(128)S(1)} %bitcast_add_fusion.source, bf16[128,64,64]{2,1,0:T(8,128)(2,1)S(1)} %get-tuple-element.31.halves, ...), custom_call_target="tpu_custom_call" | custom-call | flops 3500000000 | tf_op jit(solution)/shard_map/pallas_call | solution.py:353
  (19 shorter events, 0.1 us)
Async XLA Ops:
  0.6 1.0 %copy-start.1 = (f32[8,64,64]{2,1,0:T(8,128)S(1)}, f32[8,64,64]{2,1,0:T(8,128)}, u32[]{:S(2)}) copy-start(f32[8,64,64]{2,1,0:T(8,128)} %bases.3) | copy-start | bytes 393220
  1.6 0.9 %copy-start.3 = (f32[8,64,64]{2,1,0:T(8,128)S(1)}, f32[8,64,64]{2,1,0:T(8,128)}, u32[]{:S(2)}) copy-start(f32[8,64,64]{2,1,0:T(8,128)} %leaf_transfer.1) | copy-start | bytes 393220
  1.6 1.0 %copy-start.5 = (f32[4,64,64]{2,1,0:T(8,128)S(1)}, f32[4,64,64]{2,1,0:T(8,128)}, u32[]{:S(2)}) copy-start(f32[4,64,64]{2,1,0:T(8,128)} %top_transfer.1) | copy-start | bytes 196612
  3.4 10.3 %collective-permute-start.1 = (f32[6,64,128]{2,1,0:T(8,128)S(1)}, f32[6,64,128]{2,1,0:T(8,128)S(1)}, u32[]{:S(2)}, u32[]{:S(2)}) collective-permute-start(f32[6,64,128]{2,1,0:T(8,128)S(1)} %get-tuple-element.34.mine), channel_id=1, source_target_pairs={{0,4},{4,0},{8,12},{12,8},{16,20},{20,16},{24,28},{28,24},{1,5},{5... | collective-permute-start | bytes 589832 | tf_op jit(solution)/shard_map/ppermute | solution.py:23
  6.4 2.3 %copy-start = (bf16[128,64,64]{0,2,1:T(8,128)(2,1)S(1)}, bf16[128,64,64]{0,2,1:T(8,128)(2,1)}, u32[]{:S(2)}) copy-start(bf16[128,64,64]{0,2,1:T(8,128)(2,1)} %param.13) | copy-start | bytes 3145732
  6.4 2.3 %copy-start.6 = (s32[128]{0:T(128)S(1)}, s32[128]{0:T(128)}, u32[]{:S(2)}) copy-start(s32[128]{0:T(128)} %target.2) | copy-start | bytes 1540
  8.7 4.9 %copy-start.8 = (s32[128]{0:T(128)S(1)}, s32[128]{0:T(128)}, u32[]{:S(2)}) copy-start(s32[128]{0:T(128)} %param.16) | copy-start | bytes 1540
  8.8 4.9 %copy-start.9 = (s32[128,1]{0,1:T(1,128)S(1)}, s32[128,1]{0,1:T(1,128)}, u32[]{:S(2)}) copy-start(s32[128,1]{0,1:T(1,128)} %param.15) | copy-start | bytes 1540
  8.8 4.9 %copy-start.10 = (s32[16]{0:T(128)S(1)}, s32[16]{0:T(128)}, u32[]{:S(2)}) copy-start(s32[16]{0:T(128)} %param.19) | copy-start | bytes 196
  10.9 8.0 %collective-permute-start = (bf16[1,192,128]{2,1,0:T(8,128)(2,1)S(1)}, bf16[1,192,128]{2,1,0:T(8,128)(2,1)S(1)}, u32[]{:S(2)}, u32[]{:S(2)}) collective-permute-start(bf16[1,192,128]{2,1,0:T(8,128)(2,1)S(1)} %shard_map.141.first), channel_id=1, source_target_pairs={{0,16},{4,20},{8,24},{12,28},{16,0},{20,4},{24,8},{28,12},{1,17},{... | collective-permute-start | bytes 147464 | tf_op jit(solution)/shard_map/ppermute | solution.py:23
  15.1 4.9 %collective-permute-start.3 = (f32[192,128]{1,0:T(8,128)S(1)}, f32[192,128]{1,0:T(8,128)S(1)}, u32[]{:S(2)}, u32[]{:S(2)}) collective-permute-start(f32[192,128]{1,0:T(8,128)S(1)} %get-tuple-element.39), channel_id=1, source_target_pairs={{0,8},{4,12},{8,0},{12,4},{16,24},{20,28},{24,16},{28,20},{1,9},{5... | collective-permute-start | bytes 294920 | tf_op jit(solution)/shard_map/ppermute | solution.py:23
  19.0 10.3 %collective-permute-start.5 = (bf16[2,192,128]{2,1,0:T(8,128)(2,1)S(1)}, bf16[2,192,128]{2,1,0:T(8,128)(2,1)S(1)}, u32[]{:S(2)}, u32[]{:S(2)}) collective-permute-start(bf16[2,192,128]{2,1,0:T(8,128)(2,1)S(1)} %shard_map.144.refs_2_.rest_4_), channel_id=1, source_target_pairs={{0,4},{4,0},{8,12},{12,8},{16,20},{20,16},{24,28},{28,24},{1,5},{5... | collective-permute-start | bytes 294920 | tf_op jit(solution)/shard_map/ppermute | solution.py:23
  19.6 4.6 %collective-permute-start.2 = (bf16[2,192,128]{2,1,0:T(8,128)(2,1)S(1)}, bf16[2,192,128]{2,1,0:T(8,128)(2,1)S(1)}, u32[]{:S(2)}, u32[]{:S(2)}) collective-permute-start(bf16[2,192,128]{2,1,0:T(8,128)(2,1)S(1)} %shard_map.144.refs_2_.rest_4_), channel_id=1, source_target_pairs={{0,8},{4,12},{8,0},{12,4},{16,24},{20,28},{24,16},{28,20},{1,9},{5... | collective-permute-start | bytes 294920 | tf_op jit(solution)/shard_map/ppermute | solution.py:23
  20.0 5.7 %copy-start.2 = (f32[8,64,64]{2,1,0:T(8,128)S(1)}, f32[8,64,64]{2,1,0:T(8,128)}, u32[]{:S(2)}) copy-start(f32[8,64,64]{2,1,0:T(8,128)} %bases.3) | copy-start | bytes 393220
  20.0 5.7 %copy-start.4 = (bf16[16,64,64]{2,1,0:T(8,128)(2,1)S(1)}, bf16[16,64,64]{2,1,0:T(8,128)(2,1)}, u32[]{:S(2)}) copy-start(bf16[16,64,64]{2,1,0:T(8,128)(2,1)} %top_couplings.1) | copy-start | bytes 393220
  20.0 5.7 %copy-start.7 = (s32[16]{0:T(128)S(1)}, s32[16]{0:T(128)}, u32[]{:S(2)}) copy-start(s32[16]{0:T(128)} %target.3) | copy-start | bytes 196
  22.3 5.9 %collective-permute-start.4 = (bf16[1,192,128]{2,1,0:T(8,128)(2,1)S(1)}, bf16[1,192,128]{2,1,0:T(8,128)(2,1)S(1)}, u32[]{:S(2)}, u32[]{:S(2)}) collective-permute-start(bf16[1,192,128]{2,1,0:T(8,128)(2,1)S(1)} %get-tuple-element.40.top_low.rest_0_), channel_id=1, source_target_pairs={{0,16},{4,20},{8,24},{12,28},{16,0},{20,4},{24,8},{28,12},{1,17},{... | collective-permute-start | bytes 147464 | tf_op jit(solution)/shard_map/ppermute | solution.py:23
  24.2 5.1 %collective-permute-start.6 = (bf16[2,192,128]{2,1,0:T(8,128)(2,1)S(1)}, bf16[2,192,128]{2,1,0:T(8,128)(2,1)S(1)}, u32[]{:S(2)}, u32[]{:S(2)}) collective-permute-start(bf16[2,192,128]{2,1,0:T(8,128)(2,1)S(1)} %collective-permute-done.2.after.rest_5_), channel_id=1, source_target_pairs={{0,4},{4,0},{8,12},{12,8},{16,20},{20,16},{24,28},{28,24},{1,5},{5... | collective-permute-start | bytes 294920 | tf_op jit(solution)/shard_map/ppermute | solution.py:23

commit v7 on v6

--- a/solution.py
+++ b/solution.py
@@ -59,8 +59,14 @@
     return lax.dot_general(a, b, (((0,), (0,)), ((), ())), precision=exact, preferred_element_type=f32)
 
 
-def dot_nt(a, b):
-    return lax.dot_general(a, b, (((1,), (1,)), ((), ())), precision=exact, preferred_element_type=f32)
+def near_nn(a, b):
+    return jnp.dot(a, b, precision=lax.Precision.HIGH, preferred_element_type=f32)
+
+
+def near_nt(a, b):
+    return lax.dot_general(
+        a, b, (((1,), (1,)), ((), ())), precision=lax.Precision.HIGH, preferred_element_type=f32
+    )
 
 
 def low_nn(a, b):
@@ -273,16 +279,16 @@
     for n, lanes in enumerate((slice(0, rank), slice(rank, 2 * rank))):
         for g in range(GROUP):
             place = n * GROUP + g
-            piece = dot_nn(leaf_factor[g][:, lanes], leaf_transfer[place])
-            leaf_transfers[place] = dot_nt(piece, middle_inverse[g][:, lanes])
+            piece = near_nn(leaf_factor[g][:, lanes], leaf_transfer[place])
+            leaf_transfers[place] = near_nt(piece, middle_inverse[g][:, lanes])
     for g in range(GROUP):
         left, right = (jnp.where(spot[1] == 0, both[:, :rank], both[:, rank:]) for both in (middle_factor[g], top_inverse[g]))
-        top_transfers[g] = dot_nt(dot_nn(left, top_transfer[g]), right)
+        top_transfers[g] = near_nt(near_nn(left, top_transfer[g]), right)
     for k in range(share):
         place = spot[0] * share + k
         both = leaf_inverse[place % GROUP]
         both = jnp.where(place < GROUP, both[:, :rank], both[:, rank:])
-        leaf_bases[k] = dot_nt(bases[place], both)
+        leaf_bases[k] = near_nt(bases[place], both)
 
 
 def shares(count, steps):
@@ -431,8 +437,8 @@
     middle_inverse, middle_factor = factored([middle_gram], token, True, False)
     table = joined_by_xor(held(low, half_token), "leaf", leaf_bits[:-2], middle_inverse)
     tables = [table, swapped(table, "leaf", 1 << leaf_bits[-2])]
-    tables += [swapped(one, "leaf", 1 << leaf_bits[-1]) for one in tables]
     top_inverse, top_low = factored([top_gram, top_gram_other], table, False, True)
+    tables += [swapped(one, "leaf", 1 << leaf_bits[-1]) for one in (held(table, top_inverse), tables[1])]
     top_table = joined_by_xor(top_low, "leaf", [bit + 2 for bit in quad_bits[:-1]], top_inverse)
     top_tables = [top_table, swapped(top_table, "leaf", 4 << quad_bits[-1])]
     leaf_bases, leaf_transfers, top_transfers, top_halves = call(

time: 32.8 us -> 32.3 us (0.985)
  Pallas kernels: 18.6 us -> 18 us
  waiting for transfers between devices: 0.41 us -> 0.88 us
  starting transfers between devices: 11.3 us -> 10.9 us
    pallas_call x12 -> x13, Pallas kernels: 18.6 us -> 18 us  [call(): pl.pallas_call(kernel, out_shape=[jax.ShapeDtypeStruct(shape, dtype) for...]
    ppermute x7, waiting for transfers between devices: 0.41 us -> 0.88 us  [swapped(): return lax.ppermute(value, axis, pairs)]
    ppermute x7, starting transfers between devices: 11.3 us -> 10.9 us  [swapped(): return lax.ppermute(value, axis, pairs)]
  transfers between devices with their start and end apart: 7 -> 7, of which waited for: 1 -> 2; matrix products, arithmetic and copies ran while one was open for 0% -> 0% of each run, Pallas kernels for 43% -> 42%
where the time goes in v7:
time: 32.3 us; the launch traced here: 32.1 us
  Pallas kernels  18 us (56%)
  starting transfers between devices  10.9 us (34%)
  local copies, waits for them, and re-layouts  1.49 us (5%)
  waiting for transfers between devices  0.88 us (3%)
  between operations  0.77 us (2%)
    pallas_call x13, Pallas kernels, call(): pl.pallas_call(kernel, out_shape=[jax.ShapeDtypeStruct(shape, dtype) for...  18 us
    ppermute x7, starting transfers between devices, swapped(): return lax.ppermute(value, axis, pairs)  10.9 us
    unnamed x22, local copies, waits for them, and re-layouts  1.49 us
    ppermute x7, waiting for transfers between devices, swapped(): return lax.ppermute(value, axis, pairs)  0.88 us
  transfers between devices with their start and end apart: 7, of which 2 were waited for; matrix products, arithmetic and copies ran while one was open for 0% of the time, Pallas kernels for 42%

profile of v7, /device:TPU:0, one launch (start us, length us, event | category | flops | bytes accessed | tf_op | source)
XLA Modules:
  0.0 32.1 jit_solution(1450697832918795447)
XLA Ops:
  0.6 0.0 copy-start.1
  0.6 0.9 %copy-done.1 = f32[8,64,64]{2,1,0:T(8,128)S(1)} copy-done((f32[8,64,64]{2,1,0:T(8,128)S(1)}, f32[8,64,64]{2,1,0:T(8,128)}, u32[]{:S(2)}) %copy-start.1) | copy-done | bytes 131096
  1.6 0.5 %shard_map.137.gram.refs_0_ = f32[4,64,128]{2,1,0:T(8,128)S(1)} custom-call(f32[8,64,64]{2,1,0:T(8,128)S(1)} %copy-done.1), custom_call_target="tpu_custom_call" | custom-call | flops 1000000000 | tf_op jit(solution)/shard_map/pallas_call | solution.py:359
  2.1 0.5 %copy-done.3 = f32[8,64,64]{2,1,0:T(8,128)S(1)} copy-done((f32[8,64,64]{2,1,0:T(8,128)S(1)}, f32[8,64,64]{2,1,0:T(8,128)}, u32[]{:S(2)}) %copy-start.3) | copy-done | bytes 131096
  2.5 0.0 copy-done.5
  2.6 0.8 %shard_map.138 = (f32[6,64,128]{2,1,0:T(8,128)S(1)}, f32[8,128]{1,0:T(8,128)S(1)}) custom-call(f32[4,64,128]{2,1,0:T(8,128)S(1)} %shard_map.137.gram.refs_0_, f32[8,64,64]{2,1,0:T(8,128)S(1)} %copy-done.3, f32[4,64,64]{2,1,0:T(8,128)S(1)} %copy-done.5), custom_call_target="tpu_custom_call" | custom-call | flops 800000000 | tf_op jit(solution)/shard_map/pallas_call | solution.py:359
  3.4 3.0 %collective-permute-start.1 = (f32[6,64,128]{2,1,0:T(8,128)S(1)}, f32[6,64,128]{2,1,0:T(8,128)S(1)}, u32[]{:S(2)}, u32[]{:S(2)}) collective-permute-start(f32[6,64,128]{2,1,0:T(8,128)S(1)} %get-tuple-element.34.mine), channel_id=1, source_target_pairs={{0,4},{4,0},{8,12},{12,8},{16,20},{20,16},{24,28},{28,24},{1,5},{5... | collective-permute-start | bytes 589832 | tf_op jit(solution)/shard_map/ppermute | solution.py:23
  6.4 2.3 %shard_map.139 = (f32[4,64,128]{2,1,0:T(8,128)S(1)}, f32[4,64,128]{2,1,0:T(8,128)S(1)}, bf16[1,192,128]{2,1,0:T(8,128)(2,1)S(1)}) custom-call(f32[4,64,128]{2,1,0:T(8,128)S(1)} %shard_map.137.gram.refs_0_, f32[8,128]{1,0:T(8,128)S(1)} %get-tuple-element.29.refs_1_), custom_call_target="tpu_custom_call" | custom-call | flops 2600000000 | tf_op jit(solution)/shard_map/pallas_call | solution.py:359
  8.7 0.0 copy-done.6
  8.7 0.0 copy-start.8
  8.8 0.0 copy-start.9
  8.8 0.0 copy-start.10
  8.8 2.1 %shard_map.140 = (bf16[128,64,64]{2,1,0:T(8,128)(2,1)S(1)}, f32[8,128]{1,0:T(8,128)S(1)}) custom-call(s32[128]{0:T(128)S(1)} %copy-done.6, bf16[64,64,128]{2,1,0:T(8,128)(2,1)S(1)} %bitcast.6, f32[4,64,128]{2,1,0:T(8,128)S(1)} %get-tuple-element.30.low.leaf_factor), custom_call_target="tpu_custom_call" | custom-call | flops 2700000000 | tf_op jit(solution)/shard_map/pallas_call | solution.py:359
  10.9 2.7 %collective-permute-start = (bf16[1,192,128]{2,1,0:T(8,128)(2,1)S(1)}, bf16[1,192,128]{2,1,0:T(8,128)(2,1)S(1)}, u32[]{:S(2)}, u32[]{:S(2)}) collective-permute-start(bf16[1,192,128]{2,1,0:T(8,128)(2,1)S(1)} %shard_map.141.first), channel_id=1, source_target_pairs={{0,16},{4,20},{8,24},{12,28},{16,0},{20,4},{24,8},{28,12},{1,17},{... | collective-permute-start | bytes 147464 | tf_op jit(solution)/shard_map/ppermute | solution.py:23
  13.6 0.1 pad_add_fusion.spot
  13.7 0.0 collective-permute-done.1.other
  13.7 1.4 %shard_map.142 = (f32[4,64,128]{2,1,0:T(8,128)S(1)}, f32[4,64,128]{2,1,0:T(8,128)S(1)}, f32[192,128]{1,0:T(8,128)S(1)}, f32[8,128]{1,0:T(8,128)S(1)}) custom-call(s32[2]{0:T(128)S(1)} %pad_add_fusion.spot, f32[6,64,128]{2,1,0:T(8,128)S(1)} %get-tuple-element.34.mine, f32[6,64,128]{2,1,0:T(8,128)S(1)} %collective-permute-done.1.other, ...), custom_call_target="tpu_custom_call" | custom-call | flops 1400000000 | tf_op jit(solution)/shard_map/pallas_call | solution.py:359
  15.1 1.6 %collective-permute-start.3 = (f32[192,128]{1,0:T(8,128)S(1)}, f32[192,128]{1,0:T(8,128)S(1)}, u32[]{:S(2)}, u32[]{:S(2)}) collective-permute-start(f32[192,128]{1,0:T(8,128)S(1)} %get-tuple-element.39), channel_id=1, source_target_pairs={{0,8},{4,12},{8,0},{12,4},{16,24},{20,28},{24,16},{28,20},{1,9},{5... | collective-permute-start | bytes 294920 | tf_op jit(solution)/shard_map/ppermute | solution.py:23
  16.7 2.3 %shard_map.143 = (f32[4,64,128]{2,1,0:T(8,128)S(1)}, f32[4,64,128]{2,1,0:T(8,128)S(1)}) custom-call(f32[4,64,128]{2,1,0:T(8,128)S(1)} %get-tuple-element.35.refs_0_, f32[8,128]{1,0:T(8,128)S(1)} %get-tuple-element.36.refs_1_), custom_call_target="tpu_custom_call" | custom-call | flops 2600000000 | tf_op jit(solution)/shard_map/pallas_call | solution.py:359
  19.0 0.0 collective-permute-done.second
  19.0 0.5 %collective-permute-start.2 = (bf16[2,192,128]{2,1,0:T(8,128)(2,1)S(1)}, bf16[2,192,128]{2,1,0:T(8,128)(2,1)S(1)}, u32[]{:S(2)}, u32[]{:S(2)}) collective-permute-start(bf16[2,192,128]{2,1,0:T(8,128)(2,1)S(1)} %shard_map.144.refs_2_.value.rest_4_), channel_id=1, source_target_pairs={{0,8},{4,12},{8,0},{12,4},{16,24},{20,28},{24,16},{28,20},{1,9},{5... | collective-permute-start | bytes 294920 | tf_op jit(solution)/shard_map/ppermute | solution.py:23
  19.5 0.2 collective-permute-done.3.refs_1_
  19.7 2.3 %shard_map.145 = (f32[4,64,128]{2,1,0:T(8,128)S(1)}, bf16[1,192,128]{2,1,0:T(8,128)(2,1)S(1)}) custom-call(f32[4,64,128]{2,1,0:T(8,128)S(1)} %get-tuple-element.38.refs_0_, f32[192,128]{1,0:T(8,128)S(1)} %collective-permute-done.3.refs_1_, bf16[2,192,128]{2,1,0:T(8,128)(2,1)S(1)} %shard_map.144.refs_2_.value.rest_4_), custom_call_target="tpu_custom_call" | custom-call | flops 2600000000 | tf_op jit(solution)/shard_map/pallas_call | solution.py:359
  22.1 1.0 %collective-permute-start.4 = (bf16[1,192,128]{2,1,0:T(8,128)(2,1)S(1)}, bf16[1,192,128]{2,1,0:T(8,128)(2,1)S(1)}, u32[]{:S(2)}, u32[]{:S(2)}) collective-permute-start(bf16[1,192,128]{2,1,0:T(8,128)(2,1)S(1)} %get-tuple-element.40.top_low.rest_0_), channel_id=1, source_target_pairs={{0,16},{4,20},{8,24},{12,28},{16,0},{20,4},{24,8},{28,12},{1,17},{... | collective-permute-start | bytes 147464 | tf_op jit(solution)/shard_map/ppermute | solution.py:23
  23.1 1.0 %collective-permute-start.5 = (bf16[2,192,128]{2,1,0:T(8,128)(2,1)S(1)}, bf16[2,192,128]{2,1,0:T(8,128)(2,1)S(1)}, u32[]{:S(2)}, u32[]{:S(2)}) collective-permute-start(bf16[2,192,128]{2,1,0:T(8,128)(2,1)S(1)} %shard_map.148), channel_id=1, source_target_pairs={{0,4},{4,0},{8,12},{12,8},{16,20},{20,16},{24,28},{28,24},{1,5},{5... | collective-permute-start | bytes 294920 | tf_op jit(solution)/shard_map/ppermute | solution.py:23
  24.1 1.1 %collective-permute-start.6 = (bf16[2,192,128]{2,1,0:T(8,128)(2,1)S(1)}, bf16[2,192,128]{2,1,0:T(8,128)(2,1)S(1)}, u32[]{:S(2)}, u32[]{:S(2)}) collective-permute-start(bf16[2,192,128]{2,1,0:T(8,128)(2,1)S(1)} %collective-permute-done.2.after.rest_5_), channel_id=1, source_target_pairs={{0,4},{4,0},{8,12},{12,8},{16,20},{20,16},{24,28},{28,24},{1,5},{5... | collective-permute-start | bytes 294920 | tf_op jit(solution)/shard_map/ppermute | solution.py:23
  25.2 2.0 %shard_map.146 = (f32[2,64,64]{2,1,0:T(8,128)S(1)}, f32[8,64,64]{2,1,0:T(8,128)S(1)}, f32[4,64,64]{2,1,0:T(8,128)S(1)}, bf16[16,64,64]{2,1,0:T(8,128)(2,1)S(1)}) custom-call(s32[2]{0:T(128)S(1)} %pad_add_fusion.spot, s32[16]{0:T(128)S(1)} %copy-done.7, f32[8,64,64]{2,1,0:T(8,128)S(1)} %copy-done.2, ...), custom_call_target="tpu_custom_call" | custom-call | flops 2500000000 | tf_op jit(solution)/shard_map/pallas_call | solution.py:359
  27.2 0.0 collective-permute-done.4.rest_1_
  27.2 1.0 %shard_map.147.rest_3_ = bf16[16,64,64]{2,1,0:T(8,128)(2,1)S(1)} custom-call(s32[16]{0:T(128)S(1)} %fusion.source, bf16[16,64,64]{2,1,0:T(8,128)(2,1)S(1)} %get-tuple-element.47.halves, bf16[1,192,128]{2,1,0:T(8,128)(2,1)S(1)} %get-tuple-element.40.top_low.rest_0_, bf16[1,192,128]{2,1,0:T(8,128)(2,1)S(1)} %collective-permute-done.4.rest_1_), custom_call_target="tpu_custom_call" | custom-call | flops 1300000000 | tf_op jit(solution)/shard_map/pallas_call | solution.py:359
  28.2 0.0 collective-permute-done.5.rest_6_
  28.2 0.6 %collective-permute-done.6.rest_7_ = bf16[2,192,128]{2,1,0:T(8,128)(2,1)S(1)} collective-permute-done((bf16[2,192,128]{2,1,0:T(8,128)(2,1)S(1)}, bf16[2,192,128]{2,1,0:T(8,128)(2,1)S(1)}, u32[]{:S(2)}, u32[]{:S(2)}) %collective-permute-start.6) | collective-permute-done | bytes 98336 | tf_op jit(solution)/shard_map/ppermute | solution.py:23
  28.8 3.3 %shard_map.149 = (f32[2,64,64]{2,1,0:T(8,128)}, f32[8,64,64]{2,1,0:T(8,128)}, f32[4,64,64]{2,1,0:T(8,128)}, bf16[16,64,64]{2,1,0:T(8,128)(2,1)}, bf16[64,64,128]{2,1,0:T(8,128)(2,1)}) custom-call(s32[128]{0:T(128)S(1)} %bitcast_add_fusion.source, bf16[128,64,64]{2,1,0:T(8,128)(2,1)S(1)} %get-tuple-element.31.halves, ...), custom_call_target="tpu_custom_call" | custom-call | flops 3500000000 | tf_op jit(solution)/shard_map/pallas_call | solution.py:359
  (20 shorter events, 0.1 us)
Async XLA Ops:
  0.6 1.0 %copy-start.1 = (f32[8,64,64]{2,1,0:T(8,128)S(1)}, f32[8,64,64]{2,1,0:T(8,128)}, u32[]{:S(2)}) copy-start(f32[8,64,64]{2,1,0:T(8,128)} %bases.3) | copy-start | bytes 393220
  1.6 0.9 %copy-start.3 = (f32[8,64,64]{2,1,0:T(8,128)S(1)}, f32[8,64,64]{2,1,0:T(8,128)}, u32[]{:S(2)}) copy-start(f32[8,64,64]{2,1,0:T(8,128)} %leaf_transfer.1) | copy-start | bytes 393220
  1.6 1.0 %copy-start.5 = (f32[4,64,64]{2,1,0:T(8,128)S(1)}, f32[4,64,64]{2,1,0:T(8,128)}, u32[]{:S(2)}) copy-start(f32[4,64,64]{2,1,0:T(8,128)} %top_transfer.1) | copy-start | bytes 196612
  3.4 10.3 %collective-permute-start.1 = (f32[6,64,128]{2,1,0:T(8,128)S(1)}, f32[6,64,128]{2,1,0:T(8,128)S(1)}, u32[]{:S(2)}, u32[]{:S(2)}) collective-permute-start(f32[6,64,128]{2,1,0:T(8,128)S(1)} %get-tuple-element.34.mine), channel_id=1, source_target_pairs={{0,4},{4,0},{8,12},{12,8},{16,20},{20,16},{24,28},{28,24},{1,5},{5... | collective-permute-start | bytes 589832 | tf_op jit(solution)/shard_map/ppermute | solution.py:23
  6.4 2.3 %copy-start = (bf16[128,64,64]{0,2,1:T(8,128)(2,1)S(1)}, bf16[128,64,64]{0,2,1:T(8,128)(2,1)}, u32[]{:S(2)}) copy-start(bf16[128,64,64]{0,2,1:T(8,128)(2,1)} %param.13) | copy-start | bytes 3145732
  6.4 2.3 %copy-start.6 = (s32[128]{0:T(128)S(1)}, s32[128]{0:T(128)}, u32[]{:S(2)}) copy-start(s32[128]{0:T(128)} %target.2) | copy-start | bytes 1540
  8.7 4.9 %copy-start.8 = (s32[128]{0:T(128)S(1)}, s32[128]{0:T(128)}, u32[]{:S(2)}) copy-start(s32[128]{0:T(128)} %param.16) | copy-start | bytes 1540
  8.8 4.9 %copy-start.9 = (s32[128,1]{0,1:T(1,128)S(1)}, s32[128,1]{0,1:T(1,128)}, u32[]{:S(2)}) copy-start(s32[128,1]{0,1:T(1,128)} %param.15) | copy-start | bytes 1540
  8.8 4.9 %copy-start.10 = (s32[16]{0:T(128)S(1)}, s32[16]{0:T(128)}, u32[]{:S(2)}) copy-start(s32[16]{0:T(128)} %param.19) | copy-start | bytes 196
  10.9 8.0 %collective-permute-start = (bf16[1,192,128]{2,1,0:T(8,128)(2,1)S(1)}, bf16[1,192,128]{2,1,0:T(8,128)(2,1)S(1)}, u32[]{:S(2)}, u32[]{:S(2)}) collective-permute-start(bf16[1,192,128]{2,1,0:T(8,128)(2,1)S(1)} %shard_map.141.first), channel_id=1, source_target_pairs={{0,16},{4,20},{8,24},{12,28},{16,0},{20,4},{24,8},{28,12},{1,17},{... | collective-permute-start | bytes 147464 | tf_op jit(solution)/shard_map/ppermute | solution.py:23
  15.1 4.6 %collective-permute-start.3 = (f32[192,128]{1,0:T(8,128)S(1)}, f32[192,128]{1,0:T(8,128)S(1)}, u32[]{:S(2)}, u32[]{:S(2)}) collective-permute-start(f32[192,128]{1,0:T(8,128)S(1)} %get-tuple-element.39), channel_id=1, source_target_pairs={{0,8},{4,12},{8,0},{12,4},{16,24},{20,28},{24,16},{28,20},{1,9},{5... | collective-permute-start | bytes 294920 | tf_op jit(solution)/shard_map/ppermute | solution.py:23
  19.0 5.1 %collective-permute-start.2 = (bf16[2,192,128]{2,1,0:T(8,128)(2,1)S(1)}, bf16[2,192,128]{2,1,0:T(8,128)(2,1)S(1)}, u32[]{:S(2)}, u32[]{:S(2)}) collective-permute-start(bf16[2,192,128]{2,1,0:T(8,128)(2,1)S(1)} %shard_map.144.refs_2_.value.rest_4_), channel_id=1, source_target_pairs={{0,8},{4,12},{8,0},{12,4},{16,24},{20,28},{24,16},{28,20},{1,9},{5... | collective-permute-start | bytes 294920 | tf_op jit(solution)/shard_map/ppermute | solution.py:23
  19.7 5.4 %copy-start.2 = (f32[8,64,64]{2,1,0:T(8,128)S(1)}, f32[8,64,64]{2,1,0:T(8,128)}, u32[]{:S(2)}) copy-start(f32[8,64,64]{2,1,0:T(8,128)} %bases.3) | copy-start | bytes 393220
  19.7 5.4 %copy-start.4 = (bf16[16,64,64]{2,1,0:T(8,128)(2,1)S(1)}, bf16[16,64,64]{2,1,0:T(8,128)(2,1)}, u32[]{:S(2)}) copy-start(bf16[16,64,64]{2,1,0:T(8,128)(2,1)} %top_couplings.1) | copy-start | bytes 393220
  19.7 5.4 %copy-start.7 = (s32[16]{0:T(128)S(1)}, s32[16]{0:T(128)}, u32[]{:S(2)}) copy-start(s32[16]{0:T(128)} %target.3) | copy-start | bytes 196
  22.1 5.1 %collective-permute-start.4 = (bf16[1,192,128]{2,1,0:T(8,128)(2,1)S(1)}, bf16[1,192,128]{2,1,0:T(8,128)(2,1)S(1)}, u32[]{:S(2)}, u32[]{:S(2)}) collective-permute-start(bf16[1,192,128]{2,1,0:T(8,128)(2,1)S(1)} %get-tuple-element.40.top_low.rest_0_), channel_id=1, source_target_pairs={{0,16},{4,20},{8,24},{12,28},{16,0},{20,4},{24,8},{28,12},{1,17},{... | collective-permute-start | bytes 147464 | tf_op jit(solution)/shard_map/ppermute | solution.py:23
  23.1 5.1 %collective-permute-start.5 = (bf16[2,192,128]{2,1,0:T(8,128)(2,1)S(1)}, bf16[2,192,128]{2,1,0:T(8,128)(2,1)S(1)}, u32[]{:S(2)}, u32[]{:S(2)}) collective-permute-start(bf16[2,192,128]{2,1,0:T(8,128)(2,1)S(1)} %shard_map.148), channel_id=1, source_target_pairs={{0,4},{4,0},{8,12},{12,8},{16,20},{20,16},{24,28},{28,24},{1,5},{5... | collective-permute-start | bytes 294920 | tf_op jit(solution)/shard_map/ppermute | solution.py:23
  24.1 4.7 %collective-permute-start.6 = (bf16[2,192,128]{2,1,0:T(8,128)(2,1)S(1)}, bf16[2,192,128]{2,1,0:T(8,128)(2,1)S(1)}, u32[]{:S(2)}, u32[]{:S(2)}) collective-permute-start(bf16[2,192,128]{2,1,0:T(8,128)(2,1)S(1)} %collective-permute-done.2.after.rest_5_), channel_id=1, source_target_pairs={{0,4},{4,0},{8,12},{12,8},{16,20},{20,16},{24,28},{28,24},{1,5},{5... | collective-permute-start | bytes 294920 | tf_op jit(solution)/shard_map/ppermute | solution.py:23

commit v8 on v7

--- a/solution.py
+++ b/solution.py
@@ -437,8 +437,9 @@
     middle_inverse, middle_factor = factored([middle_gram], token, True, False)
     table = joined_by_xor(held(low, half_token), "leaf", leaf_bits[:-2], middle_inverse)
     tables = [table, swapped(table, "leaf", 1 << leaf_bits[-2])]
-    top_inverse, top_low = factored([top_gram, top_gram_other], table, False, True)
-    tables += [swapped(one, "leaf", 1 << leaf_bits[-1]) for one in (held(table, top_inverse), tables[1])]
+    late = held(table, top_gram_other)
+    top_inverse, top_low = factored([top_gram, top_gram_other], late, False, True)
+    tables += [swapped(one, "leaf", 1 << leaf_bits[-1]) for one in (late, tables[1])]
     top_table = joined_by_xor(top_low, "leaf", [bit + 2 for bit in quad_bits[:-1]], top_inverse)
     top_tables = [top_table, swapped(top_table, "leaf", 4 << quad_bits[-1])]
     leaf_bases, leaf_transfers, top_transfers, top_halves = call(

time: 32.3 us -> 32.2 us (level)
  transfers between devices with their start and end apart: 7 -> 7, of which waited for: 2 -> 3; matrix products, arithmetic and copies ran while one was open for 0% -> 0% of each run, Pallas kernels for 42% -> 42%
where the time goes in v8:
time: 32.2 us; the launch traced here: 32 us
  Pallas kernels  18 us (56%)
  starting transfers between devices  10.9 us (34%)
  local copies, waits for them, and re-layouts  1.49 us (5%)
  waiting for transfers between devices  0.78 us (2%)
  between operations  0.77 us (2%)
    pallas_call x13, Pallas kernels, call(): pl.pallas_call(kernel, out_shape=[jax.ShapeDtypeStruct(shape, dtype) for...  18 us
    ppermute x7, starting transfers between devices, swapped(): return lax.ppermute(value, axis, pairs)  10.9 us
    unnamed x22, local copies, waits for them, and re-layouts  1.49 us
    ppermute x7, waiting for transfers between devices, swapped(): return lax.ppermute(value, axis, pairs)  0.78 us
  transfers between devices with their start and end apart: 7, of which 3 were waited for; matrix products, arithmetic and copies ran while one was open for 0% of the time, Pallas kernels for 42%

profile of v8, /device:TPU:0, one launch (start us, length us, event | category | flops | bytes accessed | tf_op | source)
XLA Modules:
  0.0 32.0 jit_solution(929417649735893806)
XLA Ops:
  0.6 0.0 copy-start.1
  0.6 0.9 %copy-done.1 = f32[8,64,64]{2,1,0:T(8,128)S(1)} copy-done((f32[8,64,64]{2,1,0:T(8,128)S(1)}, f32[8,64,64]{2,1,0:T(8,128)}, u32[]{:S(2)}) %copy-start.1) | copy-done | bytes 131096
  1.6 0.5 %shard_map.137.gram.refs_0_ = f32[4,64,128]{2,1,0:T(8,128)S(1)} custom-call(f32[8,64,64]{2,1,0:T(8,128)S(1)} %copy-done.1), custom_call_target="tpu_custom_call" | custom-call | flops 1000000000 | tf_op jit(solution)/shard_map/pallas_call | solution.py:359
  2.1 0.5 %copy-done.3 = f32[8,64,64]{2,1,0:T(8,128)S(1)} copy-done((f32[8,64,64]{2,1,0:T(8,128)S(1)}, f32[8,64,64]{2,1,0:T(8,128)}, u32[]{:S(2)}) %copy-start.3) | copy-done | bytes 131096
  2.5 0.0 copy-done.5
  2.6 0.8 %shard_map.138 = (f32[6,64,128]{2,1,0:T(8,128)S(1)}, f32[8,128]{1,0:T(8,128)S(1)}) custom-call(f32[4,64,128]{2,1,0:T(8,128)S(1)} %shard_map.137.gram.refs_0_, f32[8,64,64]{2,1,0:T(8,128)S(1)} %copy-done.3, f32[4,64,64]{2,1,0:T(8,128)S(1)} %copy-done.5), custom_call_target="tpu_custom_call" | custom-call | flops 800000000 | tf_op jit(solution)/shard_map/pallas_call | solution.py:359
  3.4 3.0 %collective-permute-start.1 = (f32[6,64,128]{2,1,0:T(8,128)S(1)}, f32[6,64,128]{2,1,0:T(8,128)S(1)}, u32[]{:S(2)}, u32[]{:S(2)}) collective-permute-start(f32[6,64,128]{2,1,0:T(8,128)S(1)} %get-tuple-element.34.mine), channel_id=1, source_target_pairs={{0,4},{4,0},{8,12},{12,8},{16,20},{20,16},{24,28},{28,24},{1,5},{5... | collective-permute-start | bytes 589832 | tf_op jit(solution)/shard_map/ppermute | solution.py:23
  6.4 2.3 %shard_map.139 = (f32[4,64,128]{2,1,0:T(8,128)S(1)}, f32[4,64,128]{2,1,0:T(8,128)S(1)}, bf16[1,192,128]{2,1,0:T(8,128)(2,1)S(1)}) custom-call(f32[4,64,128]{2,1,0:T(8,128)S(1)} %shard_map.137.gram.refs_0_, f32[8,128]{1,0:T(8,128)S(1)} %get-tuple-element.29.refs_1_), custom_call_target="tpu_custom_call" | custom-call | flops 2600000000 | tf_op jit(solution)/shard_map/pallas_call | solution.py:359
  8.7 0.0 copy-done.6
  8.7 0.0 copy-start.8
  8.8 0.0 copy-start.9
  8.8 0.0 copy-start.10
  8.8 2.1 %shard_map.140 = (bf16[128,64,64]{2,1,0:T(8,128)(2,1)S(1)}, f32[8,128]{1,0:T(8,128)S(1)}) custom-call(s32[128]{0:T(128)S(1)} %copy-done.6, bf16[64,64,128]{2,1,0:T(8,128)(2,1)S(1)} %bitcast.6, f32[4,64,128]{2,1,0:T(8,128)S(1)} %get-tuple-element.30.low.leaf_factor), custom_call_target="tpu_custom_call" | custom-call | flops 2700000000 | tf_op jit(solution)/shard_map/pallas_call | solution.py:359
  10.9 2.7 %collective-permute-start = (bf16[1,192,128]{2,1,0:T(8,128)(2,1)S(1)}, bf16[1,192,128]{2,1,0:T(8,128)(2,1)S(1)}, u32[]{:S(2)}, u32[]{:S(2)}) collective-permute-start(bf16[1,192,128]{2,1,0:T(8,128)(2,1)S(1)} %shard_map.141.first), channel_id=1, source_target_pairs={{0,16},{4,20},{8,24},{12,28},{16,0},{20,4},{24,8},{28,12},{1,17},{... | collective-permute-start | bytes 147464 | tf_op jit(solution)/shard_map/ppermute | solution.py:23
  13.6 0.1 pad_add_fusion.spot
  13.7 1.4 %shard_map.142 = (f32[4,64,128]{2,1,0:T(8,128)S(1)}, f32[4,64,128]{2,1,0:T(8,128)S(1)}, f32[192,128]{1,0:T(8,128)S(1)}, f32[8,128]{1,0:T(8,128)S(1)}) custom-call(s32[2]{0:T(128)S(1)} %pad_add_fusion.spot, f32[6,64,128]{2,1,0:T(8,128)S(1)} %get-tuple-element.34.mine, f32[6,64,128]{2,1,0:T(8,128)S(1)} %collective-permute-done.1.other, ...), custom_call_target="tpu_custom_call" | custom-call | flops 1400000000 | tf_op jit(solution)/shard_map/pallas_call | solution.py:359
  15.1 1.6 %collective-permute-start.3 = (f32[192,128]{1,0:T(8,128)S(1)}, f32[192,128]{1,0:T(8,128)S(1)}, u32[]{:S(2)}, u32[]{:S(2)}) collective-permute-start(f32[192,128]{1,0:T(8,128)S(1)} %get-tuple-element.39), channel_id=1, source_target_pairs={{0,8},{4,12},{8,0},{12,4},{16,24},{20,28},{24,16},{28,20},{1,9},{5... | collective-permute-start | bytes 294920 | tf_op jit(solution)/shard_map/ppermute | solution.py:23
  16.7 2.3 %shard_map.143 = (f32[4,64,128]{2,1,0:T(8,128)S(1)}, f32[4,64,128]{2,1,0:T(8,128)S(1)}) custom-call(f32[4,64,128]{2,1,0:T(8,128)S(1)} %get-tuple-element.35.refs_0_, f32[8,128]{1,0:T(8,128)S(1)} %get-tuple-element.36.refs_1_), custom_call_target="tpu_custom_call" | custom-call | flops 2600000000 | tf_op jit(solution)/shard_map/pallas_call | solution.py:359
  19.0 0.0 collective-permute-done.second
  19.0 0.5 %collective-permute-start.2 = (bf16[2,192,128]{2,1,0:T(8,128)(2,1)S(1)}, bf16[2,192,128]{2,1,0:T(8,128)(2,1)S(1)}, u32[]{:S(2)}, u32[]{:S(2)}) collective-permute-start(bf16[2,192,128]{2,1,0:T(8,128)(2,1)S(1)} %shard_map.144.value.rest_4_), channel_id=1, source_target_pairs={{0,8},{4,12},{8,0},{12,4},{16,24},{20,28},{24,16},{28,20},{1,9},{5... | collective-permute-start | bytes 294920 | tf_op jit(solution)/shard_map/ppermute | solution.py:23
  19.5 0.2 collective-permute-done.3.after.refs_1_
  19.7 0.6 %collective-permute-start.5 = (bf16[2,192,128]{2,1,0:T(8,128)(2,1)S(1)}, bf16[2,192,128]{2,1,0:T(8,128)(2,1)S(1)}, u32[]{:S(2)}, u32[]{:S(2)}) collective-permute-start(bf16[2,192,128]{2,1,0:T(8,128)(2,1)S(1)} %shard_map.145.refs_2_), channel_id=1, source_target_pairs={{0,4},{4,0},{8,12},{12,8},{16,20},{20,16},{24,28},{28,24},{1,5},{5... | collective-permute-start | bytes 294920 | tf_op jit(solution)/shard_map/ppermute | solution.py:23
  20.3 2.3 %shard_map.146 = (f32[4,64,128]{2,1,0:T(8,128)S(1)}, bf16[1,192,128]{2,1,0:T(8,128)(2,1)S(1)}) custom-call(f32[4,64,128]{2,1,0:T(8,128)S(1)} %get-tuple-element.38.refs_0_, f32[192,128]{1,0:T(8,128)S(1)} %collective-permute-done.3.after.refs_1_, bf16[2,192,128]{2,1,0:T(8,128)(2,1)S(1)} %shard_map.145.refs_2_), custom_call_target="tpu_custom_call" | custom-call | flops 2600000000 | tf_op jit(solution)/shard_map/pallas_call | solution.py:359
  22.6 1.4 %collective-permute-start.4 = (bf16[1,192,128]{2,1,0:T(8,128)(2,1)S(1)}, bf16[1,192,128]{2,1,0:T(8,128)(2,1)S(1)}, u32[]{:S(2)}, u32[]{:S(2)}) collective-permute-start(bf16[1,192,128]{2,1,0:T(8,128)(2,1)S(1)} %get-tuple-element.40.top_low.rest_0_), channel_id=1, source_target_pairs={{0,16},{4,20},{8,24},{12,28},{16,0},{20,4},{24,8},{28,12},{1,17},{... | collective-permute-start | bytes 147464 | tf_op jit(solution)/shard_map/ppermute | solution.py:23
  24.1 0.0 collective-permute-done.2.after.rest_5_
  24.1 1.1 %collective-permute-start.6 = (bf16[2,192,128]{2,1,0:T(8,128)(2,1)S(1)}, bf16[2,192,128]{2,1,0:T(8,128)(2,1)S(1)}, u32[]{:S(2)}, u32[]{:S(2)}) collective-permute-start(bf16[2,192,128]{2,1,0:T(8,128)(2,1)S(1)} %collective-permute-done.2.after.rest_5_), channel_id=1, source_target_pairs={{0,4},{4,0},{8,12},{12,8},{16,20},{20,16},{24,28},{28,24},{1,5},{5... | collective-permute-start | bytes 294920 | tf_op jit(solution)/shard_map/ppermute | solution.py:23
  25.2 2.0 %shard_map.147 = (f32[2,64,64]{2,1,0:T(8,128)S(1)}, f32[8,64,64]{2,1,0:T(8,128)S(1)}, f32[4,64,64]{2,1,0:T(8,128)S(1)}, bf16[16,64,64]{2,1,0:T(8,128)(2,1)S(1)}) custom-call(s32[2]{0:T(128)S(1)} %pad_add_fusion.spot, s32[16]{0:T(128)S(1)} %copy-done.7, f32[8,64,64]{2,1,0:T(8,128)S(1)} %copy-done.2, ...), custom_call_target="tpu_custom_call" | custom-call | flops 2500000000 | tf_op jit(solution)/shard_map/pallas_call | solution.py:359
  27.2 0.4 %collective-permute-done.4.rest_1_ = bf16[1,192,128]{2,1,0:T(8,128)(2,1)S(1)} collective-permute-done((bf16[1,192,128]{2,1,0:T(8,128)(2,1)S(1)}, bf16[1,192,128]{2,1,0:T(8,128)(2,1)S(1)}, u32[]{:S(2)}, u32[]{:S(2)}) %collective-permute-start.4) | collective-permute-done | bytes 49184 | tf_op jit(solution)/shard_map/ppermute | solution.py:23
  27.6 1.0 %shard_map.148.rest_3_ = bf16[16,64,64]{2,1,0:T(8,128)(2,1)S(1)} custom-call(s32[16]{0:T(128)S(1)} %fusion.source, bf16[16,64,64]{2,1,0:T(8,128)(2,1)S(1)} %get-tuple-element.47.halves, bf16[1,192,128]{2,1,0:T(8,128)(2,1)S(1)} %get-tuple-element.40.top_low.rest_0_, bf16[1,192,128]{2,1,0:T(8,128)(2,1)S(1)} %collective-permute-done.4.rest_1_), custom_call_target="tpu_custom_call" | custom-call | flops 1300000000 | tf_op jit(solution)/shard_map/pallas_call | solution.py:359
  28.6 0.0 collective-permute-done.5.rest_6_
  28.6 0.1 collective-permute-done.6.rest_7_
  28.7 3.3 %shard_map.149 = (f32[2,64,64]{2,1,0:T(8,128)}, f32[8,64,64]{2,1,0:T(8,128)}, f32[4,64,64]{2,1,0:T(8,128)}, bf16[16,64,64]{2,1,0:T(8,128)(2,1)}, bf16[64,64,128]{2,1,0:T(8,128)(2,1)}) custom-call(s32[128]{0:T(128)S(1)} %bitcast_add_fusion.source, bf16[128,64,64]{2,1,0:T(8,128)(2,1)S(1)} %get-tuple-element.31.halves, ...), custom_call_target="tpu_custom_call" | custom-call | flops 3500000000 | tf_op jit(solution)/shard_map/pallas_call | solution.py:359
  (20 shorter events, 0.1 us)
Async XLA Ops:
  0.6 1.0 %copy-start.1 = (f32[8,64,64]{2,1,0:T(8,128)S(1)}, f32[8,64,64]{2,1,0:T(8,128)}, u32[]{:S(2)}) copy-start(f32[8,64,64]{2,1,0:T(8,128)} %bases.3) | copy-start | bytes 393220
  1.6 0.9 %copy-start.3 = (f32[8,64,64]{2,1,0:T(8,128)S(1)}, f32[8,64,64]{2,1,0:T(8,128)}, u32[]{:S(2)}) copy-start(f32[8,64,64]{2,1,0:T(8,128)} %leaf_transfer.1) | copy-start | bytes 393220
  1.6 1.0 %copy-start.5 = (f32[4,64,64]{2,1,0:T(8,128)S(1)}, f32[4,64,64]{2,1,0:T(8,128)}, u32[]{:S(2)}) copy-start(f32[4,64,64]{2,1,0:T(8,128)} %top_transfer.1) | copy-start | bytes 196612
  3.4 10.3 %collective-permute-start.1 = (f32[6,64,128]{2,1,0:T(8,128)S(1)}, f32[6,64,128]{2,1,0:T(8,128)S(1)}, u32[]{:S(2)}, u32[]{:S(2)}) collective-permute-start(f32[6,64,128]{2,1,0:T(8,128)S(1)} %get-tuple-element.34.mine), channel_id=1, source_target_pairs={{0,4},{4,0},{8,12},{12,8},{16,20},{20,16},{24,28},{28,24},{1,5},{5... | collective-permute-start | bytes 589832 | tf_op jit(solution)/shard_map/ppermute | solution.py:23
  6.4 2.3 %copy-start = (bf16[128,64,64]{0,2,1:T(8,128)(2,1)S(1)}, bf16[128,64,64]{0,2,1:T(8,128)(2,1)}, u32[]{:S(2)}) copy-start(bf16[128,64,64]{0,2,1:T(8,128)(2,1)} %param.13) | copy-start | bytes 3145732
  6.4 2.3 %copy-start.6 = (s32[128]{0:T(128)S(1)}, s32[128]{0:T(128)}, u32[]{:S(2)}) copy-start(s32[128]{0:T(128)} %target.2) | copy-start | bytes 1540
  8.7 4.9 %copy-start.8 = (s32[128]{0:T(128)S(1)}, s32[128]{0:T(128)}, u32[]{:S(2)}) copy-start(s32[128]{0:T(128)} %param.16) | copy-start | bytes 1540
  8.8 4.9 %copy-start.9 = (s32[128,1]{0,1:T(1,128)S(1)}, s32[128,1]{0,1:T(1,128)}, u32[]{:S(2)}) copy-start(s32[128,1]{0,1:T(1,128)} %param.15) | copy-start | bytes 1540
  8.8 4.9 %copy-start.10 = (s32[16]{0:T(128)S(1)}, s32[16]{0:T(128)}, u32[]{:S(2)}) copy-start(s32[16]{0:T(128)} %param.19) | copy-start | bytes 196
  10.9 8.0 %collective-permute-start = (bf16[1,192,128]{2,1,0:T(8,128)(2,1)S(1)}, bf16[1,192,128]{2,1,0:T(8,128)(2,1)S(1)}, u32[]{:S(2)}, u32[]{:S(2)}) collective-permute-start(bf16[1,192,128]{2,1,0:T(8,128)(2,1)S(1)} %shard_map.141.first), channel_id=1, source_target_pairs={{0,16},{4,20},{8,24},{12,28},{16,0},{20,4},{24,8},{28,12},{1,17},{... | collective-permute-start | bytes 147464 | tf_op jit(solution)/shard_map/ppermute | solution.py:23
  15.1 4.6 %collective-permute-start.3 = (f32[192,128]{1,0:T(8,128)S(1)}, f32[192,128]{1,0:T(8,128)S(1)}, u32[]{:S(2)}, u32[]{:S(2)}) collective-permute-start(f32[192,128]{1,0:T(8,128)S(1)} %get-tuple-element.39), channel_id=1, source_target_pairs={{0,8},{4,12},{8,0},{12,4},{16,24},{20,28},{24,16},{28,20},{1,9},{5... | collective-permute-start | bytes 294920 | tf_op jit(solution)/shard_map/ppermute | solution.py:23
  19.0 5.1 %collective-permute-start.2 = (bf16[2,192,128]{2,1,0:T(8,128)(2,1)S(1)}, bf16[2,192,128]{2,1,0:T(8,128)(2,1)S(1)}, u32[]{:S(2)}, u32[]{:S(2)}) collective-permute-start(bf16[2,192,128]{2,1,0:T(8,128)(2,1)S(1)} %shard_map.144.value.rest_4_), channel_id=1, source_target_pairs={{0,8},{4,12},{8,0},{12,4},{16,24},{20,28},{24,16},{28,20},{1,9},{5... | collective-permute-start | bytes 294920 | tf_op jit(solution)/shard_map/ppermute | solution.py:23
  19.7 8.9 %collective-permute-start.5 = (bf16[2,192,128]{2,1,0:T(8,128)(2,1)S(1)}, bf16[2,192,128]{2,1,0:T(8,128)(2,1)S(1)}, u32[]{:S(2)}, u32[]{:S(2)}) collective-permute-start(bf16[2,192,128]{2,1,0:T(8,128)(2,1)S(1)} %shard_map.145.refs_2_), channel_id=1, source_target_pairs={{0,4},{4,0},{8,12},{12,8},{16,20},{20,16},{24,28},{28,24},{1,5},{5... | collective-permute-start | bytes 294920 | tf_op jit(solution)/shard_map/ppermute | solution.py:23
  20.3 4.9 %copy-start.2 = (f32[8,64,64]{2,1,0:T(8,128)S(1)}, f32[8,64,64]{2,1,0:T(8,128)}, u32[]{:S(2)}) copy-start(f32[8,64,64]{2,1,0:T(8,128)} %bases.3) | copy-start | bytes 393220
  20.3 4.9 %copy-start.4 = (bf16[16,64,64]{2,1,0:T(8,128)(2,1)S(1)}, bf16[16,64,64]{2,1,0:T(8,128)(2,1)}, u32[]{:S(2)}) copy-start(bf16[16,64,64]{2,1,0:T(8,128)(2,1)} %top_couplings.1) | copy-start | bytes 393220
  20.3 4.9 %copy-start.7 = (s32[16]{0:T(128)S(1)}, s32[16]{0:T(128)}, u32[]{:S(2)}) copy-start(s32[16]{0:T(128)} %target.3) | copy-start | bytes 196
  22.6 5.0 %collective-permute-start.4 = (bf16[1,192,128]{2,1,0:T(8,128)(2,1)S(1)}, bf16[1,192,128]{2,1,0:T(8,128)(2,1)S(1)}, u32[]{:S(2)}, u32[]{:S(2)}) collective-permute-start(bf16[1,192,128]{2,1,0:T(8,128)(2,1)S(1)} %get-tuple-element.40.top_low.rest_0_), channel_id=1, source_target_pairs={{0,16},{4,20},{8,24},{12,28},{16,0},{20,4},{24,8},{28,12},{1,17},{... | collective-permute-start | bytes 147464 | tf_op jit(solution)/shard_map/ppermute | solution.py:23
  24.1 4.6 %collective-permute-start.6 = (bf16[2,192,128]{2,1,0:T(8,128)(2,1)S(1)}, bf16[2,192,128]{2,1,0:T(8,128)(2,1)S(1)}, u32[]{:S(2)}, u32[]{:S(2)}) collective-permute-start(bf16[2,192,128]{2,1,0:T(8,128)(2,1)S(1)} %collective-permute-done.2.after.rest_5_), channel_id=1, source_target_pairs={{0,4},{4,0},{8,12},{12,8},{16,20},{20,16},{24,28},{28,24},{1,5},{5... | collective-permute-start | bytes 294920 | tf_op jit(solution)/shard_map/ppermute | solution.py:23

commit v9 on v8

--- a/solution.py
+++ b/solution.py
@@ -222,7 +222,8 @@
 
 def factor_kernel(terms, has_factor, has_low, *refs):
     grams, refs = refs[:terms], refs[terms + 1 :]
-    outs, (work, factor, inverse) = refs[:-3], refs[-3:]
+    outs, (work, factor) = refs[:-2], refs[-2:]
+    inverse = outs[0]
     more = unpack_upper(grams[1]) if terms == 2 else None
     for g in range(GROUP):
         work[matrix_pair(work, g), :] = grams[0][g] if more is None else grams[0][g] + more[g]
@@ -231,7 +232,6 @@
     if has_low:
         pack_upper(pairs, outs[-1].at[0])
     for g in range(GROUP):
-        outs[0][g] = inverse[matrix_pair(work, g), :]
         if has_factor:
             outs[1][g] = pairs[g]
 
@@ -280,13 +280,13 @@
         for g in range(GROUP):
             place = n * GROUP + g
             piece = near_nn(leaf_factor[g][:, lanes], leaf_transfer[place])
-            leaf_transfers[place] = near_nt(piece, middle_inverse[g][:, lanes])
-    for g in range(GROUP):
-        left, right = (jnp.where(spot[1] == 0, both[:, :rank], both[:, rank:]) for both in (middle_factor[g], top_inverse[g]))
+            leaf_transfers[place] = near_nt(piece, middle_inverse[matrix_pair(middle_inverse, g), :][:, lanes])
+    for g in range(GROUP):
+        left, right = (jnp.where(spot[1] == 0, both[:, :rank], both[:, rank:]) for both in (middle_factor[g], top_inverse[matrix_pair(top_inverse, g), :]))
         top_transfers[g] = near_nt(near_nn(left, top_transfer[g]), right)
     for k in range(share):
         place = spot[0] * share + k
-        both = leaf_inverse[place % GROUP]
+        both = leaf_inverse[matrix_pair(leaf_inverse, place % GROUP), :]
         both = jnp.where(place < GROUP, both[:, :rank], both[:, rank:])
         leaf_bases[k] = near_nt(bases[place], both)
 
@@ -389,7 +389,7 @@
     spot = jnp.stack([near_place, parity]).astype(jnp.int32)
     square = (rank, rank)
     packed = (GROUP, rank, 2 * rank)
-    work = [pltpu.VMEM((rank * GROUP, 2 * rank), f32)] * 3
+    work = [pltpu.VMEM((rank * GROUP, 2 * rank), f32)] * 2
     turned = pltpu.VMEM((rank * (blocks + PITCH_EXTRA), rank), f32)
 
     source = place_of(coupling_dest[:, 0] ^ leaf_place, leaf_bits) * leaves + coupling_local
@@ -403,7 +403,7 @@
     def factored(grams, after, has_factor, has_low):
         return call(
             functools.partial(factor_kernel, len(grams), has_factor, has_low),
-            [(packed, f32)] * (1 + has_factor) + [((1, *uppers), bf16)] * has_low,
+            [((rank * GROUP, 2 * rank), f32)] + [(packed, f32)] * has_factor + [((1, *uppers), bf16)] * has_low,
             2.6,
             arrays=[*grams, after],
             scratch=work,

time: 32.2 us -> 32.2 us (level)
  no operation moved by 1% of the time
where the time goes in v9:
time: 32.2 us; the launch traced here: 32 us
  Pallas kernels  18 us (56%)
  starting transfers between devices  10.9 us (34%)
  local copies, waits for them, and re-layouts  1.49 us (5%)
  waiting for transfers between devices  0.78 us (2%)
  between operations  0.77 us (2%)
    pallas_call x13, Pallas kernels, call(): pl.pallas_call(kernel, out_shape=[jax.ShapeDtypeStruct(shape, dtype) for...  18 us
    ppermute x7, starting transfers between devices, swapped(): return lax.ppermute(value, axis, pairs)  10.9 us
    unnamed x22, local copies, waits for them, and re-layouts  1.49 us
    ppermute x7, waiting for transfers between devices, swapped(): return lax.ppermute(value, axis, pairs)  0.78 us
  transfers between devices with their start and end apart: 7, of which 3 were waited for; matrix products, arithmetic and copies ran while one was open for 0% of the time, Pallas kernels for 42%

profile of v9, /device:TPU:0, one launch (start us, length us, event | category | flops | bytes accessed | tf_op | source)
XLA Modules:
  0.0 32.0 jit_solution(16528241195784473733)
XLA Ops:
  0.6 0.0 copy-start.1
  0.6 0.9 %copy-done.1 = f32[8,64,64]{2,1,0:T(8,128)S(1)} copy-done((f32[8,64,64]{2,1,0:T(8,128)S(1)}, f32[8,64,64]{2,1,0:T(8,128)}, u32[]{:S(2)}) %copy-start.1) | copy-done | bytes 131096
  1.6 0.5 %shard_map.137.gram.refs_0_ = f32[4,64,128]{2,1,0:T(8,128)S(1)} custom-call(f32[8,64,64]{2,1,0:T(8,128)S(1)} %copy-done.1), custom_call_target="tpu_custom_call" | custom-call | flops 1000000000 | tf_op jit(solution)/shard_map/pallas_call | solution.py:359
  2.1 0.5 %copy-done.3 = f32[8,64,64]{2,1,0:T(8,128)S(1)} copy-done((f32[8,64,64]{2,1,0:T(8,128)S(1)}, f32[8,64,64]{2,1,0:T(8,128)}, u32[]{:S(2)}) %copy-start.3) | copy-done | bytes 131096
  2.5 0.0 copy-done.5
  2.6 0.8 %shard_map.138 = (f32[6,64,128]{2,1,0:T(8,128)S(1)}, f32[8,128]{1,0:T(8,128)S(1)}) custom-call(f32[4,64,128]{2,1,0:T(8,128)S(1)} %shard_map.137.gram.refs_0_, f32[8,64,64]{2,1,0:T(8,128)S(1)} %copy-done.3, f32[4,64,64]{2,1,0:T(8,128)S(1)} %copy-done.5), custom_call_target="tpu_custom_call" | custom-call | flops 800000000 | tf_op jit(solution)/shard_map/pallas_call | solution.py:359
  3.4 3.0 %collective-permute-start.1 = (f32[6,64,128]{2,1,0:T(8,128)S(1)}, f32[6,64,128]{2,1,0:T(8,128)S(1)}, u32[]{:S(2)}, u32[]{:S(2)}) collective-permute-start(f32[6,64,128]{2,1,0:T(8,128)S(1)} %get-tuple-element.34.mine), channel_id=1, source_target_pairs={{0,4},{4,0},{8,12},{12,8},{16,20},{20,16},{24,28},{28,24},{1,5},{5... | collective-permute-start | bytes 589832 | tf_op jit(solution)/shard_map/ppermute | solution.py:23
  6.4 2.3 %shard_map.139 = (f32[256,128]{1,0:T(8,128)S(1)}, f32[4,64,128]{2,1,0:T(8,128)S(1)}, bf16[1,192,128]{2,1,0:T(8,128)(2,1)S(1)}) custom-call(f32[4,64,128]{2,1,0:T(8,128)S(1)} %shard_map.137.gram.refs_0_, f32[8,128]{1,0:T(8,128)S(1)} %get-tuple-element.29.refs_1_), custom_call_target="tpu_custom_call" | custom-call | flops 2600000000 | tf_op jit(solution)/shard_map/pallas_call | solution.py:359
  8.7 0.0 copy-done.6
  8.7 0.0 copy-start.8
  8.8 0.0 copy-start.9
  8.8 0.0 copy-start.10
  8.8 2.1 %shard_map.140 = (bf16[128,64,64]{2,1,0:T(8,128)(2,1)S(1)}, f32[8,128]{1,0:T(8,128)S(1)}) custom-call(s32[128]{0:T(128)S(1)} %copy-done.6, bf16[64,64,128]{2,1,0:T(8,128)(2,1)S(1)} %bitcast.6, f32[4,64,128]{2,1,0:T(8,128)S(1)} %get-tuple-element.30.low.leaf_factor), custom_call_target="tpu_custom_call" | custom-call | flops 2700000000 | tf_op jit(solution)/shard_map/pallas_call | solution.py:359
  10.9 2.7 %collective-permute-start = (bf16[1,192,128]{2,1,0:T(8,128)(2,1)S(1)}, bf16[1,192,128]{2,1,0:T(8,128)(2,1)S(1)}, u32[]{:S(2)}, u32[]{:S(2)}) collective-permute-start(bf16[1,192,128]{2,1,0:T(8,128)(2,1)S(1)} %shard_map.141.first), channel_id=1, source_target_pairs={{0,16},{4,20},{8,24},{12,28},{16,0},{20,4},{24,8},{28,12},{1,17},{... | collective-permute-start | bytes 147464 | tf_op jit(solution)/shard_map/ppermute | solution.py:23
  13.6 0.1 pad_add_fusion.spot
  13.7 0.0 collective-permute-done.1.other
  13.7 1.4 %shard_map.142 = (f32[4,64,128]{2,1,0:T(8,128)S(1)}, f32[4,64,128]{2,1,0:T(8,128)S(1)}, f32[192,128]{1,0:T(8,128)S(1)}, f32[8,128]{1,0:T(8,128)S(1)}) custom-call(s32[2]{0:T(128)S(1)} %pad_add_fusion.spot, f32[6,64,128]{2,1,0:T(8,128)S(1)} %get-tuple-element.34.mine, f32[6,64,128]{2,1,0:T(8,128)S(1)} %collective-permute-done.1.other, ...), custom_call_target="tpu_custom_call" | custom-call | flops 1400000000 | tf_op jit(solution)/shard_map/pallas_call | solution.py:359
  15.1 1.6 %collective-permute-start.3 = (f32[192,128]{1,0:T(8,128)S(1)}, f32[192,128]{1,0:T(8,128)S(1)}, u32[]{:S(2)}, u32[]{:S(2)}) collective-permute-start(f32[192,128]{1,0:T(8,128)S(1)} %get-tuple-element.39), channel_id=1, source_target_pairs={{0,8},{4,12},{8,0},{12,4},{16,24},{20,28},{24,16},{28,20},{1,9},{5... | collective-permute-start | bytes 294920 | tf_op jit(solution)/shard_map/ppermute | solution.py:23
  16.7 2.3 %shard_map.143 = (f32[256,128]{1,0:T(8,128)S(1)}, f32[4,64,128]{2,1,0:T(8,128)S(1)}) custom-call(f32[4,64,128]{2,1,0:T(8,128)S(1)} %get-tuple-element.35.refs_0_, f32[8,128]{1,0:T(8,128)S(1)} %get-tuple-element.36.refs_1_), custom_call_target="tpu_custom_call" | custom-call | flops 2600000000 | tf_op jit(solution)/shard_map/pallas_call | solution.py:359
  19.0 0.5 %collective-permute-start.2 = (bf16[2,192,128]{2,1,0:T(8,128)(2,1)S(1)}, bf16[2,192,128]{2,1,0:T(8,128)(2,1)S(1)}, u32[]{:S(2)}, u32[]{:S(2)}) collective-permute-start(bf16[2,192,128]{2,1,0:T(8,128)(2,1)S(1)} %shard_map.144.value.rest_4_), channel_id=1, source_target_pairs={{0,8},{4,12},{8,0},{12,4},{16,24},{20,28},{24,16},{28,20},{1,9},{5... | collective-permute-start | bytes 294920 | tf_op jit(solution)/shard_map/ppermute | solution.py:23
  19.5 0.2 collective-permute-done.3.after.refs_1_
  19.7 0.6 %collective-permute-start.5 = (bf16[2,192,128]{2,1,0:T(8,128)(2,1)S(1)}, bf16[2,192,128]{2,1,0:T(8,128)(2,1)S(1)}, u32[]{:S(2)}, u32[]{:S(2)}) collective-permute-start(bf16[2,192,128]{2,1,0:T(8,128)(2,1)S(1)} %shard_map.145.refs_2_), channel_id=1, source_target_pairs={{0,4},{4,0},{8,12},{12,8},{16,20},{20,16},{24,28},{28,24},{1,5},{5... | collective-permute-start | bytes 294920 | tf_op jit(solution)/shard_map/ppermute | solution.py:23
  20.3 2.3 %shard_map.146 = (f32[256,128]{1,0:T(8,128)S(1)}, bf16[1,192,128]{2,1,0:T(8,128)(2,1)S(1)}) custom-call(f32[4,64,128]{2,1,0:T(8,128)S(1)} %get-tuple-element.38.refs_0_, f32[192,128]{1,0:T(8,128)S(1)} %collective-permute-done.3.after.refs_1_, bf16[2,192,128]{2,1,0:T(8,128)(2,1)S(1)} %shard_map.145.refs_2_), custom_call_target="tpu_custom_call" | custom-call | flops 2600000000 | tf_op jit(solution)/shard_map/pallas_call | solution.py:359
  22.6 1.4 %collective-permute-start.4 = (bf16[1,192,128]{2,1,0:T(8,128)(2,1)S(1)}, bf16[1,192,128]{2,1,0:T(8,128)(2,1)S(1)}, u32[]{:S(2)}, u32[]{:S(2)}) collective-permute-start(bf16[1,192,128]{2,1,0:T(8,128)(2,1)S(1)} %get-tuple-element.40.top_low.rest_0_), channel_id=1, source_target_pairs={{0,16},{4,20},{8,24},{12,28},{16,0},{20,4},{24,8},{28,12},{1,17},{... | collective-permute-start | bytes 147464 | tf_op jit(solution)/shard_map/ppermute | solution.py:23
  24.1 0.0 collective-permute-done.2.after.rest_5_
  24.1 1.1 %collective-permute-start.6 = (bf16[2,192,128]{2,1,0:T(8,128)(2,1)S(1)}, bf16[2,192,128]{2,1,0:T(8,128)(2,1)S(1)}, u32[]{:S(2)}, u32[]{:S(2)}) collective-permute-start(bf16[2,192,128]{2,1,0:T(8,128)(2,1)S(1)} %collective-permute-done.2.after.rest_5_), channel_id=1, source_target_pairs={{0,4},{4,0},{8,12},{12,8},{16,20},{20,16},{24,28},{28,24},{1,5},{5... | collective-permute-start | bytes 294920 | tf_op jit(solution)/shard_map/ppermute | solution.py:23
  25.2 2.0 %shard_map.147 = (f32[2,64,64]{2,1,0:T(8,128)S(1)}, f32[8,64,64]{2,1,0:T(8,128)S(1)}, f32[4,64,64]{2,1,0:T(8,128)S(1)}, bf16[16,64,64]{2,1,0:T(8,128)(2,1)S(1)}) custom-call(s32[2]{0:T(128)S(1)} %pad_add_fusion.spot, s32[16]{0:T(128)S(1)} %copy-done.7, f32[8,64,64]{2,1,0:T(8,128)S(1)} %copy-done.2, ...), custom_call_target="tpu_custom_call" | custom-call | flops 2500000000 | tf_op jit(solution)/shard_map/pallas_call | solution.py:359
  27.2 0.4 %collective-permute-done.4.rest_1_ = bf16[1,192,128]{2,1,0:T(8,128)(2,1)S(1)} collective-permute-done((bf16[1,192,128]{2,1,0:T(8,128)(2,1)S(1)}, bf16[1,192,128]{2,1,0:T(8,128)(2,1)S(1)}, u32[]{:S(2)}, u32[]{:S(2)}) %collective-permute-start.4) | collective-permute-done | bytes 49184 | tf_op jit(solution)/shard_map/ppermute | solution.py:23
  27.6 1.0 %shard_map.148.rest_3_ = bf16[16,64,64]{2,1,0:T(8,128)(2,1)S(1)} custom-call(s32[16]{0:T(128)S(1)} %fusion.source, bf16[16,64,64]{2,1,0:T(8,128)(2,1)S(1)} %get-tuple-element.47.halves, bf16[1,192,128]{2,1,0:T(8,128)(2,1)S(1)} %get-tuple-element.40.top_low.rest_0_, bf16[1,192,128]{2,1,0:T(8,128)(2,1)S(1)} %collective-permute-done.4.rest_1_), custom_call_target="tpu_custom_call" | custom-call | flops 1300000000 | tf_op jit(solution)/shard_map/pallas_call | solution.py:359
  28.6 0.0 collective-permute-done.5.rest_6_
  28.6 0.1 collective-permute-done.6.rest_7_
  28.7 3.3 %shard_map.149 = (f32[2,64,64]{2,1,0:T(8,128)}, f32[8,64,64]{2,1,0:T(8,128)}, f32[4,64,64]{2,1,0:T(8,128)}, bf16[16,64,64]{2,1,0:T(8,128)(2,1)}, bf16[64,64,128]{2,1,0:T(8,128)(2,1)}) custom-call(s32[128]{0:T(128)S(1)} %bitcast_add_fusion.source, bf16[128,64,64]{2,1,0:T(8,128)(2,1)S(1)} %get-tuple-element.31.halves, ...), custom_call_target="tpu_custom_call" | custom-call | flops 3500000000 | tf_op jit(solution)/shard_map/pallas_call | solution.py:359
  (20 shorter events, 0.1 us)
Async XLA Ops:
  0.6 1.0 %copy-start.1 = (f32[8,64,64]{2,1,0:T(8,128)S(1)}, f32[8,64,64]{2,1,0:T(8,128)}, u32[]{:S(2)}) copy-start(f32[8,64,64]{2,1,0:T(8,128)} %bases.3) | copy-start | bytes 393220
  1.6 0.9 %copy-start.3 = (f32[8,64,64]{2,1,0:T(8,128)S(1)}, f32[8,64,64]{2,1,0:T(8,128)}, u32[]{:S(2)}) copy-start(f32[8,64,64]{2,1,0:T(8,128)} %leaf_transfer.1) | copy-start | bytes 393220
  1.6 1.0 %copy-start.5 = (f32[4,64,64]{2,1,0:T(8,128)S(1)}, f32[4,64,64]{2,1,0:T(8,128)}, u32[]{:S(2)}) copy-start(f32[4,64,64]{2,1,0:T(8,128)} %top_transfer.1) | copy-start | bytes 196612
  3.4 10.3 %collective-permute-start.1 = (f32[6,64,128]{2,1,0:T(8,128)S(1)}, f32[6,64,128]{2,1,0:T(8,128)S(1)}, u32[]{:S(2)}, u32[]{:S(2)}) collective-permute-start(f32[6,64,128]{2,1,0:T(8,128)S(1)} %get-tuple-element.34.mine), channel_id=1, source_target_pairs={{0,4},{4,0},{8,12},{12,8},{16,20},{20,16},{24,28},{28,24},{1,5},{5... | collective-permute-start | bytes 589832 | tf_op jit(solution)/shard_map/ppermute | solution.py:23
  6.4 2.3 %copy-start = (bf16[128,64,64]{0,2,1:T(8,128)(2,1)S(1)}, bf16[128,64,64]{0,2,1:T(8,128)(2,1)}, u32[]{:S(2)}) copy-start(bf16[128,64,64]{0,2,1:T(8,128)(2,1)} %param.13) | copy-start | bytes 3145732
  6.4 2.3 %copy-start.6 = (s32[128]{0:T(128)S(1)}, s32[128]{0:T(128)}, u32[]{:S(2)}) copy-start(s32[128]{0:T(128)} %target.2) | copy-start | bytes 1540
  8.7 4.9 %copy-start.8 = (s32[128]{0:T(128)S(1)}, s32[128]{0:T(128)}, u32[]{:S(2)}) copy-start(s32[128]{0:T(128)} %param.16) | copy-start | bytes 1540
  8.8 4.9 %copy-start.9 = (s32[128,1]{0,1:T(1,128)S(1)}, s32[128,1]{0,1:T(1,128)}, u32[]{:S(2)}) copy-start(s32[128,1]{0,1:T(1,128)} %param.15) | copy-start | bytes 1540
  8.8 4.9 %copy-start.10 = (s32[16]{0:T(128)S(1)}, s32[16]{0:T(128)}, u32[]{:S(2)}) copy-start(s32[16]{0:T(128)} %param.19) | copy-start | bytes 196
  10.9 8.1 %collective-permute-start = (bf16[1,192,128]{2,1,0:T(8,128)(2,1)S(1)}, bf16[1,192,128]{2,1,0:T(8,128)(2,1)S(1)}, u32[]{:S(2)}, u32[]{:S(2)}) collective-permute-start(bf16[1,192,128]{2,1,0:T(8,128)(2,1)S(1)} %shard_map.141.first), channel_id=1, source_target_pairs={{0,16},{4,20},{8,24},{12,28},{16,0},{20,4},{24,8},{28,12},{1,17},{... | collective-permute-start | bytes 147464 | tf_op jit(solution)/shard_map/ppermute | solution.py:23
  15.1 4.6 %collective-permute-start.3 = (f32[192,128]{1,0:T(8,128)S(1)}, f32[192,128]{1,0:T(8,128)S(1)}, u32[]{:S(2)}, u32[]{:S(2)}) collective-permute-start(f32[192,128]{1,0:T(8,128)S(1)} %get-tuple-element.39), channel_id=1, source_target_pairs={{0,8},{4,12},{8,0},{12,4},{16,24},{20,28},{24,16},{28,20},{1,9},{5... | collective-permute-start | bytes 294920 | tf_op jit(solution)/shard_map/ppermute | solution.py:23
  19.0 5.1 %collective-permute-start.2 = (bf16[2,192,128]{2,1,0:T(8,128)(2,1)S(1)}, bf16[2,192,128]{2,1,0:T(8,128)(2,1)S(1)}, u32[]{:S(2)}, u32[]{:S(2)}) collective-permute-start(bf16[2,192,128]{2,1,0:T(8,128)(2,1)S(1)} %shard_map.144.value.rest_4_), channel_id=1, source_target_pairs={{0,8},{4,12},{8,0},{12,4},{16,24},{20,28},{24,16},{28,20},{1,9},{5... | collective-permute-start | bytes 294920 | tf_op jit(solution)/shard_map/ppermute | solution.py:23
  19.7 8.8 %collective-permute-start.5 = (bf16[2,192,128]{2,1,0:T(8,128)(2,1)S(1)}, bf16[2,192,128]{2,1,0:T(8,128)(2,1)S(1)}, u32[]{:S(2)}, u32[]{:S(2)}) collective-permute-start(bf16[2,192,128]{2,1,0:T(8,128)(2,1)S(1)} %shard_map.145.refs_2_), channel_id=1, source_target_pairs={{0,4},{4,0},{8,12},{12,8},{16,20},{20,16},{24,28},{28,24},{1,5},{5... | collective-permute-start | bytes 294920 | tf_op jit(solution)/shard_map/ppermute | solution.py:23
  20.3 4.8 %copy-start.2 = (f32[8,64,64]{2,1,0:T(8,128)S(1)}, f32[8,64,64]{2,1,0:T(8,128)}, u32[]{:S(2)}) copy-start(f32[8,64,64]{2,1,0:T(8,128)} %bases.3) | copy-start | bytes 393220
  20.3 4.8 %copy-start.4 = (bf16[16,64,64]{2,1,0:T(8,128)(2,1)S(1)}, bf16[16,64,64]{2,1,0:T(8,128)(2,1)}, u32[]{:S(2)}) copy-start(bf16[16,64,64]{2,1,0:T(8,128)(2,1)} %top_couplings.1) | copy-start | bytes 393220
  20.3 4.8 %copy-start.7 = (s32[16]{0:T(128)S(1)}, s32[16]{0:T(128)}, u32[]{:S(2)}) copy-start(s32[16]{0:T(128)} %target.3) | copy-start | bytes 196
  22.6 5.0 %collective-permute-start.4 = (bf16[1,192,128]{2,1,0:T(8,128)(2,1)S(1)}, bf16[1,192,128]{2,1,0:T(8,128)(2,1)S(1)}, u32[]{:S(2)}, u32[]{:S(2)}) collective-permute-start(bf16[1,192,128]{2,1,0:T(8,128)(2,1)S(1)} %get-tuple-element.40.top_low.rest_0_), channel_id=1, source_target_pairs={{0,16},{4,20},{8,24},{12,28},{16,0},{20,4},{24,8},{28,12},{1,17},{... | collective-permute-start | bytes 147464 | tf_op jit(solution)/shard_map/ppermute | solution.py:23
  24.1 4.6 %collective-permute-start.6 = (bf16[2,192,128]{2,1,0:T(8,128)(2,1)S(1)}, bf16[2,192,128]{2,1,0:T(8,128)(2,1)S(1)}, u32[]{:S(2)}, u32[]{:S(2)}) collective-permute-start(bf16[2,192,128]{2,1,0:T(8,128)(2,1)S(1)} %collective-permute-done.2.after.rest_5_), channel_id=1, source_target_pairs={{0,4},{4,0},{8,12},{12,8},{16,20},{20,16},{24,28},{28,24},{1,5},{5... | collective-permute-start | bytes 294920 | tf_op jit(solution)/shard_map/ppermute | solution.py:23
